TPU v7x, 32 devices: a whole 2x2x4 slice. The times are simulated.
32 devices in a mesh: half: 2 (over x), dp: 16 (over z, y, core).
Axes of the slice: x: 2, y: 2, z: 4, core: 2. Of those that a mesh axis runs over, the one named last changes fastest.
Arguments:
- frames: bfloat16 [32768, 1024], P(('half', 'dp')), may hold values from -6 to 6
- skip_rows: bfloat16 [32768, 1024], P(('half', 'dp')), may hold values from -6 to 6
- lengths: int32 [32, 4], P(('half', 'dp')), may hold values from 1 to 640, 1024 in all within a row
- merge_weight: bfloat16 [2048, 1024], replicated, may hold values from -0.125 to 0.125
- merge_bias: float32 [1024], replicated, may hold values from -3 to 3
- norm1_gain: float32 [1024], replicated, may hold values from 0.1 to 1.9
- norm1_bias: float32 [1024], replicated, may hold values from -1.75 to 1.75
- qkv_weight: bfloat16 [1024, 3072], replicated, may hold values from -0.1875 to 0.1875
- out_weight: bfloat16 [1024, 1024], replicated, may hold values from -0.5 to 0.5
- norm2_gain: float32 [1024], replicated, may hold values from 0.1 to 1.9
- norm2_bias: float32 [1024], replicated, may hold values from -1.75 to 1.75
- up_weight: bfloat16 [1024, 4096], replicated, may hold values from -0.1875 to 0.1875
- up_bias: float32 [4096], replicated, may hold values from -3 to 3
- down_weight: bfloat16 [4096, 1024], replicated, may hold values from -0.09375 to 0.09375
- down_bias: float32 [1024], replicated, may hold values from -3 to 3
- cotangent: bfloat16 [32768, 1024], P(('half', 'dp')), may hold values from -12 to 12
Outputs:
- output: bfloat16 [32768, 1024], P(('half', 'dp'))
- frames_grad: bfloat16 [32768, 1024], P(('half', 'dp'))
- skip_grad: bfloat16 [32768, 1024], P(('half', 'dp'))
- merge_weight_grad: float32 [2048, 1024], P(('half', 'dp'))
- merge_bias_grad: float32 [1024], P(('half', 'dp'))
- norm1_gain_grad: float32 [1024], P(('half', 'dp'))
- norm1_bias_grad: float32 [1024], P(('half', 'dp'))
- qkv_weight_grad: float32 [1024, 3072], P(('half', 'dp'))
- out_weight_grad: float32 [1024, 1024], P(('half', 'dp'))
- norm2_gain_grad: float32 [1024], P(('half', 'dp'))
- norm2_bias_grad: float32 [1024], P(('half', 'dp'))
- up_weight_grad: float32 [1024, 4096], P(('half', 'dp'))
- up_bias_grad: float32 [4096], P(('half', 'dp'))
- down_weight_grad: float32 [4096, 1024], P(('half', 'dp'))
- down_bias_grad: float32 [1024], P(('half', 'dp'))
Inputs may be any that keep to these rules, and one draw needn't show every extreme that they name: Each row of lengths sums to 1024; its utterances fill the row in order.
All inputs are finite; a program needn't handle non-finite values.
Results may differ from a plain program's by a relative error of at most 0.014.
Values may be sent and summed in bfloat16 or wider, within the bound.
No kernel may reach another device: no remote copies, remote signals or barrier semaphores. Data moves between devices by JAX's collectives and lax.ppermute only.
A program may use at most 384 MiB of HBM per device.

v0:
```python
import jax
import jax.numpy as jnp
from jax import lax
from jax.sharding import PartitionSpec as P

D = 1024
H = 16
HD = 64
ROW_LEN = 1024


epsilon = 1e-05
masked_score = -1000000000.0


def swapped(value, axis, apart):
    mask = 2**apart
    pairs = [(source, source ^ mask) for source in range(lax.axis_size(axis))]
    return lax.ppermute(value, axis, pairs)


def norm_rows(values_in, gain_vector, shift_vector):
    row_mean = jnp.mean(values_in, axis=-1, keepdims=True)
    centred = values_in - row_mean
    row_var = jnp.mean(centred * centred, axis=-1, keepdims=True)
    return centred * lax.rsqrt(row_var + epsilon) * gain_vector + shift_vector


def exact_gelu(values_in):
    return jax.nn.gelu(values_in, approximate=False)


def head_slopes():
    return jnp.exp2(-8.0 * (jnp.arange(H, dtype=jnp.float32) + 1.0) / H)


def row_segments(length_row):
    length_ends = jnp.cumsum(length_row)
    position = jnp.arange(ROW_LEN, dtype=jnp.int32)
    return jnp.sum((position[:, None] >= length_ends[None, :]).astype(jnp.int32), axis=1)


def contract_rows(left_side, right_side):
    return lax.dot_general(
        left_side, right_side, (((0,), (0,)), ((), ())), preferred_element_type=jnp.float32
    )


def contract_cols(left_side, right_side):
    return lax.dot_general(
        left_side, right_side, (((1,), (1,)), ((), ())), preferred_element_type=jnp.float32
    )


def score_block(query_block, key_row, block_start, segment, slopes, block_rows):
    raw_scores = jnp.einsum(
        "qhd,khd->hqk", query_block, key_row, preferred_element_type=jnp.float32
    ) * HD ** (-0.5)
    query_pos = block_start + jnp.arange(block_rows, dtype=jnp.int32)
    key_pos = jnp.arange(ROW_LEN, dtype=jnp.int32)
    distance = jnp.abs(query_pos[:, None] - key_pos[None, :]).astype(jnp.float32)
    raw_scores = raw_scores - slopes[:, None, None] * distance[None]
    query_segment = lax.dynamic_slice_in_dim(segment, block_start, block_rows)
    same_segment = query_segment[:, None] == segment[None, :]
    return jnp.where(same_segment[None], raw_scores, masked_score)


def attend_row(query_row, key_row, value_row, segment, slopes):
    block_rows = min(512, ROW_LEN)
    block_starts = jnp.arange(ROW_LEN // block_rows, dtype=jnp.int32) * block_rows

    def one_block(block_start):
        query_block = lax.dynamic_slice_in_dim(query_row, block_start, block_rows)
        scores = score_block(query_block, key_row, block_start, segment, slopes, block_rows)
        row_max = jnp.max(scores, axis=-1, keepdims=True)
        exponent = jnp.exp(scores - row_max)
        row_total = jnp.sum(exponent, axis=-1, keepdims=True)
        soft_low = (exponent / row_total).astype(jnp.bfloat16)
        mixed_block = jnp.einsum(
            "hqk,khd->qhd", soft_low, value_row, preferred_element_type=jnp.float32
        )
        return (mixed_block.astype(jnp.bfloat16), (row_max + jnp.log(row_total))[:, :, 0])

    mixed_blocks, log_blocks = lax.map(one_block, block_starts)
    return (mixed_blocks.reshape(ROW_LEN, H, HD), log_blocks)


def attend_row_back(query_row, key_row, value_row, grad_row, log_row, segment, slopes):
    block_rows = min(512, ROW_LEN)
    block_starts = jnp.arange(ROW_LEN // block_rows, dtype=jnp.int32) * block_rows

    def one_block(running, block_inputs):
        key_grad, value_grad = running
        block_start, log_block = block_inputs
        query_block = lax.dynamic_slice_in_dim(query_row, block_start, block_rows)
        grad_block = lax.dynamic_slice_in_dim(grad_row, block_start, block_rows)
        scores = score_block(query_block, key_row, block_start, segment, slopes, block_rows)
        soft_weights = jnp.exp(scores - log_block[:, :, None])
        soft_low = soft_weights.astype(jnp.bfloat16)
        value_grad = value_grad + jnp.einsum(
            "hqk,qhd->khd", soft_low, grad_block, preferred_element_type=jnp.float32
        )
        soft_grad = jnp.einsum(
            "qhd,khd->hqk", grad_block, value_row, preferred_element_type=jnp.float32
        )
        inner_sum = jnp.sum(soft_weights * soft_grad, axis=-1, keepdims=True)
        score_grad = (soft_weights * (soft_grad - inner_sum)).astype(jnp.bfloat16)
        query_grad = jnp.einsum(
            "hqk,khd->qhd", score_grad, key_row, preferred_element_type=jnp.float32
        ) * HD ** (-0.5)
        key_grad = key_grad + jnp.einsum(
            "hqk,qhd->khd", score_grad, query_block, preferred_element_type=jnp.float32
        ) * HD ** (-0.5)
        return ((key_grad, value_grad), query_grad)

    initial = jnp.zeros((ROW_LEN, H, HD), jnp.float32)
    (key_grad, value_grad), query_grad = lax.scan(
        one_block, (initial, initial), (block_starts, log_row)
    )
    return (query_grad.reshape(ROW_LEN, H, HD), key_grad, value_grad)


def on_device(
    frames,
    skip_rows,
    lengths,
    merge_weight,
    merge_bias,
    norm1_gain,
    norm1_bias,
    qkv_weight,
    out_weight,
    norm2_gain,
    norm2_bias,
    up_weight,
    up_bias,
    down_weight,
    down_bias,
    cotangent,
):
    token_count = frames.shape[0]
    row_count = token_count // ROW_LEN
    slopes = head_slopes()
    segments = jax.vmap(row_segments)(lengths)
    mirror = swapped(skip_rows, "half", 0)
    joined = jnp.concatenate([frames, mirror], axis=1)
    hidden = jnp.dot(joined, merge_weight, preferred_element_type=jnp.float32) + merge_bias
    normed, norm_back_one = jax.vjp(norm_rows, hidden, norm1_gain, norm1_bias)
    normed_low = normed.astype(jnp.bfloat16)
    projected = jnp.dot(normed_low, qkv_weight, preferred_element_type=jnp.float32).astype(
        jnp.bfloat16
    )
    head_view = projected.reshape(row_count, ROW_LEN, 3, H, HD)
    query_rows = head_view[:, :, 0]
    key_rows = head_view[:, :, 1]
    value_rows = head_view[:, :, 2]

    def forward_row(row_inputs):
        query_row, key_row, value_row, segment = row_inputs
        return attend_row(query_row, key_row, value_row, segment, slopes)

    mixed_rows, log_rows = lax.map(forward_row, (query_rows, key_rows, value_rows, segments))
    mixed_heads = mixed_rows.reshape(token_count, D)
    attention = jnp.dot(mixed_heads, out_weight, preferred_element_type=jnp.float32)
    residual = hidden + attention
    normed_two, norm_back_two = jax.vjp(norm_rows, residual, norm2_gain, norm2_bias)
    normed_two_low = normed_two.astype(jnp.bfloat16)
    up_value = jnp.dot(normed_two_low, up_weight, preferred_element_type=jnp.float32) + up_bias
    activated, gelu_back = jax.vjp(exact_gelu, up_value)
    activated_low = activated.astype(jnp.bfloat16)
    output = (
        residual
        + jnp.dot(activated_low, down_weight, preferred_element_type=jnp.float32)
        + down_bias
    ).astype(jnp.bfloat16)
    grad_out = cotangent.astype(jnp.float32)
    down_weight_grad = contract_rows(activated_low, cotangent)
    down_bias_grad = jnp.sum(grad_out, axis=0)
    activated_grad = contract_cols(cotangent, down_weight)
    up_grad = gelu_back(activated_grad)[0].astype(jnp.bfloat16)
    up_bias_grad = jnp.sum(up_grad.astype(jnp.float32), axis=0)
    up_weight_grad = contract_rows(normed_two_low, up_grad)
    normed_two_grad = contract_cols(up_grad, up_weight)
    residual_part, gain_two_grad, shift_two_grad = norm_back_two(normed_two_grad)
    residual_grad = grad_out + residual_part
    attention_grad = residual_grad.astype(jnp.bfloat16)
    out_weight_grad = contract_rows(mixed_heads, attention_grad)
    mixed_grad = (
        contract_cols(attention_grad, out_weight)
        .astype(jnp.bfloat16)
        .reshape(row_count, ROW_LEN, H, HD)
    )

    def backward_row(row_inputs):
        query_row, key_row, value_row, grad_row, log_row, segment = row_inputs
        return attend_row_back(query_row, key_row, value_row, grad_row, log_row, segment, slopes)

    query_grads, key_grads, value_grads = lax.map(
        backward_row, (query_rows, key_rows, value_rows, mixed_grad, log_rows, segments)
    )
    projected_grad = (
        jnp.stack([query_grads, key_grads, value_grads], axis=2)
        .reshape(token_count, 3 * D)
        .astype(jnp.bfloat16)
    )
    qkv_weight_grad = contract_rows(normed_low, projected_grad)
    normed_grad = contract_cols(projected_grad, qkv_weight)
    hidden_part, gain_one_grad, shift_one_grad = norm_back_one(normed_grad)
    hidden_grad = (residual_grad + hidden_part).astype(jnp.bfloat16)
    merge_bias_grad = jnp.sum(hidden_grad.astype(jnp.float32), axis=0)
    merge_weight_grad = contract_rows(joined, hidden_grad)
    joined_grad = contract_cols(hidden_grad, merge_weight)
    frames_grad = joined_grad[:, :D].astype(jnp.bfloat16)
    skip_grad = swapped(joined_grad[:, D:].astype(jnp.bfloat16), "half", 0)
    summed = (
        lax.psum_scatter(merge_weight_grad, ("half", "dp"), scatter_dimension=0, tiled=True),
        lax.psum_scatter(merge_bias_grad, ("half", "dp"), scatter_dimension=0, tiled=True),
        lax.psum_scatter(gain_one_grad, ("half", "dp"), scatter_dimension=0, tiled=True),
        lax.psum_scatter(shift_one_grad, ("half", "dp"), scatter_dimension=0, tiled=True),
        lax.psum_scatter(qkv_weight_grad, ("half", "dp"), scatter_dimension=0, tiled=True),
        lax.psum_scatter(out_weight_grad, ("half", "dp"), scatter_dimension=0, tiled=True),
        lax.psum_scatter(gain_two_grad, ("half", "dp"), scatter_dimension=0, tiled=True),
        lax.psum_scatter(shift_two_grad, ("half", "dp"), scatter_dimension=0, tiled=True),
        lax.psum_scatter(up_weight_grad, ("half", "dp"), scatter_dimension=0, tiled=True),
        lax.psum_scatter(up_bias_grad, ("half", "dp"), scatter_dimension=0, tiled=True),
        lax.psum_scatter(down_weight_grad, ("half", "dp"), scatter_dimension=0, tiled=True),
        lax.psum_scatter(down_bias_grad, ("half", "dp"), scatter_dimension=0, tiled=True),
    )
    return (
        output,
        frames_grad,
        skip_grad,
        summed[0],
        summed[1],
        summed[2],
        summed[3],
        summed[4],
        summed[5],
        summed[6],
        summed[7],
        summed[8],
        summed[9],
        summed[10],
        summed[11],
    )


def solution(mesh):
    in_specs = (
        P(("half", "dp"), None),
        P(("half", "dp"), None),
        P(("half", "dp"), None),
        P(),
        P(),
        P(),
        P(),
        P(),
        P(),
        P(),
        P(),
        P(),
        P(),
        P(),
        P(),
        P(("half", "dp"), None),
    )
    out_specs = (
        P(("half", "dp"), None),
        P(("half", "dp"), None),
        P(("half", "dp"), None),
        P(("half", "dp"), None),
        P(("half", "dp")),
        P(("half", "dp")),
        P(("half", "dp")),
        P(("half", "dp"), None),
        P(("half", "dp"), None),
        P(("half", "dp")),
        P(("half", "dp")),
        P(("half", "dp"), None),
        P(("half", "dp")),
        P(("half", "dp"), None),
        P(("half", "dp")),
    )
    return jax.shard_map(
        on_device, mesh=mesh, in_specs=in_specs, out_specs=out_specs, check_vma=False
    )
```

profile of v0, /device:TPU:0, one launch (start us, length us, event | category | flops | bytes accessed | tf_op | source)
XLA Modules:
  0.0 1291.0 jit_solution(15420864038396980597)
XLA Ops:
  11.1 4.0 copy.64
  17.1 39.1 %collective-permute-done = bf16[1024,1024]{1,0:T(8,128)(2,1)} collective-permute-done((bf16[1024,1024]{1,0:T(8,128)(2,1)}, bf16[1024,1024]{1,0:T(8,128)(2,1)}, u32[]{:S(2)}, u32[]{:S(2)}) %collective-permute-start) | collective-permute-done | bytes 2097184 | tf_op jit(solution)/shard_map/ppermute | solution.py:19
  58.2 4.7 add_reduce_fusion
  65.5 9.7 convolution_convert_fusion
  75.2 8.6 copy.61
  83.8 5.9 slice_bitcast_fusion
  89.7 116.4 %while.48 = (s32[]{:T(128)}, bf16[2,512,16,64]{1,3,2,0:T(8,128)(2,1)}, f32[2,16,512]{2,1,0:T(8,128)S(1)}, s32[2]{0:T(128)S(1)}, s32[1024]{0:T(1024)S(1)}, /*inde...) while((s32[]{:T(128)}, ...), condition=%wide.region_7.8_spmd.clone, body=%wide.region_4.7_spmd.clone.sunk | while | flops 2301092352 | bytes 151272432 | solution.py:84
  95.3 18.6 %fusion.100 = (f32[16,512]{1,0:T(8,128)S(1)}, f32[16,512,1024]{2,1,0:T(8,128)}) fusion(f32[512,1024]{1,0:T(8,128)} %abs_convert_fusion.4, f32[16]{0:T(128)S(1)} %multiply_exponential_fusion.4, pred[512,1024]{1,0:T(8,128)(4,1)S(1)} %broadcast_compare_fusion.4, bf16[1024,16,64]{0,2,1:T(8,128)(2,1)} %get-tuple-element.533, ...), kind=kOutput, calls=%fused_computation.6.clone.1 | convolution fusion | flops 1115676672 | bytes 39354436 | tf_op jit(solution)/shard_map/while/body/eval_jaxpr/while/body/eval_jaxpr/qhd,khd->hqk/dot_general | solution.py:56
  113.8 16.4 %fusion.101 = f32[16,512]{1,0:T(8,128)S(1)} fusion(f32[16,512,1024]{2,1,0:T(8,128)} %get-tuple-element.490, f32[16,512]{1,0:T(8,128)S(1)} %get-tuple-element.491, f32[512,1024]{1,0:T(8,128)S(1)} %copy-done.2, f32[16]{0:T(128)S(1)} %multiply_exponential_fusion.4, pred[512,1024]{1,0:T(8,128)(4,1)S(1)} %broadcast_compare_fusion.4), kind=kLoop, calls=%fused_computation.5.clone.1 | loop fusion | flops 50323456 | bytes 36241472 | tf_op jit(solution)/shard_map/while/body/eval_jaxpr/while/body/eval_jaxpr/reduce_sum | solution.py:77
  130.2 16.2 %fusion.102 = bf16[2,512,16,64]{1,3,2,0:T(8,128)(2,1)S(1)} fusion(bf16[2,512,16,64]{1,3,2,0:T(8,128)(2,1)S(1)} %copy-done.24, s32[]{:T(128)S(6)} %copy.80, bf16[1024,16,64]{0,2,1:T(8,128)(2,1)S(1)} %copy-done.3, f32[16,512,1024]{2,1,0:T(8,128)} %get-tuple-element.490, f32[16,512]{1,0:T(8,128)S(1)} %fusion.101, ...), kind=kOutput, calls=%fused_computation.11.clone.1 | convolution fusion | flops 1132986368 | bytes 39387652 | tf_op jit(solution)/shard_map/while/body/eval_jaxpr/while/body/eval_jaxpr/hqk,khd->qhd/dot_general | solution.py:79
  153.2 18.5 %fusion.100 = (f32[16,512]{1,0:T(8,128)S(1)}, f32[16,512,1024]{2,1,0:T(8,128)}) fusion(f32[512,1024]{1,0:T(8,128)} %abs_convert_fusion.4, f32[16]{0:T(128)S(1)} %multiply_exponential_fusion.4, pred[512,1024]{1,0:T(8,128)(4,1)S(1)} %broadcast_compare_fusion.4, bf16[1024,16,64]{0,2,1:T(8,128)(2,1)} %get-tuple-element.533, ...), kind=kOutput, calls=%fused_computation.6.clone.1 | convolution fusion | flops 1115676672 | bytes 39354436 | tf_op jit(solution)/shard_map/while/body/eval_jaxpr/while/body/eval_jaxpr/qhd,khd->hqk/dot_general | solution.py:56
  171.7 16.4 %fusion.101 = f32[16,512]{1,0:T(8,128)S(1)} fusion(f32[16,512,1024]{2,1,0:T(8,128)} %get-tuple-element.490, f32[16,512]{1,0:T(8,128)S(1)} %get-tuple-element.491, f32[512,1024]{1,0:T(8,128)S(1)} %copy-done.2, f32[16]{0:T(128)S(1)} %multiply_exponential_fusion.4, pred[512,1024]{1,0:T(8,128)(4,1)S(1)} %broadcast_compare_fusion.4), kind=kLoop, calls=%fused_computation.5.clone.1 | loop fusion | flops 50323456 | bytes 36241472 | tf_op jit(solution)/shard_map/while/body/eval_jaxpr/while/body/eval_jaxpr/reduce_sum | solution.py:77
  188.1 16.2 %fusion.102 = bf16[2,512,16,64]{1,3,2,0:T(8,128)(2,1)S(1)} fusion(bf16[2,512,16,64]{1,3,2,0:T(8,128)(2,1)S(1)} %copy-done.24, s32[]{:T(128)S(6)} %copy.80, bf16[1024,16,64]{0,2,1:T(8,128)(2,1)S(1)} %copy-done.3, f32[16,512,1024]{2,1,0:T(8,128)} %get-tuple-element.490, f32[16,512]{1,0:T(8,128)S(1)} %fusion.101, ...), kind=kOutput, calls=%fused_computation.11.clone.1 | convolution fusion | flops 1132986368 | bytes 39387652 | tf_op jit(solution)/shard_map/while/body/eval_jaxpr/while/body/eval_jaxpr/hqk,khd->qhd/dot_general | solution.py:79
  215.8 12.7 fusion.39
  228.5 52.2 %convert_reduce_fusion = (f32[4096]{0:T(1024)}, bf16[1024,4096]{1,0:T(8,128)(2,1)}, f32[1024,4096]{1,0:T(8,128)}) fusion(f32[1024,4096]{1,0:T(8,128)} %fusion.39, f32[4096]{0:T(1024)S(1)} %copy-done.56, bf16[1024,1024]{1,0:T(8,128)(2,1)S(1)} %copy-done.22, bf16[4096,1024]{1,0:T(8,128)(2,1)} %param.33), kind=kOutput, calls=%fused_computation.45 | convolution fusion | flops 8904503296 | bytes 52461568 | tf_op jit(solution)/shard_map/dot_general | solution.py:50
  280.6 13.3 %fusion.46 = (f32[1024]{0:T(1024)}, f32[1024,1024]{1,0:T(8,128)}) fusion(bf16[1024,4096]{1,0:T(8,128)(2,1)} %get-tuple-element.355, bf16[1024,4096]{1,0:T(8,128)(2,1)S(1)} %copy-done.64), kind=kOutput, calls=%fused_computation.112 | convolution fusion | flops 8590982144 | bytes 20975616 | tf_op jit(solution)/shard_map/dot_general | solution.py:50
  294.0 5.6 copy.65
  299.7 5.4 multiply_reduce_fusion.1
  312.3 4.4 fusion.48
  318.3 230.2 %while.49 = (s32[]{:T(128)}, f32[1024,16,64]{0,2,1:T(8,128)}, f32[1024,16,64]{0,2,1:T(8,128)}, bf16[2,512,16,64]{1,3,2,0:T(8,128)(2,1)}, s32[2]{0:T(128)S(1)}, /...) while((s32[]{:T(128)}, f32[1024,16,64]{0,2,1:T(8,128)}, ...), condition=%wide.region_14.15_spmd.clone, body=%wide.region_12.14_spmd.clone.sunk | while | flops 5468840448 | bytes 303217472 | solution.py:117
  321.2 17.2 %fusion.112 = f32[16,512,1024]{2,1,0:T(8,128)} fusion(bf16[1024,16,64]{0,2,1:T(8,128)(2,1)S(1)} %get-tuple-element.576, bf16[1024,16,64]{0,2,1:T(8,128)(2,1)} %get-tuple-element.575, s32[]{:T(128)S(6)} %select_n.44), kind=kOutput, calls=%fused_computation.32.clone.1 | convolution fusion | flops 1073741824 | bytes 36700164 | tf_op jit(solution)/shard_map/while/body/eval_jaxpr/while/body/eval_jaxpr/qhd,khd->hqk/dot_general | solution.py:103
  340.0 27.5 %multiply_reduce_fusion.8 = (f32[16,512]{1,0:T(8,128)S(1)}, f32[16,512,1024]{2,1,0:T(8,128)}) fusion(f32[16,512,1024]{2,1,0:T(8,128)} %fusion.112, f32[16,512]{1,0:T(8,128)S(1)} %dynamic-slice_bitcast_fusion.2, f32[512,1024]{1,0:T(8,128)S(1)} %abs_convert_fusion.5, f32[16]{0:T(128)S(1)} %multiply_exponential_fusion.5, ...), kind=kOutput, calls=%fused_computation.22.clone.1 | convolution fusion | flops 1132453888 | bytes 72942080 | tf_op jit(solution)/shard_map/while/body/eval_jaxpr/while/body/eval_jaxpr/qhd,khd->hqk/dot_general | solution.py:56
  367.5 27.6 %multiply_convert_fusion.3 = bf16[16,512,1024]{2,1,0:T(8,128)(2,1)} fusion(f32[16,512,1024]{2,1,0:T(8,128)} %get-tuple-element.503, f32[16,512,1024]{2,1,0:T(8,128)} %fusion.112, f32[16,512]{1,0:T(8,128)S(1)} %get-tuple-element.504), kind=kLoop, calls=%fused_computation.21.clone.1 | loop fusion | flops 25165824 | bytes 83918848 | tf_op jit(solution)/shard_map/while/body/eval_jaxpr/while/body/eval_jaxpr/convert_element_type | solution.py:107
  395.1 11.3 bitcast_add_fusion.4
  406.3 16.1 %bitcast_add_fusion.5 = f32[1024,16,64]{0,2,1:T(8,128)} fusion(f32[1024,16,64]{0,2,1:T(8,128)} %get-tuple-element.554, f32[16,512,1024]{2,1,0:T(8,128)} %get-tuple-element.503, pred[]{:T(512)S(6)} %compare.3, bf16[1024,16,64]{0,2,1:T(8,128)(2,1)} %get-tuple-element.575, s32[]{:T(128)S(6)} %select_n.44), kind=kOutput, calls=%fused_computation.26.clone.1 | convolution fusion | flops 1084227584 | bytes 42991620 | tf_op jit(solution)/shard_map/while/body/eval_jaxpr/while/body/eval_jaxpr/hqk,qhd->khd/dot_general | solution.py:100
  422.5 10.2 bitcast_dynamic-update-slice_fusion.5
  435.2 17.1 %fusion.112 = f32[16,512,1024]{2,1,0:T(8,128)} fusion(bf16[1024,16,64]{0,2,1:T(8,128)(2,1)S(1)} %get-tuple-element.576, bf16[1024,16,64]{0,2,1:T(8,128)(2,1)} %get-tuple-element.575, s32[]{:T(128)S(6)} %select_n.44), kind=kOutput, calls=%fused_computation.32.clone.1 | convolution fusion | flops 1073741824 | bytes 36700164 | tf_op jit(solution)/shard_map/while/body/eval_jaxpr/while/body/eval_jaxpr/qhd,khd->hqk/dot_general | solution.py:103
  453.9 27.4 %multiply_reduce_fusion.8 = (f32[16,512]{1,0:T(8,128)S(1)}, f32[16,512,1024]{2,1,0:T(8,128)}) fusion(f32[16,512,1024]{2,1,0:T(8,128)} %fusion.112, f32[16,512]{1,0:T(8,128)S(1)} %dynamic-slice_bitcast_fusion.2, f32[512,1024]{1,0:T(8,128)S(1)} %abs_convert_fusion.5, f32[16]{0:T(128)S(1)} %multiply_exponential_fusion.5, ...), kind=kOutput, calls=%fused_computation.22.clone.1 | convolution fusion | flops 1132453888 | bytes 72942080 | tf_op jit(solution)/shard_map/while/body/eval_jaxpr/while/body/eval_jaxpr/qhd,khd->hqk/dot_general | solution.py:56
  481.2 27.4 %multiply_convert_fusion.3 = bf16[16,512,1024]{2,1,0:T(8,128)(2,1)} fusion(f32[16,512,1024]{2,1,0:T(8,128)} %get-tuple-element.503, f32[16,512,1024]{2,1,0:T(8,128)} %fusion.112, f32[16,512]{1,0:T(8,128)S(1)} %get-tuple-element.504), kind=kLoop, calls=%fused_computation.21.clone.1 | loop fusion | flops 25165824 | bytes 83918848 | tf_op jit(solution)/shard_map/while/body/eval_jaxpr/while/body/eval_jaxpr/convert_element_type | solution.py:107
  508.6 12.3 bitcast_add_fusion.4
  521.0 17.2 %bitcast_add_fusion.5 = f32[1024,16,64]{0,2,1:T(8,128)} fusion(f32[1024,16,64]{0,2,1:T(8,128)} %get-tuple-element.554, f32[16,512,1024]{2,1,0:T(8,128)} %get-tuple-element.503, pred[]{:T(512)S(6)} %compare.3, bf16[1024,16,64]{0,2,1:T(8,128)(2,1)} %get-tuple-element.575, s32[]{:T(128)S(6)} %select_n.44), kind=kOutput, calls=%fused_computation.26.clone.1 | convolution fusion | flops 1084227584 | bytes 42991620 | tf_op jit(solution)/shard_map/while/body/eval_jaxpr/while/body/eval_jaxpr/hqk,qhd->khd/dot_general | solution.py:100
  538.2 10.1 bitcast_dynamic-update-slice_fusion.5
  554.9 4.3 convert_bitcast_fusion
  559.9 12.6 fusion.45
  572.6 5.4 copy.67
  578.0 4.4 multiply_reduce_fusion.3
  591.3 7.2 fusion.47
  599.2 13.1 %fusion.40 = f32[1024,3072]{1,0:T(8,128)} fusion(bf16[1024,3072]{0,1:T(8,128)(2,1)} %bitcast.108, f32[1024,1024]{0,1:T(8,128)} %copy-done.5, f32[1024]{0:T(1024)S(1)} %copy-done.67, f32[1024]{0:T(1024)S(1)} %copy-done.44, f32[1024]{0:T(1024)S(1)} %copy-done.46, f32[1024]{0:T(1024)S(1)} %copy-done.36, f32[1024]{0:T(1024)S(1)} %copy-done.39), kind=kOutput, calls=%fused_computation.107 | convolution fusion | flops 6448742400 | bytes 23089152 | tf_op jit(solution)/shard_map/dot_general | solution.py:44
  613.0 16.8 %fusion.38 = f32[1024,4096]{1,0:T(8,128)} fusion(bf16[1024,4096]{1,0:T(8,128)(2,1)} %get-tuple-element.355, f32[1024,1024]{0,1:T(8,128)} %copy-done.9, f32[1024]{0:T(1024)S(1)} %copy-done.69, f32[1024]{0:T(1024)S(1)} %copy-done.60, f32[1024]{0:T(1024)S(1)} %copy-done.49, f32[1024]{0:T(1024)S(1)} %copy-done.42), kind=kOutput, calls=%fused_computation.105 | convolution fusion | flops 8595177472 | bytes 29376512 | tf_op jit(solution)/shard_map/dot_general | solution.py:44
  630.6 12.7 multiply_convert_fusion.1
  646.6 11.5 fusion.49
  659.7 7.1 convolution_convert_fusion.1
  671.1 15.5 %add_convert_fusion.2 = bf16[1024,1024]{0,1:T(8,128)(2,1)} fusion(f32[1024,1024]{0,1:T(8,128)} %copy-done.9, f32[1024]{0:T(1024)S(1)} %copy-done.70, bf16[1024,4096]{1,0:T(8,128)(2,1)} %copy-done.17, bf16[4096,1024]{1,0:T(8,128)(2,1)} %param.33), kind=kOutput, calls=%fused_computation.73 | convolution fusion | flops 8593080320 | bytes 23072768 | tf_op jit(solution)/shard_map/dot_general | solution.py:173
  686.5 4.0 copy.70
  690.5 80.7 %all-reduce.7 = (f32[1024]{0:T(1024)S(1)}, f32[1024]{0:T(1024)S(1)}, f32[1024]{0:T(1024)S(1)}, f32[1024]{0:T(1024)S(1)}, f32[1024]{0:T(1024)S(1)}, /*index=5*/f32[4096]{0:T(1024)S(1)}, f32[1024]{0:T(1024)S(1)}) all-reduce(f32[1024]{0:T(1024)S(1)} %get-tuple-element.357, ...), channel_id=3, replica_groups=mesh['half'=2,'dp'=16] {'half','dp'}, use_global_device_ids=true, to_apply=%region_19.20.clone | all-reduce | flops 10240 | bytes 81920
  775.3 133.1 %reduce-scatter.8.cloned.1.call-done = f32[32,3072]{1,0:T(8,128)} async-done(((f32[1024,3072]{1,0:T(8,128)}), f32[32,3072]{1,0:T(8,128)}) %reduce-scatter.8.cloned.1.call-update) | async-done | bytes 393232 | tf_op jit(solution)/shard_map/reduce_scatter | solution.py:220
  908.4 185.9 %reduce-scatter.12.cloned.1.call-done = f32[32,4096]{1,0:T(8,128)} async-done(((f32[1024,4096]{1,0:T(8,128)}), f32[32,4096]{1,0:T(8,128)}) %reduce-scatter.12.cloned.1.call-update) | async-done | bytes 524304 | tf_op jit(solution)/shard_map/reduce_scatter | solution.py:224
  1094.3 186.7 %reduce-scatter.14.cloned.1.call-done = f32[128,1024]{1,0:T(8,128)} async-done(((f32[4096,1024]{1,0:T(8,128)}), f32[128,1024]{1,0:T(8,128)}) %reduce-scatter.14.cloned.1.call-update) | async-done | bytes 524304 | tf_op jit(solution)/shard_map/reduce_scatter | solution.py:226
  (251 shorter events, 76.9 us)
Async XLA Ops:
  7.2 203.5 %copy-start = (bf16[1024,1024]{1,0:T(8,128)(2,1)S(1)}, bf16[1024,1024]{1,0:T(8,128)(2,1)}, u32[]{:S(2)}) copy-start(bf16[1024,1024]{1,0:T(8,128)(2,1)} %param.28) | copy-start | bytes 6291460
  7.2 768.1 %reduce-scatter.10.cloned.1.call-start = ((), (), s32[]{:S(2)}) async-start(), calls=%async_computation.7 | async-start | bytes 4325376 | tf_op jit(solution)/shard_map/reduce_scatter | solution.py:221
  7.2 49.0 %collective-permute-start = (bf16[1024,1024]{1,0:T(8,128)(2,1)}, bf16[1024,1024]{1,0:T(8,128)(2,1)}, u32[]{:S(2)}, u32[]{:S(2)}) collective-permute-start(bf16[1024,1024]{1,0:T(8,128)(2,1)} %param.21), channel_id=1, source_target_pairs={{0,16},{16,0},{1,17},{17,1},{2,18},{18,2},{3,19},{19,3},{4,20},{20... | collective-permute-start | bytes 6291464 | tf_op jit(solution)/shard_map/ppermute | solution.py:19
  15.1 43.1 %copy-start.37 = (f32[1024]{0:T(1024)S(1)}, f32[1024]{0:T(1024)}, u32[]{:S(2)}) copy-start(f32[1024]{0:T(1024)} %param.24) | copy-start | bytes 12292
  15.1 43.1 %copy-start.65 = (bf16[2048,1024]{1,0:T(8,128)(2,1)S(1)}, bf16[2048,1024]{1,0:T(8,128)(2,1)}, u32[]{:S(2)}) copy-start(bf16[2048,1024]{1,0:T(8,128)(2,1)} %param.23) | copy-start | bytes 12582916
  56.2 9.3 slice-start.2
  58.2 4.7 copy-start.31
  58.2 7.3 slice-start.3
  95.3 18.6 %copy-start.2 = (f32[512,1024]{1,0:T(8,128)S(1)}, f32[512,1024]{1,0:T(8,128)}, u32[]{:S(2)}) copy-start(f32[512,1024]{1,0:T(8,128)} %abs_convert_fusion.4) | copy-start | bytes 6291460 | tf_op jit(solution)/shard_map/while/body/eval_jaxpr/while
  113.8 16.4 %copy-start.3 = (bf16[1024,16,64]{0,2,1:T(8,128)(2,1)S(1)}, bf16[1024,16,64]{0,2,1:T(8,128)(2,1)}, u32[]{:S(2)}) copy-start(bf16[1024,16,64]{0,2,1:T(8,128)(2,1)} %get-tuple-element.534) | copy-start | bytes 6291460 | tf_op jit(solution)/shard_map/while/body/eval_jaxpr/while
  113.8 16.4 %copy-start.24 = (bf16[2,512,16,64]{1,3,2,0:T(8,128)(2,1)S(1)}, bf16[2,512,16,64]{1,3,2,0:T(8,128)(2,1)}, u32[]{:S(2)}) copy-start(bf16[2,512,16,64]{1,3,2,0:T(8,128)(2,1)} %get-tuple-element.517) | copy-start | bytes 6291460 | tf_op jit(solution)/shard_map/while/body/eval_jaxpr/while
  153.2 18.5 %copy-start.2 = (f32[512,1024]{1,0:T(8,128)S(1)}, f32[512,1024]{1,0:T(8,128)}, u32[]{:S(2)}) copy-start(f32[512,1024]{1,0:T(8,128)} %abs_convert_fusion.4) | copy-start | bytes 6291460 | tf_op jit(solution)/shard_map/while/body/eval_jaxpr/while
  171.7 16.4 %copy-start.3 = (bf16[1024,16,64]{0,2,1:T(8,128)(2,1)S(1)}, bf16[1024,16,64]{0,2,1:T(8,128)(2,1)}, u32[]{:S(2)}) copy-start(bf16[1024,16,64]{0,2,1:T(8,128)(2,1)} %get-tuple-element.534) | copy-start | bytes 6291460 | tf_op jit(solution)/shard_map/while/body/eval_jaxpr/while
  171.7 16.4 %copy-start.24 = (bf16[2,512,16,64]{1,3,2,0:T(8,128)(2,1)S(1)}, bf16[2,512,16,64]{1,3,2,0:T(8,128)(2,1)}, u32[]{:S(2)}) copy-start(bf16[2,512,16,64]{1,3,2,0:T(8,128)(2,1)} %get-tuple-element.517) | copy-start | bytes 6291460 | tf_op jit(solution)/shard_map/while/body/eval_jaxpr/while
  206.0 4.5 copy-start.29
  206.1 4.6 copy-start.6
  206.1 4.6 copy-start.38
  210.7 5.0 slice-start.1
  213.5 15.0 %copy-start.9 = (f32[1024,1024]{0,1:T(8,128)}, f32[1024,1024]{0,1:T(8,128)S(1)}, u32[]{:S(2)}) copy-start(f32[1024,1024]{0,1:T(8,128)S(1)} %get-tuple-element.374) | copy-start | bytes 12582916
  213.5 14.9 %copy-start.40 = (f32[1024]{0:T(1024)}, f32[1024]{0:T(1024)S(1)}, u32[]{:S(2)}) copy-start(f32[1024]{0:T(1024)S(1)} %broadcast_multiply_fusion) | copy-start | bytes 12292
  215.7 12.7 copy-start.47
  215.7 12.7 copy-start.22
  215.7 12.7 copy-start.56
  228.5 52.2 %copy-start.64 = (bf16[1024,4096]{1,0:T(8,128)(2,1)S(1)}, bf16[1024,4096]{1,0:T(8,128)(2,1)}, u32[]{:S(2)}) copy-start(bf16[1024,4096]{1,0:T(8,128)(2,1)} %param.31) | copy-start | bytes 25165828
  294.0 5.6 copy-start.41
  294.0 5.6 copy-start.48
  294.0 5.6 copy-start.59
  299.6 5.4 copy-start.55
  299.6 5.4 copy-start.10
  299.6 5.9 copy-start.13
  316.7 458.6 %reduce-scatter.6.cloned.1.call-start = ((), (), s32[]{:S(2)}) async-start(), calls=%async_computation.5 | async-start | bytes 8650752 | tf_op jit(solution)/shard_map/reduce_scatter | solution.py:216
  321.2 18.8 %copy-start.14 = (bf16[1024,16,64]{0,2,1:T(8,128)(2,1)S(1)}, bf16[1024,16,64]{0,2,1:T(8,128)(2,1)}, u32[]{:S(2)}) copy-start(bf16[1024,16,64]{0,2,1:T(8,128)(2,1)} %get-tuple-element.571) | copy-start | bytes 6291460 | tf_op jit(solution)/shard_map/while/body/eval_jaxpr/while
  321.2 18.8 %copy-start.28 = (bf16[1024,16,64]{0,2,1:T(8,128)(2,1)S(1)}, bf16[1024,16,64]{0,2,1:T(8,128)(2,1)}, u32[]{:S(2)}) copy-start(bf16[1024,16,64]{0,2,1:T(8,128)(2,1)} %get-tuple-element.573) | copy-start | bytes 6291460 | tf_op jit(solution)/shard_map/while/body/eval_jaxpr/while
  435.2 18.7 %copy-start.14 = (bf16[1024,16,64]{0,2,1:T(8,128)(2,1)S(1)}, bf16[1024,16,64]{0,2,1:T(8,128)(2,1)}, u32[]{:S(2)}) copy-start(bf16[1024,16,64]{0,2,1:T(8,128)(2,1)} %get-tuple-element.571) | copy-start | bytes 6291460 | tf_op jit(solution)/shard_map/while/body/eval_jaxpr/while
  435.2 18.7 %copy-start.28 = (bf16[1024,16,64]{0,2,1:T(8,128)(2,1)S(1)}, bf16[1024,16,64]{0,2,1:T(8,128)(2,1)}, u32[]{:S(2)}) copy-start(bf16[1024,16,64]{0,2,1:T(8,128)(2,1)} %get-tuple-element.573) | copy-start | bytes 6291460 | tf_op jit(solution)/shard_map/while/body/eval_jaxpr/while
  559.9 12.6 copy-start.19
  572.6 5.4 copy-start.36
  572.6 5.4 copy-start.39
  572.6 5.4 copy-start.44
  578.0 4.6 copy-start.7
  578.0 5.9 copy-start.8
  578.0 5.9 copy-start.46
  598.5 309.9 %reduce-scatter.8.cloned.1.call-start = ((), (), s32[]{:S(2)}) async-start(), calls=%async_computation.6 | async-start | bytes 12976128 | tf_op jit(solution)/shard_map/reduce_scatter | solution.py:220
  612.3 481.9 %reduce-scatter.12.cloned.1.call-start = ((), (), s32[]{:S(2)}) async-start(), calls=%async_computation.8 | async-start | bytes 17301504 | tf_op jit(solution)/shard_map/reduce_scatter | solution.py:224
  629.9 651.1 %reduce-scatter.14.cloned.1.call-start = ((), (), s32[]{:S(2)}) async-start(), calls=%async_computation.9 | async-start | bytes 17301504 | tf_op jit(solution)/shard_map/reduce_scatter | solution.py:226
  630.6 16.0 %copy-start.23 = (bf16[1024,1024]{1,0:T(8,128)(2,1)S(1)}, bf16[1024,1024]{1,0:T(8,128)(2,1)}, u32[]{:S(2)}) copy-start(bf16[1024,1024]{1,0:T(8,128)(2,1)} %param.35) | copy-start | bytes 6291460
  669.3 106.0 %collective-permute-start.1 = (bf16[1024,1024]{1,0:T(8,128)(2,1)}, bf16[1024,1024]{1,0:T(8,128)(2,1)}, u32[]{:S(2)}, u32[]{:S(2)}) collective-permute-start(bf16[1024,1024]{1,0:T(8,128)(2,1)} %get-tuple-element.368), channel_id=1, source_target_pairs={{0,16},{16,0},{1,17},{17,1},{2,18},{18,2},{3,19},{19,3},{4,20},{20... | collective-permute-start | bytes 6291464 | tf_op jit(solution)/shard_map/ppermute | solution.py:19
  671.1 613.0 %copy-start.1 = (bf16[1024,1024]{1,0:T(8,128)(2,1)S(1)}, bf16[1024,1024]{1,0:T(8,128)(2,1)}, u32[]{:S(2)}) copy-start(bf16[1024,1024]{1,0:T(8,128)(2,1)} %param.28) | copy-start | bytes 6291460
  (42 other events, 97.2 us)
Sparse Core Ops, SparseCore 0:
  316.8 143.0 reduce-scatter.9
  598.6 151.3 reduce-scatter.5
  756.7 151.6 reduce-scatter.7
  911.2 183.0 reduce-scatter.11
  1097.1 183.7 reduce-scatter.13
where the time goes:
time: 1300 us; the launch traced here: 1290 us
  waiting for transfers between devices  545 us (42%)
  matrix products  423 us (33%)
  other arithmetic  133 us (10%)
  blocking collectives  80.7 us (6%)
  local copies, waits for them, and re-layouts  80.3 us (6%)
  between operations  15 us (1%)
    reduce_scatter x1, waiting for transfers between devices, on_device(): lax.psum_scatter(down_weight_grad, ('half', 'dp'), scatter_dimension=0, t...  187 us
    reduce_scatter x1, waiting for transfers between devices, on_device(): lax.psum_scatter(up_weight_grad, ('half', 'dp'), scatter_dimension=0, til...  186 us
    reduce_scatter x1, waiting for transfers between devices, on_device(): lax.psum_scatter(qkv_weight_grad, ('half', 'dp'), scatter_dimension=0, ti...  133 us
    dot_general x4, matrix products, score_block(): jnp.einsum('qhd,khd->hqk', query_block, key_row, preferred_element_type=j...  91.9 us
    dot_general x5, matrix products, contract_cols(): lax.dot_general(left_side, right_side, (((1,), (1,)), ((), ())), preferre...  88.9 us
    unnamed x1, blocking collectives  80.7 us
    convert_element_type x2, other arithmetic, one_block(): score_grad = (soft_weights * (soft_grad - inner_sum)).astype(jnp.bfloat16)  55 us
    dot_general x5, matrix products, contract_rows(): lax.dot_general(left_side, right_side, (((0,), (0,)), ((), ())), preferre...  53.1 us
  transfers between devices with their start and end apart: 7, of which 4 were waited for; matrix products, arithmetic and copies ran while one was open for 28% of the time, Pallas kernels for 0%

commit v1 on v0

--- a/solution.py
+++ b/solution.py
@@ -118,6 +118,71 @@
         one_block, (initial, initial), (block_starts, log_row)
     )
     return (query_grad.reshape(ROW_LEN, H, HD), key_grad, value_grad)
+
+
+def mesh_bits():
+    dp_bits = lax.axis_size("dp").bit_length() - 1
+    half_bits = lax.axis_size("half").bit_length() - 1
+    return [("half", bit) for bit in reversed(range(half_bits))] + [
+        ("dp", bit) for bit in reversed(range(dp_bits))
+    ]
+
+
+def halve(block, order, kept_type):
+    bits = mesh_bits()
+    left = list(range(len(bits)))
+    for step, digit in enumerate(order):
+        axis, apart = bits[digit]
+        mine = (lax.axis_index(axis) >> apart) & 1
+        at = left.index(digit)
+        left.pop(at)
+        sent = lax.dynamic_index_in_dim(block, 1 - mine, at, keepdims=False)
+        kept = lax.dynamic_index_in_dim(block, mine, at, keepdims=False)
+        got = swapped(sent, axis, apart)
+        block = kept.astype(jnp.float32) + got.astype(jnp.float32)
+        if step < len(order) - 1:
+            block = block.astype(kept_type)
+    return block
+
+
+def reduce_orders():
+    count = len(mesh_bits())
+    core, second = count - 1, count - 2
+    rest = list(range(second - 1, 0, -1))
+    return ([core, 0, second] + rest, [core, second, 0] + rest)
+
+
+def sum_matrices(matrices):
+    count = len(mesh_bits())
+    results = []
+    for matrix in matrices:
+        rows, columns = matrix.shape
+        block = matrix.astype(jnp.bfloat16).reshape((2,) * count + (rows >> count, columns))
+        cut = columns // 2
+        orders = reduce_orders()
+        results.append(
+            jnp.concatenate(
+                [
+                    halve(block[..., :cut], orders[0], jnp.bfloat16),
+                    halve(block[..., cut:], orders[1], jnp.bfloat16),
+                ],
+                axis=1,
+            )
+        )
+    return results
+
+
+def sum_vectors(vectors):
+    count = len(mesh_bits())
+    parts = [vector.reshape(1 << count, -1) for vector in vectors]
+    joined = jnp.concatenate(parts, axis=1)
+    total = halve(joined.reshape((2,) * count + (joined.shape[1],)), reduce_orders()[0], jnp.float32)
+    cuts = []
+    start = 0
+    for part in parts:
+        cuts.append(total[start : start + part.shape[1]])
+        start += part.shape[1]
+    return cuts
 
 
 def on_device(
@@ -212,19 +277,33 @@
     joined_grad = contract_cols(hidden_grad, merge_weight)
     frames_grad = joined_grad[:, :D].astype(jnp.bfloat16)
     skip_grad = swapped(joined_grad[:, D:].astype(jnp.bfloat16), "half", 0)
+    matrices = sum_matrices(
+        (merge_weight_grad, qkv_weight_grad, out_weight_grad, up_weight_grad, down_weight_grad)
+    )
+    vectors = sum_vectors(
+        (
+            merge_bias_grad,
+            gain_one_grad,
+            shift_one_grad,
+            gain_two_grad,
+            shift_two_grad,
+            up_bias_grad,
+            down_bias_grad,
+        )
+    )
     summed = (
-        lax.psum_scatter(merge_weight_grad, ("half", "dp"), scatter_dimension=0, tiled=True),
-        lax.psum_scatter(merge_bias_grad, ("half", "dp"), scatter_dimension=0, tiled=True),
-        lax.psum_scatter(gain_one_grad, ("half", "dp"), scatter_dimension=0, tiled=True),
-        lax.psum_scatter(shift_one_grad, ("half", "dp"), scatter_dimension=0, tiled=True),
-        lax.psum_scatter(qkv_weight_grad, ("half", "dp"), scatter_dimension=0, tiled=True),
-        lax.psum_scatter(out_weight_grad, ("half", "dp"), scatter_dimension=0, tiled=True),
-        lax.psum_scatter(gain_two_grad, ("half", "dp"), scatter_dimension=0, tiled=True),
-        lax.psum_scatter(shift_two_grad, ("half", "dp"), scatter_dimension=0, tiled=True),
-        lax.psum_scatter(up_weight_grad, ("half", "dp"), scatter_dimension=0, tiled=True),
-        lax.psum_scatter(up_bias_grad, ("half", "dp"), scatter_dimension=0, tiled=True),
-        lax.psum_scatter(down_weight_grad, ("half", "dp"), scatter_dimension=0, tiled=True),
-        lax.psum_scatter(down_bias_grad, ("half", "dp"), scatter_dimension=0, tiled=True),
+        matrices[0],
+        vectors[0],
+        vectors[1],
+        vectors[2],
+        matrices[1],
+        matrices[2],
+        vectors[3],
+        vectors[4],
+        matrices[3],
+        vectors[5],
+        matrices[4],
+        vectors[6],
     )
     return (
         output,

time: 1300 us -> 1000 us (0.77)
  waiting for transfers between devices: 545 us -> 235 us
  blocking collectives: 80.7 us -> 0 us
  starting transfers between devices: 4.94 us -> 76.5 us
  local copies, waits for them, and re-layouts: 80.3 us -> 116 us
    reduce_scatter x5 -> x0, waiting for transfers between devices: 506 us -> none  [the longest x1 187 us: on_device(): lax.psum_scatter(down_weight_grad, ('half', 'dp'), scatter_dimension=0, t...]
    ppermute x2 -> x57, waiting for transfers between devices: 39.1 us -> 235 us  [swapped(): return lax.ppermute(value, axis, pairs)]
    unnamed x1 -> x0, blocking collectives: 80.7 us -> none
    ppermute x2 -> x57, starting transfers between devices: 4.73 us -> 76.5 us  [swapped(): return lax.ppermute(value, axis, pairs)]
    slice x0 -> x7, local copies, waits for them, and re-layouts: none -> 26.1 us  [the longest x5 25 us: sum_matrices(): block[..., :cut]]
    dynamic_slice x0 -> x11, local copies, waits for them, and re-layouts: none -> 13.5 us  [the longest x10 13.4 us: halve(): kept = lax.dynamic_index_in_dim(block, mine, at, keepdims=False)]
    unnamed x154 -> x178, local copies, waits for them, and re-layouts: 34.7 us -> 24.4 us
  transfers between devices with their start and end apart: 7 -> 57, of which waited for: 4 -> 37; matrix products, arithmetic and copies ran while one was open for 28% -> 5% of each run, Pallas kernels for 0% -> 0%
where the time goes in v1:
time: 1000 us; the launch traced here: 996 us
  matrix products  411 us (41%)
  waiting for transfers between devices  235 us (24%)
  other arithmetic  144 us (14%)
  local copies, waits for them, and re-layouts  116 us (12%)
  starting transfers between devices  76.5 us (8%)
    ppermute x57, waiting for transfers between devices, swapped(): return lax.ppermute(value, axis, pairs)  235 us
    dot_general x4, matrix products, score_block(): jnp.einsum('qhd,khd->hqk', query_block, key_row, preferred_element_type=j...  93 us
    dot_general x5, matrix products, contract_cols(): lax.dot_general(left_side, right_side, (((1,), (1,)), ((), ())), preferre...  86.1 us
    ppermute x57, starting transfers between devices, swapped(): return lax.ppermute(value, axis, pairs)  76.5 us
    convert_element_type x2, other arithmetic, one_block(): score_grad = (soft_weights * (soft_grad - inner_sum)).astype(jnp.bfloat16)  55.2 us
    dot_general x5, matrix products, contract_rows(): lax.dot_general(left_side, right_side, (((0,), (0,)), ((), ())), preferre...  49.7 us
    dot_general x2, matrix products, one_block(): jnp.einsum('qhd,khd->hqk', grad_block, value_row, preferred_element_type=...  34.2 us
    reduce_sum x2, other arithmetic, one_block(): row_total = jnp.sum(exponent, axis=-1, keepdims=True)  32.8 us
  transfers between devices with their start and end apart: 57, of which 37 were waited for; matrix products, arithmetic and copies ran while one was open for 5% of the time, Pallas kernels for 0%

profile of v1, /device:TPU:0, one launch (start us, length us, event | category | flops | bytes accessed | tf_op | source)
XLA Modules:
  0.0 995.5 jit_solution(14246253797707005698)
XLA Ops:
  10.5 39.1 %collective-permute-done = bf16[1024,1024]{1,0:T(8,128)(2,1)} collective-permute-done((bf16[1024,1024]{1,0:T(8,128)(2,1)}, bf16[1024,1024]{1,0:T(8,128)(2,1)}, u32[]{:S(2)}, u32[]{:S(2)}) %collective-permute-start) | collective-permute-done | bytes 2097184 | tf_op jit(solution)/shard_map/ppermute | solution.py:19
  59.0 9.7 convolution_convert_fusion.3
  68.7 8.7 copy.71
  77.3 5.8 slice_bitcast_fusion
  83.2 115.1 %while.48 = (s32[]{:T(128)}, bf16[2,512,16,64]{1,3,2,0:T(8,128)(2,1)}, f32[2,16,512]{2,1,0:T(8,128)S(1)}, s32[2]{0:T(128)S(1)}, s32[1024]{0:T(1024)S(1)}, /*inde...) while((s32[]{:T(128)}, ...), condition=%wide.region_7.8_spmd.clone, body=%wide.region_4.7_spmd.clone.sunk | while | flops 2301092352 | bytes 142883792 | solution.py:84
  87.7 19.2 %fusion.146 = (f32[16,512]{1,0:T(8,128)S(1)}, f32[16,512,1024]{2,1,0:T(8,128)}) fusion(f32[512,1024]{1,0:T(8,128)S(1)} %abs_convert_fusion.4, f32[16]{0:T(128)S(1)} %multiply_exponential_fusion.4, pred[512,1024]{1,0:T(8,128)(4,1)S(1)} %broadcast_compare_fusion.4, bf16[1024,16,64]{0,2,1:T(8,128)(2,1)} %get-tuple-element.561, ...), kind=kOutput, calls=%fused_computation.6.clone.1 | convolution fusion | flops 1115676672 | bytes 39354436 | tf_op jit(solution)/shard_map/while/body/eval_jaxpr/while/body/eval_jaxpr/qhd,khd->hqk/dot_general | solution.py:56
  107.0 16.4 %fusion.147 = f32[16,512]{1,0:T(8,128)S(1)} fusion(f32[16,512,1024]{2,1,0:T(8,128)} %get-tuple-element.518, f32[16,512]{1,0:T(8,128)S(1)} %get-tuple-element.519, f32[512,1024]{1,0:T(8,128)S(1)} %abs_convert_fusion.4, f32[16]{0:T(128)S(1)} %multiply_exponential_fusion.4, pred[512,1024]{1,0:T(8,128)(4,1)S(1)} %broadcast_compare_fusion.4), kind=kLoop, calls=%fused_computation.5.clone.1 | loop fusion | flops 50323456 | bytes 36241472 | tf_op jit(solution)/shard_map/while/body/eval_jaxpr/while/body/eval_jaxpr/reduce_sum | solution.py:77
  123.4 16.2 %fusion.148 = bf16[2,512,16,64]{1,3,2,0:T(8,128)(2,1)S(1)} fusion(bf16[2,512,16,64]{1,3,2,0:T(8,128)(2,1)S(1)} %copy-done.35, s32[]{:T(128)S(6)} %copy.195, bf16[1024,16,64]{0,2,1:T(8,128)(2,1)S(1)} %copy-done.4, f32[16,512,1024]{2,1,0:T(8,128)} %get-tuple-element.518, f32[16,512]{1,0:T(8,128)S(1)} %fusion.147, ...), kind=kOutput, calls=%fused_computation.11.clone.1 | convolution fusion | flops 1132986368 | bytes 39387652 | tf_op jit(solution)/shard_map/while/body/eval_jaxpr/while/body/eval_jaxpr/hqk,khd->qhd/dot_general | solution.py:79
  145.0 19.2 %fusion.146 = (f32[16,512]{1,0:T(8,128)S(1)}, f32[16,512,1024]{2,1,0:T(8,128)}) fusion(f32[512,1024]{1,0:T(8,128)S(1)} %abs_convert_fusion.4, f32[16]{0:T(128)S(1)} %multiply_exponential_fusion.4, pred[512,1024]{1,0:T(8,128)(4,1)S(1)} %broadcast_compare_fusion.4, bf16[1024,16,64]{0,2,1:T(8,128)(2,1)} %get-tuple-element.561, ...), kind=kOutput, calls=%fused_computation.6.clone.1 | convolution fusion | flops 1115676672 | bytes 39354436 | tf_op jit(solution)/shard_map/while/body/eval_jaxpr/while/body/eval_jaxpr/qhd,khd->hqk/dot_general | solution.py:56
  164.1 16.4 %fusion.147 = f32[16,512]{1,0:T(8,128)S(1)} fusion(f32[16,512,1024]{2,1,0:T(8,128)} %get-tuple-element.518, f32[16,512]{1,0:T(8,128)S(1)} %get-tuple-element.519, f32[512,1024]{1,0:T(8,128)S(1)} %abs_convert_fusion.4, f32[16]{0:T(128)S(1)} %multiply_exponential_fusion.4, pred[512,1024]{1,0:T(8,128)(4,1)S(1)} %broadcast_compare_fusion.4), kind=kLoop, calls=%fused_computation.5.clone.1 | loop fusion | flops 50323456 | bytes 36241472 | tf_op jit(solution)/shard_map/while/body/eval_jaxpr/while/body/eval_jaxpr/reduce_sum | solution.py:77
  180.6 16.2 %fusion.148 = bf16[2,512,16,64]{1,3,2,0:T(8,128)(2,1)S(1)} fusion(bf16[2,512,16,64]{1,3,2,0:T(8,128)(2,1)S(1)} %copy-done.35, s32[]{:T(128)S(6)} %copy.195, bf16[1024,16,64]{0,2,1:T(8,128)(2,1)S(1)} %copy-done.4, f32[16,512,1024]{2,1,0:T(8,128)} %get-tuple-element.518, f32[16,512]{1,0:T(8,128)S(1)} %fusion.147, ...), kind=kOutput, calls=%fused_computation.11.clone.1 | convolution fusion | flops 1132986368 | bytes 39387652 | tf_op jit(solution)/shard_map/while/body/eval_jaxpr/while/body/eval_jaxpr/hqk,khd->qhd/dot_general | solution.py:79
  207.9 12.8 %fusion.83 = f32[1024,4096]{1,0:T(8,128)} fusion(bf16[1024,4096]{1,0:T(8,128)(2,1)S(1)} %bitcast.439, f32[1024,1024]{0,1:T(8,128)S(1)} %get-tuple-element.396, f32[1024]{0:T(1024)S(1)} %copy-done.75, f32[1024]{0:T(1024)S(1)} %copy-done.67, f32[1024]{0:T(1024)S(1)} %fusion.79, f32[1024]{0:T(1024)S(1)} %broadcast_multiply_fusion), kind=kOutput, calls=%fused_computation.306 | convolution fusion | flops 8595177472 | bytes 29376512 | tf_op jit(solution)/shard_map/dot_general | solution.py:233
  220.8 52.2 %convert_reduce_fusion = (f32[4096]{0:T(1024)}, bf16[1024,4096]{1,0:T(8,128)(2,1)}, f32[1024,4096]{1,0:T(8,128)}) fusion(f32[1024,4096]{1,0:T(8,128)} %fusion.83, f32[4096]{0:T(1024)S(1)} %copy-done.65, bf16[1024,1024]{1,0:T(8,128)(2,1)S(1)} %copy-done.32, bf16[4096,1024]{1,0:T(8,128)(2,1)} %param.33), kind=kOutput, calls=%fused_computation.45 | convolution fusion | flops 8904503296 | bytes 52461568 | tf_op jit(solution)/shard_map/dot_general | solution.py:50
  273.1 13.5 %fusion.95 = (f32[1024]{0:T(1024)}, f32[1024,1024]{1,0:T(8,128)}) fusion(bf16[1024,4096]{1,0:T(8,128)(2,1)} %get-tuple-element.335, bf16[1024,4096]{1,0:T(8,128)(2,1)S(1)} %copy-done.72), kind=kOutput, calls=%fused_computation.317 | convolution fusion | flops 8590982144 | bytes 20975616 | tf_op jit(solution)/shard_map/dot_general | solution.py:50
  286.6 15.3 %convolution_convert_fusion.1 = bf16[1024,4096]{1,0:T(8,128)(2,1)} fusion(bf16[1024,4096]{1,0:T(8,128)(2,1)} %get-tuple-element.335, f32[1024,1024]{0,1:T(8,128)S(1)} %copy-done.13, f32[1024]{0:T(1024)S(1)} %copy-done.76, f32[1024]{0:T(1024)S(1)} %copy-done.68, f32[1024]{0:T(1024)S(1)} %copy-done.60, f32[1024]{0:T(1024)S(1)} %copy-done.52), kind=kOutput, calls=%fused_computation.62 | convolution fusion | flops 8599371776 | bytes 20987904 | tf_op jit(solution)/shard_map/dot_general | solution.py:44
  324.7 228.9 %while.49 = (s32[]{:T(128)}, f32[1024,16,64]{0,2,1:T(8,128)}, f32[1024,16,64]{0,2,1:T(8,128)}, bf16[2,512,16,64]{1,3,2,0:T(8,128)(2,1)}, s32[2]{0:T(128)S(1)}, /...) while((s32[]{:T(128)}, f32[1024,16,64]{0,2,1:T(8,128)}, ...), condition=%wide.region_14.15_spmd.clone, body=%wide.region_12.14_spmd.clone.sunk | while | flops 5468840448 | bytes 361937856 | solution.py:117
  329.0 17.1 %fusion.158 = f32[16,512,1024]{2,1,0:T(8,128)} fusion(bf16[1024,16,64]{0,2,1:T(8,128)(2,1)S(1)} %copy-done.5, bf16[1024,16,64]{0,2,1:T(8,128)(2,1)} %get-tuple-element.603, s32[]{:T(128)S(6)} %select_n.224), kind=kOutput, calls=%fused_computation.32.clone.1 | convolution fusion | flops 1073741824 | bytes 36700164 | tf_op jit(solution)/shard_map/while/body/eval_jaxpr/while/body/eval_jaxpr/qhd,khd->hqk/dot_general | solution.py:103
  346.2 27.3 %multiply_reduce_fusion.8 = (f32[16,512]{1,0:T(8,128)S(1)}, f32[16,512,1024]{2,1,0:T(8,128)}) fusion(f32[16,512,1024]{2,1,0:T(8,128)} %fusion.158, f32[16,512]{1,0:T(8,128)S(1)} %dynamic-slice_bitcast_fusion.42, f32[512,1024]{1,0:T(8,128)S(1)} %abs_convert_fusion.5, f32[16]{0:T(128)S(1)} %multiply_exponential_fusion.5, ...), kind=kOutput, calls=%fused_computation.22.clone.1 | convolution fusion | flops 1132453888 | bytes 72942080 | tf_op jit(solution)/shard_map/while/body/eval_jaxpr/while/body/eval_jaxpr/qhd,khd->hqk/dot_general | solution.py:56
  373.5 27.6 %multiply_convert_fusion.3 = bf16[16,512,1024]{2,1,0:T(8,128)(2,1)} fusion(f32[16,512,1024]{2,1,0:T(8,128)} %get-tuple-element.531, f32[16,512,1024]{2,1,0:T(8,128)} %fusion.158, f32[16,512]{1,0:T(8,128)S(1)} %get-tuple-element.532), kind=kLoop, calls=%fused_computation.21.clone.1 | loop fusion | flops 25165824 | bytes 83918848 | tf_op jit(solution)/shard_map/while/body/eval_jaxpr/while/body/eval_jaxpr/convert_element_type | solution.py:107
  401.1 15.6 %bitcast_add_fusion.8 = f32[1024,16,64]{0,2,1:T(8,128)} fusion(f32[1024,16,64]{0,2,1:T(8,128)} %get-tuple-element.582, f32[16,512,1024]{2,1,0:T(8,128)} %get-tuple-element.531, pred[]{:T(512)S(6)} %compare.3, bf16[1024,16,64]{0,2,1:T(8,128)(2,1)S(1)} %copy-done.11, s32[]{:T(128)S(6)} %select_n.224), kind=kOutput, calls=%fused_computation.26.clone.1 | convolution fusion | flops 1084227584 | bytes 42991620 | tf_op jit(solution)/shard_map/while/body/eval_jaxpr/while/body/eval_jaxpr/hqk,qhd->khd/dot_general | solution.py:100
  416.7 10.4 %bitcast_dynamic-update-slice_fusion.5 = bf16[2,512,16,64]{1,3,2,0:T(8,128)(2,1)} fusion(bf16[2,512,16,64]{1,3,2,0:T(8,128)(2,1)} %get-tuple-element.583, s32[]{:T(128)S(6)} %copy.205, bf16[16,512,1024]{2,1,0:T(8,128)(2,1)} %multiply_convert_fusion.3, bf16[1024,16,64]{0,2,1:T(8,128)(2,1)} %get-tuple-element.601), kind=kOutput, calls=%fused_computation.28.clone.1 | convolution fusion | flops 1074266112 | bytes 20971524 | tf_op jit(solution)/shard_map/while/body/eval_jaxpr/while/body/eval_jaxpr/hqk,khd->qhd/dot_general | solution.py:108
  427.0 9.5 bitcast_add_fusion.7
  442.7 17.0 %fusion.158 = f32[16,512,1024]{2,1,0:T(8,128)} fusion(bf16[1024,16,64]{0,2,1:T(8,128)(2,1)S(1)} %copy-done.5, bf16[1024,16,64]{0,2,1:T(8,128)(2,1)} %get-tuple-element.603, s32[]{:T(128)S(6)} %select_n.224), kind=kOutput, calls=%fused_computation.32.clone.1 | convolution fusion | flops 1073741824 | bytes 36700164 | tf_op jit(solution)/shard_map/while/body/eval_jaxpr/while/body/eval_jaxpr/qhd,khd->hqk/dot_general | solution.py:103
  459.8 27.3 %multiply_reduce_fusion.8 = (f32[16,512]{1,0:T(8,128)S(1)}, f32[16,512,1024]{2,1,0:T(8,128)}) fusion(f32[16,512,1024]{2,1,0:T(8,128)} %fusion.158, f32[16,512]{1,0:T(8,128)S(1)} %dynamic-slice_bitcast_fusion.42, f32[512,1024]{1,0:T(8,128)S(1)} %abs_convert_fusion.5, f32[16]{0:T(128)S(1)} %multiply_exponential_fusion.5, ...), kind=kOutput, calls=%fused_computation.22.clone.1 | convolution fusion | flops 1132453888 | bytes 72942080 | tf_op jit(solution)/shard_map/while/body/eval_jaxpr/while/body/eval_jaxpr/qhd,khd->hqk/dot_general | solution.py:56
  487.1 27.6 %multiply_convert_fusion.3 = bf16[16,512,1024]{2,1,0:T(8,128)(2,1)} fusion(f32[16,512,1024]{2,1,0:T(8,128)} %get-tuple-element.531, f32[16,512,1024]{2,1,0:T(8,128)} %fusion.158, f32[16,512]{1,0:T(8,128)S(1)} %get-tuple-element.532), kind=kLoop, calls=%fused_computation.21.clone.1 | loop fusion | flops 25165824 | bytes 83918848 | tf_op jit(solution)/shard_map/while/body/eval_jaxpr/while/body/eval_jaxpr/convert_element_type | solution.py:107
  514.7 16.8 %bitcast_add_fusion.8 = f32[1024,16,64]{0,2,1:T(8,128)} fusion(f32[1024,16,64]{0,2,1:T(8,128)} %get-tuple-element.582, f32[16,512,1024]{2,1,0:T(8,128)} %get-tuple-element.531, pred[]{:T(512)S(6)} %compare.3, bf16[1024,16,64]{0,2,1:T(8,128)(2,1)S(1)} %copy-done.11, s32[]{:T(128)S(6)} %select_n.224), kind=kOutput, calls=%fused_computation.26.clone.1 | convolution fusion | flops 1084227584 | bytes 42991620 | tf_op jit(solution)/shard_map/while/body/eval_jaxpr/while/body/eval_jaxpr/hqk,qhd->khd/dot_general | solution.py:100
  531.5 10.3 %bitcast_dynamic-update-slice_fusion.5 = bf16[2,512,16,64]{1,3,2,0:T(8,128)(2,1)} fusion(bf16[2,512,16,64]{1,3,2,0:T(8,128)(2,1)} %get-tuple-element.583, s32[]{:T(128)S(6)} %copy.205, bf16[16,512,1024]{2,1,0:T(8,128)(2,1)} %multiply_convert_fusion.3, bf16[1024,16,64]{0,2,1:T(8,128)(2,1)} %get-tuple-element.601), kind=kOutput, calls=%fused_computation.28.clone.1 | convolution fusion | flops 1074266112 | bytes 20971524 | tf_op jit(solution)/shard_map/while/body/eval_jaxpr/while/body/eval_jaxpr/hqk,khd->qhd/dot_general | solution.py:108
  541.8 9.5 bitcast_add_fusion.7
  565.1 10.4 %fusion.94 = (f32[1024]{0:T(1024)S(1)}, f32[1024,1024]{1,0:T(8,128)}) fusion(bf16[1024,3072]{0,1:T(8,128)(2,1)S(1)} %bitcast.419, bf16[1024,3072]{1,0:T(8,128)(2,1)} %param.27), kind=kOutput, calls=%fused_computation.316 | convolution fusion | flops 6443498496 | bytes 16781312 | tf_op jit(solution)/shard_map/dot_general | solution.py:50
  575.6 9.3 convolution_convert_fusion.2
  602.3 6.4 convolution_convert_fusion.4
  608.6 6.2 convolution_convert_fusion.5
  614.9 10.8 %multiply_convert_fusion.1 = bf16[1024,4096]{1,0:T(8,128)(2,1)} fusion(f32[1024,4096]{1,0:T(8,128)} %get-tuple-element.336, f32[1024,4096]{1,0:T(8,128)S(1)} %bitcast.414, f32[4096]{0:T(1024)S(1)} %copy-done.66), kind=kLoop, calls=%fused_computation.47 | loop fusion | flops 16777216 | bytes 41959424 | tf_op jit(solution)/shard_map/convert_element_type | solution.py:235
  625.7 15.1 %convolution_convert_fusion = bf16[4096,1024]{1,0:T(8,128)(2,1)} fusion(bf16[1024,4096]{1,0:T(8,128)(2,1)} %multiply_convert_fusion.1, bf16[1024,1024]{1,0:T(8,128)(2,1)S(1)} %copy-done.33), kind=kOutput, calls=%fused_computation.61 | convolution fusion | flops 8594128896 | bytes 18874368 | tf_op jit(solution)/shard_map/dot_general | solution.py:44
  640.8 13.8 %add_convert_fusion.2 = bf16[1024,1024]{0,1:T(8,128)(2,1)S(1)} fusion(f32[1024,1024]{0,1:T(8,128)S(1)} %copy-done.15, f32[1024]{0:T(1024)S(1)} %copy-done.79, bf16[1024,4096]{1,0:T(8,128)(2,1)} %multiply_convert_fusion.1, bf16[4096,1024]{1,0:T(8,128)(2,1)} %param.33), kind=kOutput, calls=%fused_computation.84 | convolution fusion | flops 8593080320 | bytes 23072768 | tf_op jit(solution)/shard_map/dot_general | solution.py:238
  657.2 5.9 fusion.86
  663.1 6.4 fusion.87
  669.6 6.9 constant_dynamic-slice_fusion.5
  681.7 6.2 fusion.88
  720.4 6.6 collective-permute-done.28
  728.1 6.2 collective-permute-done.33
  764.5 10.3 %collective-permute-done.3 = bf16[2,2,2,64,512]{4,3,0,1,2:T(8,128)(2,1)S(1)} collective-permute-done((bf16[2,2,2,64,512]{4,3,0,1,2:T(8,128)(2,1)S(1)}, bf16[2,2,2,64,512]{4,3,0,1,2:T(8,128)(2,1)S(1)}, u32[]{:S(2)}, u32[]{:S(2)}) %collective-permute-start.3) | collective-permute-done | bytes 524320 | tf_op jit(solution)/shard_map/ppermute | solution.py:19
  781.8 5.7 collective-permute-done.4
  788.2 6.6 collective-permute-done.9
  827.5 39.4 %collective-permute-done.1 = bf16[1024,1024]{1,0:T(8,128)(2,1)S(1)} collective-permute-done((bf16[1024,1024]{1,0:T(8,128)(2,1)}, bf16[1024,1024]{1,0:T(8,128)(2,1)S(1)}, u32[]{:S(2)}, u32[]{:S(2)}) %collective-permute-start.1) | collective-permute-done | bytes 2097184 | tf_op jit(solution)/shard_map/ppermute | solution.py:19
  866.9 16.8 %collective-permute-done.18 = bf16[2,2,2,32,1536]{4,3,0,1,2:T(8,128)(2,1)S(1)} collective-permute-done((bf16[2,2,2,32,1536]{4,3,0,1,2:T(8,128)(2,1)}, bf16[2,2,2,32,1536]{4,3,0,1,2:T(8,128)(2,1)S(1)}, u32[]{:S(2)}, u32[]{:S(2)}) %collective-permute-start.18) | collective-permute-done | bytes 786464 | tf_op jit(solution)/shard_map/ppermute | solution.py:19
  886.4 16.4 %collective-permute-done.19 = bf16[2,2,32,1536]{3,2,0,1:T(8,128)(2,1)S(1)} collective-permute-done((bf16[2,2,32,1536]{3,2,0,1:T(8,128)(2,1)S(1)}, bf16[2,2,32,1536]{3,2,0,1:T(8,128)(2,1)S(1)}, u32[]{:S(2)}, u32[]{:S(2)}) %collective-permute-start.19) | collective-permute-done | bytes 393248 | tf_op jit(solution)/shard_map/ppermute | solution.py:19
  902.9 24.5 %collective-permute-done.24 = bf16[2,2,32,1536]{3,2,0,1:T(8,128)(2,1)S(1)} collective-permute-done((bf16[2,2,32,1536]{3,2,0,1:T(8,128)(2,1)S(1)}, bf16[2,2,32,1536]{3,2,0,1:T(8,128)(2,1)S(1)}, u32[]{:S(2)}, u32[]{:S(2)}) %collective-permute-start.24) | collective-permute-done | bytes 393248 | tf_op jit(solution)/shard_map/ppermute | solution.py:19
  (512 shorter events, 276.8 us)
Async XLA Ops:
  0.7 49.0 %collective-permute-start = (bf16[1024,1024]{1,0:T(8,128)(2,1)}, bf16[1024,1024]{1,0:T(8,128)(2,1)}, u32[]{:S(2)}, u32[]{:S(2)}) collective-permute-start(bf16[1024,1024]{1,0:T(8,128)(2,1)} %param.21), channel_id=1, source_target_pairs={{0,16},{16,0},{1,17},{17,1},{2,18},{18,2},{3,19},{19,3},{4,20},{20... | collective-permute-start | bytes 6291464 | tf_op jit(solution)/shard_map/ppermute | solution.py:19
  681.7 35.2 %collective-permute-start.27 = (bf16[2,2,2,2,32,512]{5,4,1,2,3,0:T(8,128)(2,1)}, bf16[2,2,2,2,32,512]{5,4,1,2,3,0:T(8,128)(2,1)}, u32[]{:S(2)}, u32[]{:S(2)}) collective-permute-start(bf16[2,2,2,2,32,512]{5,4,1,2,3,0:T(8,128)(2,1)} %bitcast.377), channel_id=1, source_target_pairs={{0,1},{1,0},{2,3},{3,2},{4,5},{5,4},{6,7},{7,6},{8,9},{9,8},{10,11... | collective-permute-start | bytes 1572872 | tf_op jit(solution)/shard_map/ppermute | solution.py:19
  693.2 5.9 collective-permute-start.12
  699.0 119.9 %collective-permute-start.47 = (bf16[2,2,2,2,128,512]{5,4,1,2,3,0:T(8,128)(2,1)S(1)}, bf16[2,2,2,2,128,512]{5,4,1,2,3,0:T(8,128)(2,1)S(1)}, u32[]{:S(2)}, u32[]{:S(2)}) collective-permute-start(bf16[2,2,2,2,128,512]{5,4,1,2,3,0:T(8,128)(2,1)S(1)} %bitcast.424), channel_id=1, source_target_pairs={{0,1},{1,0},{2,3},{3,2},{4,5},{5,4},{6,7},{7,6},{8,9},{9,8},{10,11... | collective-permute-start | bytes 6291464 | tf_op jit(solution)/shard_map/ppermute | solution.py:19
  702.4 74.3 %collective-permute-start.17 = (bf16[2,2,2,2,32,1536]{5,4,1,2,3,0:T(8,128)(2,1)}, bf16[2,2,2,2,32,1536]{5,4,1,2,3,0:T(8,128)(2,1)}, u32[]{:S(2)}, u32[]{:S(2)}) collective-permute-start(bf16[2,2,2,2,32,1536]{5,4,1,2,3,0:T(8,128)(2,1)} %bitcast.373), channel_id=1, source_target_pairs={{0,1},{1,0},{2,3},{3,2},{4,5},{5,4},{6,7},{7,6},{8,9},{9,8},{10,11... | collective-permute-start | bytes 4718600 | tf_op jit(solution)/shard_map/ppermute | solution.py:19
  710.1 8.5 collective-permute-start.32
  715.6 42.0 %collective-permute-start.2 = (bf16[2,2,2,2,64,512]{5,4,1,2,3,0:T(8,128)(2,1)S(1)}, bf16[2,2,2,2,64,512]{5,4,1,2,3,0:T(8,128)(2,1)S(1)}, u32[]{:S(2)}, u32[]{:S(2)}) collective-permute-start(bf16[2,2,2,2,64,512]{5,4,1,2,3,0:T(8,128)(2,1)S(1)} %bitcast.431), channel_id=1, source_target_pairs={{0,1},{1,0},{2,3},{3,2},{4,5},{5,4},{6,7},{7,6},{8,9},{9,8},{10,11... | collective-permute-start | bytes 3145736 | tf_op jit(solution)/shard_map/ppermute | solution.py:19
  716.8 43.9 %collective-permute-start.7 = (bf16[2,2,2,2,64,512]{5,4,1,2,0,3:T(8,128)(2,1)S(1)}, bf16[2,2,2,2,64,512]{5,4,1,2,0,3:T(8,128)(2,1)S(1)}, u32[]{:S(2)}, u32[]{:S(2)}) collective-permute-start(bf16[2,2,2,2,64,512]{5,4,1,2,0,3:T(8,128)(2,1)S(1)} %bitcast.430), channel_id=1, source_target_pairs={{0,1},{1,0},{2,3},{3,2},{4,5},{5,4},{6,7},{7,6},{8,9},{9,8},{10,11... | collective-permute-start | bytes 3145736 | tf_op jit(solution)/shard_map/ppermute | solution.py:19
  718.6 8.3 collective-permute-start.28
  726.9 7.4 collective-permute-start.33
  757.6 21.6 %collective-permute-start.22 = (bf16[2,2,2,2,32,1536]{5,4,1,2,0,3:T(8,128)(2,1)S(1)}, bf16[2,2,2,2,32,1536]{5,4,1,2,0,3:T(8,128)(2,1)S(1)}, u32[]{:S(2)}, u32[]{:S(2)}) collective-permute-start(bf16[2,2,2,2,32,1536]{5,4,1,2,0,3:T(8,128)(2,1)S(1)} %bitcast.429), channel_id=1, source_target_pairs={{0,1},{1,0},{2,3},{3,2},{4,5},{5,4},{6,7},{7,6},{8,9},{9,8},{10,11... | collective-permute-start | bytes 4718600 | tf_op jit(solution)/shard_map/ppermute | solution.py:19
  757.6 5.1 collective-permute-start.36
  760.7 14.1 %collective-permute-start.3 = (bf16[2,2,2,64,512]{4,3,0,1,2:T(8,128)(2,1)S(1)}, bf16[2,2,2,64,512]{4,3,0,1,2:T(8,128)(2,1)S(1)}, u32[]{:S(2)}, u32[]{:S(2)}) collective-permute-start(bf16[2,2,2,64,512]{4,3,0,1,2:T(8,128)(2,1)S(1)} %dynamic-slice_bitcast_fusion.12), channel_id=1, source_target_pairs={{0,16},{16,0},{1,17},{17,1},{2,18},{18,2},{3,19},{19,3},{4,20},{20... | collective-permute-start | bytes 1572872 | tf_op jit(solution)/shard_map/ppermute | solution.py:19
  762.7 13.8 %collective-permute-start.8 = (bf16[2,2,2,64,512]{4,3,1,2,0:T(8,128)(2,1)S(1)}, bf16[2,2,2,64,512]{4,3,1,2,0:T(8,128)(2,1)S(1)}, u32[]{:S(2)}, u32[]{:S(2)}) collective-permute-start(bf16[2,2,2,64,512]{4,3,1,2,0:T(8,128)(2,1)S(1)} %dynamic-slice_bitcast_fusion.11), channel_id=1, source_target_pairs={{0,2},{1,3},{2,0},{3,1},{4,6},{5,7},{6,4},{7,5},{8,10},{9,11},{10,... | collective-permute-start | bytes 1572872 | tf_op jit(solution)/shard_map/ppermute | solution.py:19
  774.8 47.0 %collective-permute-start.52 = (bf16[2,2,2,2,128,512]{5,4,1,2,0,3:T(8,128)(2,1)S(1)}, bf16[2,2,2,2,128,512]{5,4,1,2,0,3:T(8,128)(2,1)S(1)}, u32[]{:S(2)}, u32[]{:S(2)}) collective-permute-start(bf16[2,2,2,2,128,512]{5,4,1,2,0,3:T(8,128)(2,1)S(1)} %bitcast.423), channel_id=1, source_target_pairs={{0,1},{1,0},{2,3},{3,2},{4,5},{5,4},{6,7},{7,6},{8,9},{9,8},{10,11... | collective-permute-start | bytes 6291464 | tf_op jit(solution)/shard_map/ppermute | solution.py:19
  776.5 47.5 %collective-permute-start.37 = (bf16[2,2,2,2,32,2048]{5,4,1,2,3,0:T(8,128)(2,1)S(1)}, bf16[2,2,2,2,32,2048]{5,4,1,2,3,0:T(8,128)(2,1)S(1)}, u32[]{:S(2)}, u32[]{:S(2)}) collective-permute-start(bf16[2,2,2,2,32,2048]{5,4,1,2,3,0:T(8,128)(2,1)S(1)} %bitcast.425), channel_id=1, source_target_pairs={{0,1},{1,0},{2,3},{3,2},{4,5},{5,4},{6,7},{7,6},{8,9},{9,8},{10,11... | collective-permute-start | bytes 6291464 | tf_op jit(solution)/shard_map/ppermute | solution.py:19
  776.7 48.9 %collective-permute-start.42 = (bf16[2,2,2,2,32,2048]{5,4,1,2,0,3:T(8,128)(2,1)S(1)}, bf16[2,2,2,2,32,2048]{5,4,1,2,0,3:T(8,128)(2,1)S(1)}, u32[]{:S(2)}, u32[]{:S(2)}) collective-permute-start(bf16[2,2,2,2,32,2048]{5,4,1,2,0,3:T(8,128)(2,1)S(1)} %bitcast.422), channel_id=1, source_target_pairs={{0,1},{1,0},{2,3},{3,2},{4,5},{5,4},{6,7},{7,6},{8,9},{9,8},{10,11... | collective-permute-start | bytes 6291464 | tf_op jit(solution)/shard_map/ppermute | solution.py:19
  779.2 8.3 collective-permute-start.4
  787.5 7.4 collective-permute-start.9
  794.8 5.2 collective-permute-start.5
  800.0 5.7 collective-permute-start.10
  805.7 6.6 collective-permute-start.6
  812.3 5.9 collective-permute-start.11
  818.2 48.8 %collective-permute-start.1 = (bf16[1024,1024]{1,0:T(8,128)(2,1)}, bf16[1024,1024]{1,0:T(8,128)(2,1)S(1)}, u32[]{:S(2)}, u32[]{:S(2)}) collective-permute-start(bf16[1024,1024]{1,0:T(8,128)(2,1)} %get-tuple-element.364), channel_id=1, source_target_pairs={{0,16},{16,0},{1,17},{17,1},{2,18},{18,2},{3,19},{19,3},{4,20},{20... | collective-permute-start | bytes 6291464 | tf_op jit(solution)/shard_map/ppermute | solution.py:19
  818.9 64.9 %collective-permute-start.18 = (bf16[2,2,2,32,1536]{4,3,0,1,2:T(8,128)(2,1)}, bf16[2,2,2,32,1536]{4,3,0,1,2:T(8,128)(2,1)S(1)}, u32[]{:S(2)}, u32[]{:S(2)}) collective-permute-start(bf16[2,2,2,32,1536]{4,3,0,1,2:T(8,128)(2,1)} %dynamic-slice_bitcast_fusion.6), channel_id=1, source_target_pairs={{0,16},{16,0},{1,17},{17,1},{2,18},{18,2},{3,19},{19,3},{4,20},{20... | collective-permute-start | bytes 2359304 | tf_op jit(solution)/shard_map/ppermute | solution.py:19
  821.9 63.2 %collective-permute-start.23 = (bf16[2,2,2,32,1536]{4,3,1,2,0:T(8,128)(2,1)S(1)}, bf16[2,2,2,32,1536]{4,3,1,2,0:T(8,128)(2,1)S(1)}, u32[]{:S(2)}, u32[]{:S(2)}) collective-permute-start(bf16[2,2,2,32,1536]{4,3,1,2,0:T(8,128)(2,1)S(1)} %dynamic-slice_bitcast_fusion.5), channel_id=1, source_target_pairs={{0,2},{1,3},{2,0},{3,1},{4,6},{5,7},{6,4},{7,5},{8,10},{9,11},{10,... | collective-permute-start | bytes 2359304 | tf_op jit(solution)/shard_map/ppermute | solution.py:19
  824.0 128.2 %collective-permute-start.48 = (bf16[2,2,2,128,512]{4,3,0,1,2:T(8,128)(2,1)S(1)}, bf16[2,2,2,128,512]{4,3,0,1,2:T(8,128)(2,1)S(1)}, u32[]{:S(2)}, u32[]{:S(2)}) collective-permute-start(bf16[2,2,2,128,512]{4,3,0,1,2:T(8,128)(2,1)S(1)} %dynamic-slice_bitcast_fusion.2), channel_id=1, source_target_pairs={{0,16},{16,0},{1,17},{17,1},{2,18},{18,2},{3,19},{19,3},{4,20},{20... | collective-permute-start | bytes 3145736 | tf_op jit(solution)/shard_map/ppermute | solution.py:19
  825.6 128.0 %collective-permute-start.53 = (bf16[2,2,2,128,512]{4,3,1,2,0:T(8,128)(2,1)S(1)}, bf16[2,2,2,128,512]{4,3,1,2,0:T(8,128)(2,1)S(1)}, u32[]{:S(2)}, u32[]{:S(2)}) collective-permute-start(bf16[2,2,2,128,512]{4,3,1,2,0:T(8,128)(2,1)S(1)} %dynamic-slice_bitcast_fusion.1), channel_id=1, source_target_pairs={{0,2},{1,3},{2,0},{3,1},{4,6},{5,7},{6,4},{7,5},{8,10},{9,11},{10,... | collective-permute-start | bytes 3145736 | tf_op jit(solution)/shard_map/ppermute | solution.py:19
  866.9 91.0 %collective-permute-start.38 = (bf16[2,2,2,32,2048]{4,3,0,1,2:T(8,128)(2,1)S(1)}, bf16[2,2,2,32,2048]{4,3,0,1,2:T(8,128)(2,1)S(1)}, u32[]{:S(2)}, u32[]{:S(2)}) collective-permute-start(bf16[2,2,2,32,2048]{4,3,0,1,2:T(8,128)(2,1)S(1)} %dynamic-slice_bitcast_fusion.4), channel_id=1, source_target_pairs={{0,16},{16,0},{1,17},{17,1},{2,18},{18,2},{3,19},{19,3},{4,20},{20... | collective-permute-start | bytes 3145736 | tf_op jit(solution)/shard_map/ppermute | solution.py:19
  883.8 75.6 %collective-permute-start.43 = (bf16[2,2,2,32,2048]{4,3,1,2,0:T(8,128)(2,1)S(1)}, bf16[2,2,2,32,2048]{4,3,1,2,0:T(8,128)(2,1)S(1)}, u32[]{:S(2)}, u32[]{:S(2)}) collective-permute-start(bf16[2,2,2,32,2048]{4,3,1,2,0:T(8,128)(2,1)S(1)} %dynamic-slice_bitcast_fusion.3), channel_id=1, source_target_pairs={{0,2},{1,3},{2,0},{3,1},{4,6},{5,7},{6,4},{7,5},{8,10},{9,11},{10,... | collective-permute-start | bytes 3145736 | tf_op jit(solution)/shard_map/ppermute | solution.py:19
  885.1 17.7 %collective-permute-start.19 = (bf16[2,2,32,1536]{3,2,0,1:T(8,128)(2,1)S(1)}, bf16[2,2,32,1536]{3,2,0,1:T(8,128)(2,1)S(1)}, u32[]{:S(2)}, u32[]{:S(2)}) collective-permute-start(bf16[2,2,32,1536]{3,2,0,1:T(8,128)(2,1)S(1)} %dynamic-slice_bitcast_fusion.14), channel_id=1, source_target_pairs={{0,2},{1,3},{2,0},{3,1},{4,6},{5,7},{6,4},{7,5},{8,10},{9,11},{10,... | collective-permute-start | bytes 1179656 | tf_op jit(solution)/shard_map/ppermute | solution.py:19
  902.8 24.6 %collective-permute-start.24 = (bf16[2,2,32,1536]{3,2,0,1:T(8,128)(2,1)S(1)}, bf16[2,2,32,1536]{3,2,0,1:T(8,128)(2,1)S(1)}, u32[]{:S(2)}, u32[]{:S(2)}) collective-permute-start(bf16[2,2,32,1536]{3,2,0,1:T(8,128)(2,1)S(1)} %dynamic-slice_bitcast_fusion.13), channel_id=1, source_target_pairs={{0,16},{16,0},{1,17},{17,1},{2,18},{18,2},{3,19},{19,3},{4,20},{20... | collective-permute-start | bytes 1179656 | tf_op jit(solution)/shard_map/ppermute | solution.py:19
  927.4 6.2 collective-permute-start.20
  933.7 5.7 collective-permute-start.25
  939.4 6.4 collective-permute-start.21
  945.8 5.6 collective-permute-start.26
  952.5 9.2 collective-permute-start.49
  954.0 11.1 %collective-permute-start.54 = (bf16[2,2,128,512]{3,2,0,1:T(8,128)(2,1)S(1)}, bf16[2,2,128,512]{3,2,0,1:T(8,128)(2,1)S(1)}, u32[]{:S(2)}, u32[]{:S(2)}) collective-permute-start(bf16[2,2,128,512]{3,2,0,1:T(8,128)(2,1)S(1)} %dynamic-slice_bitcast_fusion.7), channel_id=1, source_target_pairs={{0,16},{16,0},{1,17},{17,1},{2,18},{18,2},{3,19},{19,3},{4,20},{20... | collective-permute-start | bytes 1572872 | tf_op jit(solution)/shard_map/ppermute | solution.py:19
  958.4 9.2 collective-permute-start.39
  959.8 10.8 %collective-permute-start.44 = (bf16[2,2,32,2048]{3,2,0,1:T(8,128)(2,1)S(1)}, bf16[2,2,32,2048]{3,2,0,1:T(8,128)(2,1)S(1)}, u32[]{:S(2)}, u32[]{:S(2)}) collective-permute-start(bf16[2,2,32,2048]{3,2,0,1:T(8,128)(2,1)S(1)} %dynamic-slice_bitcast_fusion.9), channel_id=1, source_target_pairs={{0,16},{16,0},{1,17},{17,1},{2,18},{18,2},{3,19},{19,3},{4,20},{20... | collective-permute-start | bytes 1572872 | tf_op jit(solution)/shard_map/ppermute | solution.py:19
  961.9 10.9 %collective-permute-start.50 = (bf16[2,128,512]{2,1,0:T(8,128)(2,1)S(1)}, bf16[2,128,512]{2,1,0:T(8,128)(2,1)S(1)}, u32[]{:S(2)}, u32[]{:S(2)}) collective-permute-start(bf16[2,128,512]{2,1,0:T(8,128)(2,1)S(1)} %dynamic-slice_bitcast_fusion.16), channel_id=1, source_target_pairs={{0,4},{1,5},{2,6},{3,7},{4,0},{5,1},{6,2},{7,3},{8,12},{9,13},{10,... | collective-permute-start | bytes 786440 | tf_op jit(solution)/shard_map/ppermute | solution.py:19
  965.2 11.8 %collective-permute-start.55 = (bf16[2,128,512]{2,1,0:T(8,128)(2,1)S(1)}, bf16[2,128,512]{2,1,0:T(8,128)(2,1)S(1)}, u32[]{:S(2)}, u32[]{:S(2)}) collective-permute-start(bf16[2,128,512]{2,1,0:T(8,128)(2,1)S(1)} %dynamic-slice_bitcast_fusion.15), channel_id=1, source_target_pairs={{0,4},{1,5},{2,6},{3,7},{4,0},{5,1},{6,2},{7,3},{8,12},{9,13},{10,... | collective-permute-start | bytes 786440 | tf_op jit(solution)/shard_map/ppermute | solution.py:19
  967.8 13.5 %collective-permute-start.40 = (bf16[2,32,2048]{2,1,0:T(8,128)(2,1)S(1)}, bf16[2,32,2048]{2,1,0:T(8,128)(2,1)S(1)}, u32[]{:S(2)}, u32[]{:S(2)}) collective-permute-start(bf16[2,32,2048]{2,1,0:T(8,128)(2,1)S(1)} %dynamic-slice_bitcast_fusion.18), channel_id=1, source_target_pairs={{0,4},{1,5},{2,6},{3,7},{4,0},{5,1},{6,2},{7,3},{8,12},{9,13},{10,... | collective-permute-start | bytes 786440 | tf_op jit(solution)/shard_map/ppermute | solution.py:19
  970.8 14.6 %collective-permute-start.45 = (bf16[2,32,2048]{2,1,0:T(8,128)(2,1)S(1)}, bf16[2,32,2048]{2,1,0:T(8,128)(2,1)S(1)}, u32[]{:S(2)}, u32[]{:S(2)}) collective-permute-start(bf16[2,32,2048]{2,1,0:T(8,128)(2,1)S(1)} %dynamic-slice_bitcast_fusion.17), channel_id=1, source_target_pairs={{0,4},{1,5},{2,6},{3,7},{4,0},{5,1},{6,2},{7,3},{8,12},{9,13},{10,... | collective-permute-start | bytes 786440 | tf_op jit(solution)/shard_map/ppermute | solution.py:19
  972.9 16.8 %collective-permute-start.51 = (bf16[128,512]{1,0:T(8,128)(2,1)S(1)}, bf16[128,512]{1,0:T(8,128)(2,1)S(1)}, u32[]{:S(2)}, u32[]{:S(2)}) collective-permute-start(bf16[128,512]{1,0:T(8,128)(2,1)S(1)} %dynamic-slice_bitcast_fusion.26), channel_id=1, source_target_pairs={{0,8},{1,9},{2,10},{3,11},{4,12},{5,13},{6,14},{7,15},{8,0},{9,1},... | collective-permute-start | bytes 393224 | tf_op jit(solution)/shard_map/ppermute | solution.py:19
  977.1 12.6 %collective-permute-start.56 = (bf16[128,512]{1,0:T(8,128)(2,1)S(1)}, bf16[128,512]{1,0:T(8,128)(2,1)S(1)}, u32[]{:S(2)}, u32[]{:S(2)}) collective-permute-start(bf16[128,512]{1,0:T(8,128)(2,1)S(1)} %dynamic-slice_bitcast_fusion.25), channel_id=1, source_target_pairs={{0,8},{1,9},{2,10},{3,11},{4,12},{5,13},{6,14},{7,15},{8,0},{9,1},... | collective-permute-start | bytes 393224 | tf_op jit(solution)/shard_map/ppermute | solution.py:19
  981.3 8.3 collective-permute-start.41
  985.6 7.3 collective-permute-start.46
  (109 other events, 1117.6 us)

commit v2 on v0

v2 whole, which is shorter than its diff:
```python
import functools

import jax
import jax.numpy as jnp
from jax import lax
from jax.experimental import pallas as pl
from jax.experimental.pallas import tpu as pltpu
from jax.sharding import PartitionSpec as P

D = 1024
H = 16
HD = 64
ROW_LEN = 1024
BLOCK = 128
BLOCKS = ROW_LEN // BLOCK
TILE = 256
HEADS = 8
GROUPS = H // HEADS
FAR = 1e30
epsilon = 1e-05
f32 = jnp.float32
bf16 = jnp.bfloat16
MIB = 1024 * 1024


def nn(left, right):
    return jnp.dot(left, right, preferred_element_type=f32)


def nt(left, right):
    return lax.dot_general(left, right, (((1,), (1,)), ((), ())), preferred_element_type=f32)


def tn(left, right):
    return lax.dot_general(left, right, (((0,), (0,)), ((), ())), preferred_element_type=f32)


def settings(megabytes):
    return pltpu.CompilerParams(vmem_limit_bytes=megabytes * MIB)


def cost(flops, moved):
    return pl.CostEstimate(flops=int(flops), bytes_accessed=int(moved), transcendentals=0)


def held(shape):
    zeros = (0,) * len(shape)
    return pl.BlockSpec(shape, lambda *_: zeros, pipeline_mode=pl.Buffered(1))


def tiled(columns):
    return pl.BlockSpec((TILE, columns), lambda i: (i, 0))


def summed_over(columns):
    return pl.BlockSpec((1, columns), lambda i: (0, 0))


def swapped(value, axis, apart):
    mask = 2**apart
    pairs = [(source, source ^ mask) for source in range(lax.axis_size(axis))]
    return lax.ppermute(value, axis, pairs)


def mesh_bits():
    dp_bits = lax.axis_size("dp").bit_length() - 1
    half_bits = lax.axis_size("half").bit_length() - 1
    return [("half", bit) for bit in reversed(range(half_bits))] + [
        ("dp", bit) for bit in reversed(range(dp_bits))
    ]


def halve(block, left, order, kept_type):
    bits = mesh_bits()
    left = list(left)
    for step, digit in enumerate(order):
        axis, apart = bits[digit]
        mine = (lax.axis_index(axis) >> apart) & 1
        at = left.index(digit)
        left.pop(at)
        sent = lax.dynamic_index_in_dim(block, 1 - mine, at, keepdims=False)
        kept = lax.dynamic_index_in_dim(block, mine, at, keepdims=False)
        got = swapped(sent, axis, apart)
        block = kept.astype(f32) + got.astype(f32)
        if step < len(order) - 1:
            block = block.astype(kept_type)
    return block


def digits():
    count = len(mesh_bits())
    core, second = count - 1, count - 2
    return core, 0, second, list(range(second - 1, 0, -1))


def reduced(pair, first):
    count = len(mesh_bits())
    sent, kept = pair
    core, x, y, rest = digits()
    got = swapped(sent, "dp", 0)
    block = (kept.astype(f32) + got.astype(f32)).astype(bf16)
    rows, columns = block.shape
    block = block.reshape((2,) * (count - 1) + (rows >> (count - 1), columns))
    orders = {"x": [x, y] + rest, "y": [y, x] + rest, "z": rest + [y, x]}
    if len(first) == 1:
        return halve(block, range(count - 1), orders[first], bf16)
    cut = columns // 2
    return jnp.concatenate(
        [
            halve(block[..., :cut], range(count - 1), orders[first[0]], bf16),
            halve(block[..., cut:], range(count - 1), orders[first[1]], bf16),
        ],
        axis=1,
    )


def reduced_vectors(vectors):
    count = len(mesh_bits())
    core, x, y, rest = digits()
    parts = [vector.reshape(1 << count, -1) for vector in vectors]
    joined = jnp.concatenate(parts, axis=1)
    total = halve(
        joined.reshape((2,) * count + (joined.shape[1],)), range(count), [core, x, y] + rest, f32
    )
    cuts = []
    start = 0
    for part in parts:
        cuts.append(total[start : start + part.shape[1]])
        start += part.shape[1]
    return cuts


def split_rows(total, core, rows_each):
    rows, columns = total.shape
    cut = total.reshape(rows // (2 * rows_each), 2, rows_each, columns)
    first, second = cut[:, 0], cut[:, 1]
    even = core == 0
    sent = jnp.where(even, second, first).reshape(rows // 2, columns)
    kept = jnp.where(even, first, second).reshape(rows // 2, columns)
    return sent.astype(bf16), kept.astype(bf16)


def row_stats(values):
    mean = jnp.mean(values, axis=-1, keepdims=True)
    centred = values - mean
    scale = lax.rsqrt(jnp.mean(centred * centred, axis=-1, keepdims=True) + epsilon)
    return centred * scale, scale


def norm_back(values, gain, grad):
    normal, scale = row_stats(values)
    inner = grad * gain
    along = jnp.mean(inner * normal, axis=-1, keepdims=True)
    return scale * (inner - jnp.mean(inner, axis=-1, keepdims=True) - normal * along), grad * normal


def add_rows(out_ref, values):
    @pl.when(pl.program_id(0) == 0)
    def _():
        out_ref[...] = jnp.zeros_like(out_ref)

    out_ref[...] += jnp.sum(values, axis=0, keepdims=True)


def enter_kernel(part, mirror, merge, gain, shift, qkv, hidden, normed, projected):
    value = part[...] + nn(mirror[...], merge[...])
    hidden[...] = value
    low = (row_stats(value)[0] * gain[...] + shift[...]).astype(bf16)
    normed[...] = low
    projected[...] = nn(low, qkv[...]).astype(bf16)


def enter(part, mirror, merge_low, gain, shift, qkv):
    tokens = part.shape[0]
    return pl.pallas_call(
        enter_kernel,
        grid=(tokens // TILE,),
        in_specs=[tiled(D), tiled(D), held((D, D)), held((1, D)), held((1, D)), held((D, 3 * D))],
        out_specs=[tiled(D), tiled(D), tiled(3 * D)],
        out_shape=[
            jax.ShapeDtypeStruct((tokens, D), f32),
            jax.ShapeDtypeStruct((tokens, D), bf16),
            jax.ShapeDtypeStruct((tokens, 3 * D), bf16),
        ],
        compiler_params=settings(40),
        cost_estimate=cost(8 * tokens * D * D, 26 * MIB),
        name="enter",
    )(part, mirror, merge_low, gain, shift, qkv)


def leave_kernel(hidden, mixed, out_weight, gain, shift, residual, normed):
    value = hidden[...] + nn(mixed[...], out_weight[...])
    residual[...] = value
    normed[...] = (row_stats(value)[0] * gain[...] + shift[...]).astype(bf16)


def leave(hidden, mixed, out_weight, gain, shift):
    tokens = hidden.shape[0]
    return pl.pallas_call(
        leave_kernel,
        grid=(tokens // TILE,),
        in_specs=[tiled(D), tiled(D), held((D, D)), held((1, D)), held((1, D))],
        out_specs=[tiled(D), tiled(D)],
        out_shape=[jax.ShapeDtypeStruct((tokens, D), f32), jax.ShapeDtypeStruct((tokens, D), bf16)],
        compiler_params=settings(32),
        cost_estimate=cost(2 * tokens * D * D, 14 * MIB),
        name="leave",
    )(hidden, mixed, out_weight, gain, shift)


def windows(lengths):
    ends = jnp.cumsum(lengths, axis=1)
    starts = ends - lengths
    low = (jnp.arange(BLOCKS, dtype=jnp.int32) * BLOCK)[None, :, None]
    holds_low = (low >= starts[:, None, :]) & (low < ends[:, None, :])
    high = low + (BLOCK - 1)
    holds_high = (high >= starts[:, None, :]) & (high < ends[:, None, :])
    window_low = jnp.sum(jnp.where(holds_low, starts[:, None, :], 0), axis=2) // BLOCK
    window_high = (jnp.sum(jnp.where(holds_high, ends[:, None, :], 0), axis=2) + BLOCK - 1) // BLOCK
    return window_low.reshape(-1), (window_high - window_low).reshape(-1)


def row_segments(lengths):
    ends = jnp.cumsum(lengths, axis=1)
    position = jnp.arange(ROW_LEN, dtype=jnp.int32)
    return jnp.sum((position[None, :, None] >= ends[:, None, :]).astype(jnp.int32), axis=2)


def head_slopes():
    return jnp.array([2.0 ** (-8.0 * (head + 1.0) / H) for head in range(H)], f32)


def fill_distance(far_ref, column, line):
    for b in range(BLOCKS):
        rows = slice(b * BLOCK, (b + 1) * BLOCK)
        i = lax.broadcasted_iota(jnp.int32, (BLOCK, ROW_LEN), 0) + b * BLOCK
        j = lax.broadcasted_iota(jnp.int32, (BLOCK, ROW_LEN), 1)
        distance = jnp.abs(i - j).astype(f32)
        far_ref[rows, :] = jnp.where(column[rows, :] == line[...], distance, FAR)


def masked_pair(value, lows):
    zero = jnp.zeros_like(value)
    return jnp.concatenate([jnp.where(lows, value, zero), jnp.where(lows, zero, value)], axis=0)


def over_blocks(low_ref, count_ref, row, variant):
    def block(b, carry):
        rows = pl.ds(pl.multiple_of(b * BLOCK, BLOCK), BLOCK)
        start = pl.multiple_of(low_ref[row * BLOCKS + b] * BLOCK, BLOCK)
        count = count_ref[row * BLOCKS + b]
        for n in range(1, BLOCKS + 1):
            pl.when(count == n)(functools.partial(variant, rows, pl.ds(start, n * BLOCK)))
        return carry

    lax.fori_loop(0, BLOCKS, block, 0)


def attend_kernel(
    low_ref, count_ref, slope_ref, column, line, q_ref, k_ref, v_ref, o_ref, lse_ref, far_ref, value_ref
):
    row = pl.program_id(0)
    group = pl.program_id(1)

    @pl.when(group == 0)
    def _():
        fill_distance(far_ref, column, line)
        lse_ref[...] = jnp.zeros_like(lse_ref)

    lane = lax.broadcasted_iota(jnp.int32, (1, 128), 1)
    lows = lane < HD
    for pair in range(HEADS // 2):
        value_ref[pair, :, :128] = v_ref[:, pair * 128 : pair * 128 + 128]
        value_ref[pair, :, 128:] = jnp.ones((ROW_LEN, 128), bf16)

    def variant(rows, cols):
        far = far_ref[rows, cols]
        logs = lse_ref[rows, :]
        for pair in range(HEADS // 2):
            at = slice(pair * 128, pair * 128 + 128)
            head = group * HEADS + pair * 2
            query = masked_pair(q_ref[rows, at] * bf16(HD**-0.5), lows)
            score = nt(query, k_ref[cols, at])
            score = score - jnp.concatenate([slope_ref[head] * far, slope_ref[head + 1] * far], axis=0)
            top = jnp.max(score, axis=1, keepdims=True)
            soft = jnp.exp(score - top).astype(bf16)
            both = nn(soft, value_ref[pair, cols, :])
            total = both[:, 128:]
            log_total = top + jnp.log(total)
            logs = jnp.where(lane == head, log_total[:BLOCK], logs)
            logs = jnp.where(lane == head + 1, log_total[BLOCK:], logs)
            mixed = jnp.where(lows, both[:BLOCK, :128], both[BLOCK:, :128])
            o_ref[rows, at] = (mixed / jnp.where(lows, total[:BLOCK], total[BLOCK:])).astype(bf16)
        lse_ref[rows, :] = logs

    over_blocks(low_ref, count_ref, row, variant)


def head_group(part):
    return pl.BlockSpec((ROW_LEN, HEADS * HD), lambda r, g, *_: (r, part * GROUPS + g))


def attention_operands(lengths):
    rows = lengths.shape[0]
    segments = row_segments(lengths)
    return windows(lengths) + (
        head_slopes(),
        segments.reshape(rows * ROW_LEN, 1),
        segments.reshape(rows, 1, ROW_LEN),
    )


def segment_specs():
    return [
        pl.BlockSpec((ROW_LEN, 1), lambda r, g, *_: (r, 0)),
        pl.BlockSpec((None, 1, ROW_LEN), lambda r, g, *_: (r, 0, 0)),
    ]


def attend(projected, operands):
    tokens = projected.shape[0]
    rows = tokens // ROW_LEN
    return pl.pallas_call(
        attend_kernel,
        out_shape=[jax.ShapeDtypeStruct((tokens, D), bf16), jax.ShapeDtypeStruct((tokens, 128), f32)],
        grid_spec=pltpu.PrefetchScalarGridSpec(
            num_scalar_prefetch=3,
            grid=(rows, GROUPS),
            in_specs=segment_specs() + [head_group(0), head_group(1), head_group(2)],
            out_specs=[head_group(0), pl.BlockSpec((ROW_LEN, 128), lambda r, g, *_: (r, 0))],
            scratch_shapes=[
                pltpu.VMEM((ROW_LEN, ROW_LEN), f32),
                pltpu.VMEM((HEADS // 2, ROW_LEN, 256), bf16),
            ],
        ),
        compiler_params=settings(48),
        cost_estimate=cost(rows * 20e9, 30 * MIB),
        name="attend",
    )(*operands, projected, projected, projected)


def attend_back_kernel(
    low_ref,
    count_ref,
    slope_ref,
    column,
    line,
    q_ref,
    k_ref,
    v_ref,
    grad_ref,
    lse_ref,
    delta_ref,
    out_ref,
    far_ref,
    turned_ref,
    key_ref,
):
    row = pl.program_id(0)
    group = pl.program_id(1)

    @pl.when(group == 0)
    def _():
        fill_distance(far_ref, column, line)

    lows = lax.broadcasted_iota(jnp.int32, (1, 128), 1) < HD
    tops = lax.broadcasted_iota(jnp.int32, (128, 1), 0) < HD
    turned_ref[...] = jnp.zeros_like(turned_ref)
    for pair in range(HEADS // 2):
        key_ref[pair] = k_ref[:, pair * 128 : pair * 128 + 128].T

    def variant(rows, cols):
        far = far_ref[rows, cols]
        for pair in range(HEADS // 2):
            at = slice(pair * 128, pair * 128 + 128)
            head = group * HEADS + pair * 2
            query = q_ref[cols, at] * bf16(HD**-0.5)
            grad = grad_ref[cols, at]
            score = nt(masked_pair(k_ref[rows, at], lows), query)
            soft_grad = nt(masked_pair(v_ref[rows, at], lows), grad)
            softs, score_grads = [], []
            for side in range(2):
                part = slice(side * BLOCK, side * BLOCK + BLOCK)
                own = pl.ds(pair * 2 + side, 1)
                soft = jnp.exp(score[part] - slope_ref[head + side] * far - lse_ref[own, cols])
                score_grads.append((soft * (soft_grad[part] - delta_ref[own, cols])).astype(bf16))
                softs.append(soft.astype(bf16))
            score_grad = jnp.concatenate(score_grads, axis=0)
            value_grad = nn(jnp.concatenate(softs, axis=0), grad)
            key_grad = nn(score_grad, query)
            out_ref[2, rows, at] = jnp.where(lows, value_grad[:BLOCK], value_grad[BLOCK:]).astype(bf16)
            out_ref[1, rows, at] = jnp.where(lows, key_grad[:BLOCK], key_grad[BLOCK:]).astype(bf16)
            key = key_ref[pair, :, rows]
            zero = jnp.zeros_like(key)
            keys = jnp.concatenate([jnp.where(tops, key, zero), jnp.where(tops, zero, key)], axis=1)
            turned_ref[at, cols] += nn(keys, score_grad)

    over_blocks(low_ref, count_ref, row, variant)
    out_ref[0] = (turned_ref[...].T * HD**-0.5).astype(bf16)


def attend_back(projected, grad, lse_rows, delta_rows, operands):
    tokens = projected.shape[0]
    rows = tokens // ROW_LEN
    thin = pl.BlockSpec((None, HEADS, ROW_LEN), lambda r, g, *_: (r, g, 0))
    return pl.pallas_call(
        attend_back_kernel,
        out_shape=jax.ShapeDtypeStruct((3, tokens, D), bf16),
        grid_spec=pltpu.PrefetchScalarGridSpec(
            num_scalar_prefetch=3,
            grid=(rows, GROUPS),
            in_specs=segment_specs()
            + [head_group(0), head_group(1), head_group(2), head_group(0), thin, thin],
            out_specs=pl.BlockSpec((3, ROW_LEN, HEADS * HD), lambda r, g, *_: (0, r, g)),
            scratch_shapes=[
                pltpu.VMEM((ROW_LEN, ROW_LEN), f32),
                pltpu.VMEM((HEADS * HD, ROW_LEN), f32),
                pltpu.VMEM((HEADS // 2, 128, ROW_LEN), bf16),
            ],
        ),
        compiler_params=settings(48),
        cost_estimate=cost(rows * 30e9, 30 * MIB),
        name="attend_back",
    )(*operands, projected, projected, projected, grad, lse_rows, delta_rows)


PULL = 0.44
ERFC = (
    0.1241083994,
    0.1244657618,
    0.1084788423,
    0.1084610390,
    -0.0110834557,
    0.1493682951,
    -0.1395405297,
    0.0357417408,
)


def gelu_pair(value):
    size = jnp.abs(value)
    t = 1.0 / (1.0 + (PULL * 0.5**0.5) * size)
    poly = jnp.full_like(t, ERFC[-1])
    for term in reversed(ERFC[:-1]):
        poly = poly * t + term
    bell = jnp.exp(value * value * -0.5)
    tail = bell * t * poly
    whole = jnp.where(value < 0, tail, 1.0 - tail)
    return value * whole, whole + value * (bell * (0.5 / jnp.pi) ** 0.5)


def feed_kernel(
    rows_up,
    rows_down,
    core_ref,
    normed,
    cotangent,
    residual,
    down_bias,
    up_weight,
    up_bias,
    down_weight,
    back,
    output,
    normed_grad,
    bias_grad,
    up_sent,
    up_kept,
    down_sent,
    down_kept,
    total,
):
    step = pl.program_id(0)
    core = core_ref[0]

    @pl.when(step == 0)
    def _():
        total[...] = residual[...] + down_bias[...]
        normed_grad[...] = jnp.zeros_like(normed_grad)

    value = nn(normed[...], up_weight[...]) + up_bias[...]
    active, slope = gelu_pair(value)
    active = active.astype(bf16)
    grad = (back[...].astype(f32) * slope).astype(bf16)
    bias_grad[...] = jnp.sum(grad.astype(f32), axis=0, keepdims=True)
    total[...] += nn(active, down_weight[...])
    normed_grad[...] += nt(grad, up_weight[...])
    down_sent[...], down_kept[...] = split_rows(tn(active, cotangent[...]), core, rows_down)
    up_sent[...], up_kept[...] = split_rows(tn(normed[...], grad), core, rows_up)

    @pl.when(step == pl.num_programs(0) - 1)
    def _():
        output[...] = total[...].astype(bf16)


def feed(core, normed, cotangent, residual, down_bias, up_weight, up_bias, down_weight, back, width=512):
    tokens = normed.shape[0]
    hidden_units = up_weight.shape[1]
    devices = lax.axis_size("half") * lax.axis_size("dp")
    across = lambda rows: pl.BlockSpec((rows, width), lambda i: (0, i))
    down = lambda rows: pl.BlockSpec((rows, D), lambda i: (i, 0))
    shape = jax.ShapeDtypeStruct
    return pl.pallas_call(
        functools.partial(feed_kernel, D // devices, hidden_units // devices),
        grid=(hidden_units // width,),
        in_specs=[
            pl.BlockSpec(memory_space=pltpu.SMEM),
            held((tokens, D)),
            held((tokens, D)),
            held((tokens, D)),
            held((1, D)),
            across(D),
            across(1),
            down(width),
            across(tokens),
        ],
        out_specs=[
            pl.BlockSpec((tokens, D), lambda i: (0, 0)),
            pl.BlockSpec((tokens, D), lambda i: (0, 0)),
            across(1),
            across(D // 2),
            across(D // 2),
            down(width // 2),
            down(width // 2),
        ],
        out_shape=[
            shape((tokens, D), bf16),
            shape((tokens, D), f32),
            shape((1, hidden_units), f32),
            shape((D // 2, hidden_units), bf16),
            shape((D // 2, hidden_units), bf16),
            shape((hidden_units // 2, D), bf16),
            shape((hidden_units // 2, D), bf16),
        ],
        scratch_shapes=[pltpu.VMEM((tokens, D), f32)],
        compiler_params=settings(60),
        cost_estimate=cost(10 * tokens * D * hidden_units, 60 * MIB),
        name="feed",
    )(core, normed, cotangent, residual, down_bias, up_weight, up_bias, down_weight, back)


def second_back_kernel(
    normed_grad,
    residual,
    cotangent,
    gain,
    out_weight,
    mixed,
    lse,
    residual_grad,
    attention_grad,
    mixed_grad,
    delta_rows,
    lse_rows,
    gain_grad,
    shift_grad,
    bias_grad,
):
    incoming = normed_grad[...]
    outer = cotangent[...].astype(f32)
    through, gain_terms = norm_back(residual[...], gain[...], incoming)
    value = outer + through
    residual_grad[...] = value
    low = value.astype(bf16)
    attention_grad[...] = low
    mixed_low = nt(low, out_weight[...]).astype(bf16)
    mixed_grad[...] = mixed_low
    product = mixed_low.astype(f32) * mixed[...].astype(f32)
    high = product.astype(bf16)
    rest = (product - high.astype(f32)).astype(bf16)
    of_head = lax.broadcasted_iota(jnp.int32, (H, D), 1) // HD
    member = (of_head == lax.broadcasted_iota(jnp.int32, (H, D), 0)).astype(bf16)
    delta_rows[...] = nt(member, high) + nt(member, rest)
    lse_rows[...] = lse[...].T[:H]
    add_rows(gain_grad, gain_terms)
    add_rows(shift_grad, incoming)
    add_rows(bias_grad, outer)


def second_back(normed_grad, residual, cotangent, gain, out_weight, mixed, lse):
    tokens = residual.shape[0]
    per_row = ROW_LEN // TILE
    shape = jax.ShapeDtypeStruct
    thin = pl.BlockSpec((None, H, TILE), lambda i: (i // per_row, 0, i % per_row))
    return pl.pallas_call(
        second_back_kernel,
        grid=(tokens // TILE,),
        in_specs=[tiled(D), tiled(D), tiled(D), held((1, D)), held((D, D)), tiled(D), tiled(128)],
        out_specs=[tiled(D), tiled(D), tiled(D), thin, thin, summed_over(D), summed_over(D), summed_over(D)],
        out_shape=[
            shape((tokens, D), f32),
            shape((tokens, D), bf16),
            shape((tokens, D), bf16),
            shape((tokens // ROW_LEN, H, ROW_LEN), f32),
            shape((tokens // ROW_LEN, H, ROW_LEN), f32),
            shape((1, D), f32),
            shape((1, D), f32),
            shape((1, D), f32),
        ],
        compiler_params=settings(40),
        cost_estimate=cost(3 * tokens * D * D, 22 * MIB),
        name="second_back",
    )(normed_grad, residual, cotangent, gain, out_weight, mixed, lse)


def first_back_kernel(
    projected_grad, hidden, residual_grad, gain, qkv, merge, hidden_grad, frames_grad, skip_grad, gain_grad, shift_grad, bias_grad
):
    incoming = nt(projected_grad[0], qkv[:, :D])
    incoming += nt(projected_grad[1], qkv[:, D : 2 * D])
    incoming += nt(projected_grad[2], qkv[:, 2 * D :])
    through, gain_terms = norm_back(hidden[...], gain[...], incoming)
    low = (residual_grad[...] + through).astype(bf16)
    hidden_grad[...] = low
    skip_grad[...] = nt(low, merge[D:, :]).astype(bf16)
    frames_grad[...] = nt(low, merge[:D, :]).astype(bf16)
    add_rows(gain_grad, gain_terms)
    add_rows(shift_grad, incoming)
    add_rows(bias_grad, low.astype(f32))


def first_back(projected_grad, hidden, residual_grad, gain, qkv, merge):
    tokens = hidden.shape[0]
    shape = jax.ShapeDtypeStruct
    return pl.pallas_call(
        first_back_kernel,
        grid=(tokens // TILE,),
        in_specs=[
            pl.BlockSpec((3, TILE, D), lambda i: (0, i, 0)),
            tiled(D),
            tiled(D),
            held((1, D)),
            held((D, 3 * D)),
            held((2 * D, D)),
        ],
        out_specs=[tiled(D), tiled(D), tiled(D), summed_over(D), summed_over(D), summed_over(D)],
        out_shape=[shape((tokens, D), bf16)] * 3 + [shape((1, D), f32)] * 3,
        compiler_params=settings(48),
        cost_estimate=cost(10 * tokens * D * D, 32 * MIB),
        name="first_back",
    )(projected_grad, hidden, residual_grad, gain, qkv, merge)


def weight_kernel(rows_each, core_ref, left, right, sent, kept):
    sent[...], kept[...] = split_rows(tn(left[...], right[...]), core_ref[0], rows_each)


def weight_pair_kernel(rows_each, core_ref, first, second, right, sent, kept):
    half = sent.shape[0] // 2
    for at, left in enumerate((first, second)):
        rows = slice(at * half, at * half + half)
        sent[rows, :], kept[rows, :] = split_rows(tn(left[...], right[...]), core_ref[0], rows_each)


def weight_grad(core, lefts, right, right_spec, steps, width, name):
    tokens = lefts[0].shape[0]
    devices = lax.axis_size("half") * lax.axis_size("dp")
    rows = len(lefts) * D
    kernel = weight_kernel if len(lefts) == 1 else weight_pair_kernel
    out = pl.BlockSpec((rows // 2, width), lambda i: (0, i))
    return pl.pallas_call(
        functools.partial(kernel, rows // devices),
        grid=(steps,),
        in_specs=[pl.BlockSpec(memory_space=pltpu.SMEM)] + [held((tokens, D))] * len(lefts) + [right_spec],
        out_specs=[out, out],
        out_shape=[jax.ShapeDtypeStruct((rows // 2, steps * width), bf16)] * 2,
        compiler_params=settings(48),
        cost_estimate=cost(2 * tokens * rows * steps * width, 16 * MIB),
        name=name,
    )(core, *lefts, right)


def columns_of(tokens, width):
    return pl.BlockSpec((tokens, width), lambda i: (0, i))


def on_device(
    frames,
    skip_rows,
    lengths,
    merge_weight,
    merge_bias,
    norm1_gain,
    norm1_bias,
    qkv_weight,
    out_weight,
    norm2_gain,
    norm2_bias,
    up_weight,
    up_bias,
    down_weight,
    down_bias,
    cotangent,
):
    tokens = frames.shape[0]
    line = lambda vector: vector.reshape(1, -1)
    core = (lax.axis_index("dp") & 1).astype(jnp.int32).reshape(1)
    mirror = swapped(skip_rows, "half", 0)
    operands = attention_operands(lengths)
    back = nt(cotangent, down_weight).astype(bf16)
    part = nn(frames, merge_weight[:D]) + merge_bias
    hidden, normed, projected = enter(
        part, mirror, merge_weight[D:], line(norm1_gain), line(norm1_bias), qkv_weight
    )
    mixed, lse = attend(projected, operands)
    residual, normed_two = leave(hidden, mixed, out_weight, line(norm2_gain), line(norm2_bias))
    output, normed_two_grad, up_bias_grad, up_sent, up_kept, down_sent, down_kept = feed(
        core, normed_two, cotangent, residual, line(down_bias), up_weight, line(up_bias), down_weight, back
    )
    down_weight_grad = reduced((down_sent, down_kept), "x")
    up_weight_grad = reduced((up_sent, up_kept), "y")
    residual_grad, attention_grad, mixed_grad, delta_rows, lse_rows, gain_two, shift_two, down_bias_grad = (
        second_back(normed_two_grad, residual, cotangent, line(norm2_gain), out_weight, mixed, lse)
    )
    out_weight_grad = reduced(
        weight_grad(core, (mixed,), attention_grad, columns_of(tokens, 512), 2, 512, "out_grad"), "x"
    )
    projected_grad = attend_back(projected, mixed_grad, lse_rows, delta_rows, operands)
    hidden_grad, frames_grad, skip_part, gain_one, shift_one, merge_bias_grad = first_back(
        projected_grad, hidden, residual_grad, line(norm1_gain), qkv_weight, merge_weight
    )
    skip_grad = swapped(skip_part, "half", 0)
    third = pl.BlockSpec((None, tokens, D), lambda i: (i, 0, 0))
    qkv_weight_grad = reduced(weight_grad(core, (normed,), projected_grad, third, 3, D, "qkv_grad"), "yz")
    merge_weight_grad = reduced(
        weight_grad(core, (frames, mirror), hidden_grad, columns_of(tokens, 512), 2, 512, "merge_grad"), "yz"
    )
    vectors = reduced_vectors(
        (merge_bias_grad, gain_one, shift_one, gain_two, shift_two, up_bias_grad, down_bias_grad)
    )
    return (
        output,
        frames_grad,
        skip_grad,
        merge_weight_grad,
        vectors[0],
        vectors[1],
        vectors[2],
        qkv_weight_grad,
        out_weight_grad,
        vectors[3],
        vectors[4],
        up_weight_grad,
        vectors[5],
        down_weight_grad,
        vectors[6],
    )


def solution(mesh):
    rows = P(("half", "dp"), None)
    parts = P(("half", "dp"))
    in_specs = (rows, rows, rows) + (P(),) * 12 + (rows,)
    out_specs = (rows, rows, rows, rows, parts, parts, parts, rows, rows, parts, parts, rows, parts, rows, parts)
    return jax.shard_map(
        on_device, mesh=mesh, in_specs=in_specs, out_specs=out_specs, check_vma=False
    )
```

time: 1300 us -> 529 us (0.41)
  matrix products: 423 us -> 21.4 us
  waiting for transfers between devices: 545 us -> 195 us
  Pallas kernels: 0 us -> 206 us
  other arithmetic: 133 us -> 22.1 us
  blocking collectives: 80.7 us -> 0 us
  local copies, waits for them, and re-layouts: 80.3 us -> 24.3 us
  starting transfers between devices: 4.94 us -> 52.8 us
  between operations: 15 us -> 1.81 us
    reduce_scatter x5 -> x0, waiting for transfers between devices: 506 us -> none  [the longest x1 187 us: on_device(): lax.psum_scatter(down_weight_grad, ('half', 'dp'), scatter_dimension=0, t...]
    dot_general x29 -> x2, matrix products: 423 us -> 21.4 us  [the longest x1 14.8 us: nt(): lax.dot_general(left, right, (((1,), (1,)), ((), ())), preferred_element_...]
    pallas_call x0 -> x10, Pallas kernels: none -> 206 us  [the longest x1 72.1 us: feed(): pl.pallas_call(functools.partial(feed_kernel, D // devices, hidden_units...]
    ppermute x2 -> x40, waiting for transfers between devices: 39.1 us -> 195 us  [swapped(): return lax.ppermute(value, axis, pairs)]
    unnamed x1 -> x0, blocking collectives: 80.7 us -> none
    convert_element_type x8 -> x26, other arithmetic: 72.9 us -> 12.5 us  [the longest x5 7.89 us: reduced(): block = (kept.astype(f32) + got.astype(f32)).astype(bf16)]
    reduce_sum x10 -> x2, other arithmetic: 50.2 us -> 0.17 us  [the longest x1 0.09 us: windows(): jnp.sum(jnp.where(holds_high, ends[:, None, :], 0), axis=2) + BLOCK - 1]
    ppermute x2 -> x40, starting transfers between devices: 4.73 us -> 52.8 us  [swapped(): return lax.ppermute(value, axis, pairs)]
  transfers between devices with their start and end apart: 7 -> 40, of which waited for: 4 -> 23; matrix products, arithmetic and copies ran while one was open for 28% -> 9% of each run, Pallas kernels for 0% -> 4%
where the time goes in v2:
time: 529 us; the launch traced here: 523 us
  Pallas kernels  206 us (39%)
  waiting for transfers between devices  195 us (37%)
  starting transfers between devices  52.8 us (10%)
  local copies, waits for them, and re-layouts  24.3 us (5%)
  other arithmetic  22.1 us (4%)
  matrix products  21.4 us (4%)
    ppermute x40, waiting for transfers between devices, swapped(): return lax.ppermute(value, axis, pairs)  195 us
    pallas_call x1, Pallas kernels, feed(): pl.pallas_call(functools.partial(feed_kernel, D // devices, hidden_units...  72.1 us
    ppermute x40, starting transfers between devices, swapped(): return lax.ppermute(value, axis, pairs)  52.8 us
    pallas_call x1, Pallas kernels, attend_back(): pl.pallas_call(attend_back_kernel, out_shape=jax.ShapeDtypeStruct((3, tok...  34.3 us
    pallas_call x1, Pallas kernels, attend(): pl.pallas_call(attend_kernel, out_shape=[jax.ShapeDtypeStruct((tokens, D)...  26.3 us
    pallas_call x3, Pallas kernels, weight_grad(): pl.pallas_call(functools.partial(kernel, rows // devices), grid=(steps,),...  22.7 us
    pallas_call x1, Pallas kernels, first_back(): pl.pallas_call(first_back_kernel, grid=(tokens // TILE,), in_specs=[pl.Bl...  20.4 us
    pallas_call x1, Pallas kernels, enter(): pl.pallas_call(enter_kernel, grid=(tokens // TILE,), in_specs=[tiled(D),...  15.3 us
  transfers between devices with their start and end apart: 40, of which 23 were waited for; matrix products, arithmetic and copies ran while one was open for 9% of the time, Pallas kernels for 4%

profile of v2, /device:TPU:0, one launch (start us, length us, event | category | flops | bytes accessed | tf_op | source)
XLA Modules:
  0.0 523.2 jit_solution(12789070751862914439)
XLA Ops:
  0.6 3.0 collective-permute-start
  5.1 1.8 slice.40.merge
  7.2 6.5 %broadcast_add_fusion.part = f32[1024,1024]{1,0:T(8,128)} fusion(f32[1024]{0:T(1024)S(1)} %copy-done.25, bf16[1024,1024]{1,0:T(8,128)(2,1)} %first.1, bf16[2048,1024]{1,0:T(8,128)(2,1)} %merge.1), kind=kOutput, calls=%fused_computation.18 | convolution fusion | flops 2148532224 | bytes 8392704 | tf_op jit(solution)/shard_map/dot_general | solution.py:27
  13.9 14.8 %convolution_convert_fusion.back = bf16[1024,4096]{1,0:T(8,128)(2,1)} fusion(bf16[1024,1024]{1,0:T(8,128)(2,1)} %cotangent.3, bf16[4096,1024]{1,0:T(8,128)(2,1)} %down_weight.1), kind=kOutput, calls=%fused_computation.2 | convolution fusion | flops 8594128896 | bytes 18874368 | tf_op jit(solution)/shard_map/dot_general | solution.py:31
  28.7 20.9 %collective-permute-done.mirror.second = bf16[1024,1024]{1,0:T(8,128)(2,1)} collective-permute-done((bf16[1024,1024]{1,0:T(8,128)(2,1)}, bf16[1024,1024]{1,0:T(8,128)(2,1)}, u32[]{:S(2)}, u32[]{:S(2)}) %collective-permute-start) | collective-permute-done | bytes 2097184 | tf_op jit(solution)/shard_map/ppermute | solution.py:62
  49.6 15.3 %enter.1 = (f32[1024,1024]{1,0:T(8,128)S(1)}, bf16[1024,1024]{1,0:T(8,128)(2,1)S(1)}, bf16[1024,3072]{1,0:T(8,128)(2,1)}) custom-call(f32[1024,1024]{1,0:T(8,128)} %broadcast_add_fusion.part, bf16[1024,1024]{1,0:T(8,128)(2,1)} %collective-permute-done.mirror.second, bf16[1024,1024]{1,0:T(8,128)(2,1)S(1)} %slice.40.merge, f32[1,1024]{1,0:T(1,128)S(1)} %bitcast.210, ...), custom_call_target="tpu_custom_call" | custom-call | flops 8589934592 | bytes 27262976 | tf_op jit(solution)/shard_map/enter/pallas_call | solution.py:175
  66.3 26.3 %attend.1 = (bf16[1024,1024]{1,0:T(8,128)(2,1)S(1)}, f32[1024,128]{1,0:T(8,128)S(1)}) custom-call(s32[8]{0:T(128)S(1)} %get-tuple-element.88.low_ref, s32[8]{0:T(128)S(1)} %get-tuple-element.87.count_ref, f32[16]{0:T(128)S(1)} %copy-done.15, s32[1024,1]{1,0:T(8,128)S(1)} %copy.54.column, s32[1,1,1024]{2,1,0:T(1,128)S(1)} %bitcast.206, ...), custom_call_target="tpu_custom_call" | custom-call | flops 20000000000 | bytes 31457280 | tf_op jit(solution)/shard_map/attend/pallas_call | solution.py:323
  92.6 4.0 leave.1
  96.7 2.0 copy-done.5
  100.0 72.1 %feed.1 = (bf16[1024,1024]{1,0:T(8,128)(2,1)}, f32[1024,1024]{1,0:T(8,128)}, f32[1,4096]{1,0:T(1,128)}, bf16[512,4096]{1,0:T(8,128)(2,1)}, bf16[512,4096]{1,0:T(...) custom-call(s32[1]{0:T(128)} %bitcast.core_ref, bf16[1024,1024]{1,0:T(8,128)(2,1)} %copy-done.12, ...), custom_call_target="tpu_custom_call" | custom-call | flops 42949672960 | bytes 62914560 | tf_op jit(solution)/shard_map/feed/pallas_call | solution.py:503
  175.2 11.2 %second_back.1 = (f32[1024,1024]{1,0:T(8,128)}, bf16[1024,1024]{1,0:T(8,128)(2,1)S(1)}, bf16[1024,1024]{1,0:T(8,128)(2,1)S(1)}, f32[1,16,1024]{2,1,0:T(8,128)S(1...) custom-call(f32[1024,1024]{1,0:T(8,128)} %get-tuple-element.55.normed_gra, ...), custom_call_target="tpu_custom_call" | custom-call | flops 3221225472 | bytes 23068672 | tf_op jit(solution)/shard_map/second_back/pallas_call | solution.py:585
  187.8 34.3 %attend_back.1.projected_grad.right = bf16[3,1024,1024]{2,1,0:T(8,128)(2,1)} custom-call(s32[8]{0:T(128)S(1)} %get-tuple-element.88.low_ref, s32[8]{0:T(128)S(1)} %get-tuple-element.87.count_ref, f32[16]{0:T(128)S(1)} %copy-done.15, s32[1024,1]{1,0:T(8,128)S(1)} %copy.54.column, s32[1,1,1024]{2,1,0:T(1,128)S(1)} %bitcast.207, ...), custom_call_target="tpu_custom_call" | custom-call | flops 30000001024 | bytes 31457280 | tf_op jit(solution)/shard_map/attend_back/pallas_call | solution.py:406
  222.1 20.4 %first_back.1 = (bf16[1024,1024]{1,0:T(8,128)(2,1)S(1)}, bf16[1024,1024]{1,0:T(8,128)(2,1)}, bf16[1024,1024]{1,0:T(8,128)(2,1)S(1)}, f32[1,1024]{1,0:T(1,128)S(1...) custom-call(bf16[3,1024,1024]{2,1,0:T(8,128)(2,1)} %attend_back.1.projected_grad.right, f32[1024,1024]{1,0:T(8,128)} %copy-done.4, ...), custom_call_target="tpu_custom_call" | custom-call | flops 10737418240 | bytes 33554432 | tf_op jit(solution)/shard_map/first_back/pallas_call | solution.py:625
  250.5 2.0 collective-permute-start.11
  252.6 4.0 out_grad.1
  256.7 3.8 collective-permute-start.12
  260.5 8.4 %merge_grad.1 = (bf16[1024,1024]{1,0:T(8,128)(2,1)}, bf16[1024,1024]{1,0:T(8,128)(2,1)S(1)}) custom-call(s32[1]{0:T(128)} %bitcast.core_ref, bf16[1024,1024]{1,0:T(8,128)(2,1)} %first.1, bf16[1024,1024]{1,0:T(8,128)(2,1)} %collective-permute-done.mirror.second, bf16[1024,1024]{1,0:T(8,128)(2,1)} %copy-done.16), custom_call_target="tpu_custom_call" | custom-call | flops 4294967296 | bytes 16777216 | tf_op jit(solution)/shard_map/merge_grad/pallas_call | solution.py:661
  268.9 8.8 %collective-permute-start.13 = (f32[2,2,320]{2,1,0:T(2,128)S(1)}, f32[2,2,320]{2,1,0:T(2,128)S(1)}, u32[]{:S(2)}, u32[]{:S(2)}) collective-permute-start(f32[2,2,320]{2,1,0:T(2,128)S(1)} %bitcast.225), channel_id=1, source_target_pairs={{0,2},{1,3},{2,0},{3,1},{4,6},{5,7},{6,4},{7,5},{8,10},{9,11},{10,... | collective-permute-start | bytes 15368 | tf_op jit(solution)/shard_map/ppermute | solution.py:62
  279.1 2.0 collective-permute-start.26
  281.2 3.5 collective-permute-done.14
  286.0 7.5 %collective-permute-done.26 = bf16[2,2,2,32,1024]{4,3,0,1,2:T(8,128)(2,1)S(1)} collective-permute-done((bf16[2,2,2,32,1024]{4,3,0,1,2:T(8,128)(2,1)}, bf16[2,2,2,32,1024]{4,3,0,1,2:T(8,128)(2,1)S(1)}, u32[]{:S(2)}, u32[]{:S(2)}) %collective-permute-start.26) | collective-permute-done | bytes 524320 | tf_op jit(solution)/shard_map/ppermute | solution.py:62
  294.1 10.3 %qkv_grad.1 = (bf16[512,3072]{1,0:T(8,128)(2,1)S(1)}, bf16[512,3072]{1,0:T(8,128)(2,1)}) custom-call(s32[1]{0:T(128)} %bitcast.core_ref, bf16[1024,1024]{1,0:T(8,128)(2,1)S(1)} %copy-done.18, bf16[3,1024,1024]{2,1,0:T(8,128)(2,1)} %attend_back.1.projected_grad.right), custom_call_target="tpu_custom_call" | custom-call | flops 6442450944 | bytes 16777216 | tf_op jit(solution)/shard_map/qkv_grad/pallas_call | solution.py:661
  304.6 1.8 collective-permute-start.1
  307.7 2.6 add_convert_fusion.3
  310.8 1.8 collective-permute-start.3
  314.7 3.9 collective-permute-done.29
  320.5 32.0 %collective-permute-done.1 = bf16[1024,1024]{1,0:T(8,128)(2,1)S(1)} collective-permute-done((bf16[1024,1024]{1,0:T(8,128)(2,1)S(1)}, bf16[1024,1024]{1,0:T(8,128)(2,1)S(1)}, u32[]{:S(2)}, u32[]{:S(2)}) %collective-permute-start.1) | collective-permute-done | bytes 2097184 | tf_op jit(solution)/shard_map/ppermute | solution.py:62
  352.8 1.8 collective-permute-start.4
  354.8 1.8 collective-permute-start.8
  356.6 5.0 collective-permute-done.4
  362.9 6.3 %collective-permute-done.8 = bf16[2,2,64,512]{3,2,0,1:T(8,128)(2,1)S(1)} collective-permute-done((bf16[2,2,64,512]{3,2,0,1:T(8,128)(2,1)S(1)}, bf16[2,2,64,512]{3,2,0,1:T(8,128)(2,1)S(1)}, u32[]{:S(2)}, u32[]{:S(2)}) %collective-permute-start.8) | collective-permute-done | bytes 262176 | tf_op jit(solution)/shard_map/ppermute | solution.py:62
  369.3 1.6 collective-permute-start.9
  372.8 2.0 collective-permute-done.9
  377.2 1.8 collective-permute-start.17
  380.6 14.7 %collective-permute-done.17 = bf16[2,2,2,32,1536]{4,3,1,2,0:T(8,128)(2,1)S(1)} collective-permute-done((bf16[2,2,2,32,1536]{4,3,1,2,0:T(8,128)(2,1)S(1)}, bf16[2,2,2,32,1536]{4,3,1,2,0:T(8,128)(2,1)S(1)}, u32[]{:S(2)}, u32[]{:S(2)}) %collective-permute-start.17) | collective-permute-done | bytes 786464 | tf_op jit(solution)/shard_map/ppermute | solution.py:62
  396.3 1.7 collective-permute-start.18
  399.8 2.2 add_convert_fusion
  406.9 1.6 collective-permute-start.31
  409.8 8.3 %collective-permute-done.22 = bf16[2,2,32,1536]{3,2,0,1:T(8,128)(2,1)S(1)} collective-permute-done((bf16[2,2,32,1536]{3,2,0,1:T(8,128)(2,1)}, bf16[2,2,32,1536]{3,2,0,1:T(8,128)(2,1)S(1)}, u32[]{:S(2)}, u32[]{:S(2)}) %collective-permute-start.22) | collective-permute-done | bytes 393248 | tf_op jit(solution)/shard_map/ppermute | solution.py:62
  418.9 2.3 collective-permute-done.19
  421.4 35.2 %collective-permute-done.23 = bf16[2,32,1536]{2,1,0:T(8,128)(2,1)S(1)} collective-permute-done((bf16[2,32,1536]{2,1,0:T(8,128)(2,1)S(1)}, bf16[2,32,1536]{2,1,0:T(8,128)(2,1)S(1)}, u32[]{:S(2)}, u32[]{:S(2)}) %collective-permute-start.23) | collective-permute-done | bytes 196640 | tf_op jit(solution)/shard_map/ppermute | solution.py:62
  462.8 17.4 %collective-permute-done.37 = bf16[2,2,128,1024]{3,2,0,1:T(8,128)(2,1)S(1)} collective-permute-done((bf16[2,2,128,1024]{3,2,0,1:T(8,128)(2,1)S(1)}, bf16[2,2,128,1024]{3,2,0,1:T(8,128)(2,1)S(1)}, u32[]{:S(2)}, u32[]{:S(2)}) %collective-permute-start.37) | collective-permute-done | bytes 1048608 | tf_op jit(solution)/shard_map/ppermute | solution.py:62
  481.0 2.6 collective-permute-done.32
  484.7 13.8 %collective-permute-done.38 = bf16[2,128,1024]{2,1,0:T(8,128)(2,1)S(1)} collective-permute-done((bf16[2,128,1024]{2,1,0:T(8,128)(2,1)S(1)}, bf16[2,128,1024]{2,1,0:T(8,128)(2,1)S(1)}, u32[]{:S(2)}, u32[]{:S(2)}) %collective-permute-start.38) | collective-permute-done | bytes 524320 | tf_op jit(solution)/shard_map/ppermute | solution.py:62
  499.5 6.9 %collective-permute-done.33 = bf16[2,32,4096]{2,1,0:T(8,128)(2,1)S(1)} collective-permute-done((bf16[2,32,4096]{2,1,0:T(8,128)(2,1)S(1)}, bf16[2,32,4096]{2,1,0:T(8,128)(2,1)S(1)}, u32[]{:S(2)}, u32[]{:S(2)}) %collective-permute-start.33) | collective-permute-done | bytes 524320 | tf_op jit(solution)/shard_map/ppermute | solution.py:62
  506.5 3.0 collective-permute-start.34
  510.3 7.4 %collective-permute-done.39 = bf16[128,1024]{1,0:T(8,128)(2,1)S(1)} collective-permute-done((bf16[128,1024]{1,0:T(8,128)(2,1)S(1)}, bf16[128,1024]{1,0:T(8,128)(2,1)S(1)}, u32[]{:S(2)}, u32[]{:S(2)}) %collective-permute-start.39) | collective-permute-done | bytes 262176 | tf_op jit(solution)/shard_map/ppermute | solution.py:62
  518.6 2.2 collective-permute-done.34
  (206 shorter events, 56.8 us)
Async XLA Ops:
  0.6 49.0 %collective-permute-start = (bf16[1024,1024]{1,0:T(8,128)(2,1)}, bf16[1024,1024]{1,0:T(8,128)(2,1)}, u32[]{:S(2)}, u32[]{:S(2)}) collective-permute-start(bf16[1024,1024]{1,0:T(8,128)(2,1)} %param.18), channel_id=1, source_target_pairs={{0,16},{16,0},{1,17},{17,1},{2,18},{18,2},{3,19},{19,3},{4,20},{20... | collective-permute-start | bytes 6291464 | tf_op jit(solution)/shard_map/ppermute | solution.py:62
  13.9 35.7 %copy-start.13 = (f32[1024]{0:T(1024)S(1)}, f32[1024]{0:T(1024)}, u32[]{:S(2)}) copy-start(f32[1024]{0:T(1024)} %param.23) | copy-start | bytes 12292
  13.9 35.7 %copy-start.14 = (f32[1024]{0:T(1024)S(1)}, f32[1024]{0:T(1024)}, u32[]{:S(2)}) copy-start(f32[1024]{0:T(1024)} %param.22) | copy-start | bytes 12292
  66.2 26.4 %copy-start.4 = (f32[1024,1024]{1,0:T(8,128)}, f32[1024,1024]{1,0:T(8,128)S(1)}, u32[]{:S(2)}) copy-start(f32[1024,1024]{1,0:T(8,128)S(1)} %get-tuple-element.49.hidden) | copy-start | bytes 12582916
  66.2 26.4 %copy-start = (bf16[1024,1024]{1,0:T(8,128)(2,1)S(1)}, bf16[1024,1024]{1,0:T(8,128)(2,1)}, u32[]{:S(2)}) copy-start(bf16[1024,1024]{1,0:T(8,128)(2,1)} %out_weight.3) | copy-start | bytes 6291460
  66.2 26.4 %copy-start.7 = (f32[1024]{0:T(1024)S(1)}, f32[1024]{0:T(1024)}, u32[]{:S(2)}) copy-start(f32[1024]{0:T(1024)} %param.26) | copy-start | bytes 12292
  66.2 26.4 %copy-start.8 = (f32[1024]{0:T(1024)S(1)}, f32[1024]{0:T(1024)}, u32[]{:S(2)}) copy-start(f32[1024]{0:T(1024)} %param.27) | copy-start | bytes 12292
  222.1 28.1 %copy-start.24 = (f32[1,4096]{1,0:T(1,128)S(1)}, f32[1,4096]{1,0:T(1,128)}, u32[]{:S(2)}) copy-start(f32[1,4096]{1,0:T(1,128)} %get-tuple-element.71) | copy-start | bytes 49156
  222.1 30.5 %copy-start.3 = (bf16[1024,1024]{1,0:T(8,128)(2,1)S(1)}, bf16[1024,1024]{1,0:T(8,128)(2,1)}, u32[]{:S(2)}) copy-start(bf16[1024,1024]{1,0:T(8,128)(2,1)} %copy-done.1) | copy-start | bytes 6291460
  250.5 6.1 %collective-permute-start.11 = (f32[2,2,2,2,320]{4,3,2,1,0:T(2,128)S(1)}, f32[2,2,2,2,320]{4,3,2,1,0:T(2,128)S(1)}, u32[]{:S(2)}, u32[]{:S(2)}) collective-permute-start(f32[2,2,2,2,320]{4,3,2,1,0:T(2,128)S(1)} %bitcast.223), channel_id=1, source_target_pairs={{0,1},{1,0},{2,3},{3,2},{4,5},{5,4},{6,7},{7,6},{8,9},{9,8},{10,11... | collective-permute-start | bytes 61448 | tf_op jit(solution)/shard_map/ppermute | solution.py:62
  256.6 21.1 %collective-permute-start.25 = (bf16[512,1024]{1,0:T(8,128)(2,1)S(1)}, bf16[512,1024]{1,0:T(8,128)(2,1)S(1)}, u32[]{:S(2)}, u32[]{:S(2)}) collective-permute-start(bf16[512,1024]{1,0:T(8,128)(2,1)S(1)} %get-tuple-element.78), channel_id=1, source_target_pairs={{0,1},{1,0},{2,3},{3,2},{4,5},{5,4},{6,7},{7,6},{8,9},{9,8},{10,11... | collective-permute-start | bytes 3145736 | tf_op jit(solution)/shard_map/ppermute | solution.py:62
  256.7 12.1 %collective-permute-start.12 = (f32[2,2,2,320]{3,2,1,0:T(2,128)S(1)}, f32[2,2,2,320]{3,2,1,0:T(2,128)S(1)}, u32[]{:S(2)}, u32[]{:S(2)}) collective-permute-start(f32[2,2,2,320]{3,2,1,0:T(2,128)S(1)} %fusion.27), channel_id=1, source_target_pairs={{0,16},{16,0},{1,17},{17,1},{2,18},{18,2},{3,19},{19,3},{4,20},{20... | collective-permute-start | bytes 30728 | tf_op jit(solution)/shard_map/ppermute | solution.py:62
  268.9 38.9 %collective-permute-start.2 = (bf16[1024,1024]{1,0:T(8,128)(2,1)}, bf16[1024,1024]{1,0:T(8,128)(2,1)}, u32[]{:S(2)}, u32[]{:S(2)}) collective-permute-start(bf16[1024,1024]{1,0:T(8,128)(2,1)} %get-tuple-element.65), channel_id=1, source_target_pairs={{0,1},{1,0},{2,3},{3,2},{4,5},{5,4},{6,7},{7,6},{8,9},{9,8},{10,11... | collective-permute-start | bytes 6291464 | tf_op jit(solution)/shard_map/ppermute | solution.py:62
  268.9 12.1 %collective-permute-start.13 = (f32[2,2,320]{2,1,0:T(2,128)S(1)}, f32[2,2,320]{2,1,0:T(2,128)S(1)}, u32[]{:S(2)}, u32[]{:S(2)}) collective-permute-start(f32[2,2,320]{2,1,0:T(2,128)S(1)} %bitcast.225), channel_id=1, source_target_pairs={{0,2},{1,3},{2,0},{3,1},{4,6},{5,7},{6,4},{7,5},{8,10},{9,11},{10,... | collective-permute-start | bytes 15368 | tf_op jit(solution)/shard_map/ppermute | solution.py:62
  279.1 14.5 %collective-permute-start.26 = (bf16[2,2,2,32,1024]{4,3,0,1,2:T(8,128)(2,1)}, bf16[2,2,2,32,1024]{4,3,0,1,2:T(8,128)(2,1)S(1)}, u32[]{:S(2)}, u32[]{:S(2)}) collective-permute-start(bf16[2,2,2,32,1024]{4,3,0,1,2:T(8,128)(2,1)} %bitcast.199), channel_id=1, source_target_pairs={{0,16},{16,0},{1,17},{17,1},{2,18},{18,2},{3,19},{19,3},{4,20},{20... | collective-permute-start | bytes 1572872 | tf_op jit(solution)/shard_map/ppermute | solution.py:62
  281.1 3.7 collective-permute-start.14
  281.2 118.6 %collective-permute-start.35 = (bf16[2048,1024]{1,0:T(8,128)(2,1)}, bf16[2048,1024]{1,0:T(8,128)(2,1)S(1)}, u32[]{:S(2)}, u32[]{:S(2)}) collective-permute-start(bf16[2048,1024]{1,0:T(8,128)(2,1)} %get-tuple-element.82), channel_id=1, source_target_pairs={{0,1},{1,0},{2,3},{3,2},{4,5},{5,4},{6,7},{7,6},{8,9},{9,8},{10,11... | collective-permute-start | bytes 12582920 | tf_op jit(solution)/shard_map/ppermute | solution.py:62
  284.8 19.8 %collective-permute-start.15 = (f32[320]{0:T(512)S(1)}, f32[320]{0:T(512)S(1)}, u32[]{:S(2)}, u32[]{:S(2)}) collective-permute-start(f32[320]{0:T(512)S(1)} %get-tuple-element.83), channel_id=1, source_target_pairs={{0,8},{1,9},{2,10},{3,11},{4,12},{5,13},{6,14},{7,15},{8,0},{9,1},... | collective-permute-start | bytes 3848 | tf_op jit(solution)/shard_map/ppermute | solution.py:62
  293.8 13.8 %collective-permute-start.27 = (bf16[2,2,32,1024]{3,2,0,1:T(8,128)(2,1)S(1)}, bf16[2,2,32,1024]{3,2,0,1:T(8,128)(2,1)S(1)}, u32[]{:S(2)}, u32[]{:S(2)}) collective-permute-start(bf16[2,2,32,1024]{3,2,0,1:T(8,128)(2,1)S(1)} %dynamic-slice_bitcast_fusion.8), channel_id=1, source_target_pairs={{0,2},{1,3},{2,0},{3,1},{4,6},{5,7},{6,4},{7,5},{8,10},{9,11},{10,... | collective-permute-start | bytes 786440 | tf_op jit(solution)/shard_map/ppermute | solution.py:62
  304.5 71.1 %collective-permute-start.16 = (bf16[512,3072]{1,0:T(8,128)(2,1)S(1)}, bf16[512,3072]{1,0:T(8,128)(2,1)S(1)}, u32[]{:S(2)}, u32[]{:S(2)}) collective-permute-start(bf16[512,3072]{1,0:T(8,128)(2,1)S(1)} %get-tuple-element.75), channel_id=1, source_target_pairs={{0,1},{1,0},{2,3},{3,2},{4,5},{5,4},{6,7},{7,6},{8,9},{9,8},{10,11... | collective-permute-start | bytes 9437192 | tf_op jit(solution)/shard_map/ppermute | solution.py:62
  304.6 48.0 %collective-permute-start.1 = (bf16[1024,1024]{1,0:T(8,128)(2,1)S(1)}, bf16[1024,1024]{1,0:T(8,128)(2,1)S(1)}, u32[]{:S(2)}, u32[]{:S(2)}) collective-permute-start(bf16[1024,1024]{1,0:T(8,128)(2,1)S(1)} %copy-done.10), channel_id=1, source_target_pairs={{0,16},{16,0},{1,17},{17,1},{2,18},{18,2},{3,19},{19,3},{4,20},{20... | collective-permute-start | bytes 6291464 | tf_op jit(solution)/shard_map/ppermute | solution.py:62
  307.7 5.6 %collective-permute-start.28 = (bf16[2,32,1024]{2,1,0:T(8,128)(2,1)S(1)}, bf16[2,32,1024]{2,1,0:T(8,128)(2,1)S(1)}, u32[]{:S(2)}, u32[]{:S(2)}) collective-permute-start(bf16[2,32,1024]{2,1,0:T(8,128)(2,1)S(1)} %dynamic-slice_bitcast_fusion.13), channel_id=1, source_target_pairs={{0,4},{1,5},{2,6},{3,7},{4,0},{5,1},{6,2},{7,3},{8,12},{9,13},{10,... | collective-permute-start | bytes 393224 | tf_op jit(solution)/shard_map/ppermute | solution.py:62
  310.8 41.8 %collective-permute-start.3 = (bf16[2,2,2,64,512]{4,3,1,2,0:T(8,128)(2,1)S(1)}, bf16[2,2,2,64,512]{4,3,1,2,0:T(8,128)(2,1)S(1)}, u32[]{:S(2)}, u32[]{:S(2)}) collective-permute-start(bf16[2,2,2,64,512]{4,3,1,2,0:T(8,128)(2,1)S(1)} %bitcast.221), channel_id=1, source_target_pairs={{0,2},{1,3},{2,0},{3,1},{4,6},{5,7},{6,4},{7,5},{8,10},{9,11},{10,... | collective-permute-start | bytes 1572872 | tf_op jit(solution)/shard_map/ppermute | solution.py:62
  313.3 5.3 %collective-permute-start.29 = (bf16[32,1024]{1,0:T(8,128)(2,1)S(1)}, bf16[32,1024]{1,0:T(8,128)(2,1)S(1)}, u32[]{:S(2)}, u32[]{:S(2)}) collective-permute-start(bf16[32,1024]{1,0:T(8,128)(2,1)S(1)} %dynamic-slice_bitcast_fusion.18), channel_id=1, source_target_pairs={{0,8},{1,9},{2,10},{3,11},{4,12},{5,13},{6,14},{7,15},{8,0},{9,1},... | collective-permute-start | bytes 196616 | tf_op jit(solution)/shard_map/ppermute | solution.py:62
  318.6 36.0 %collective-permute-start.7 = (bf16[2,2,2,64,512]{4,3,0,2,1:T(8,128)(2,1)S(1)}, bf16[2,2,2,64,512]{4,3,0,2,1:T(8,128)(2,1)S(1)}, u32[]{:S(2)}, u32[]{:S(2)}) collective-permute-start(bf16[2,2,2,64,512]{4,3,0,2,1:T(8,128)(2,1)S(1)} %bitcast.222), channel_id=1, source_target_pairs={{0,4},{1,5},{2,6},{3,7},{4,0},{5,1},{6,2},{7,3},{8,12},{9,13},{10,... | collective-permute-start | bytes 1572872 | tf_op jit(solution)/shard_map/ppermute | solution.py:62
  352.6 51.5 %collective-permute-start.30 = (bf16[512,4096]{1,0:T(8,128)(2,1)}, bf16[512,4096]{1,0:T(8,128)(2,1)S(1)}, u32[]{:S(2)}, u32[]{:S(2)}) collective-permute-start(bf16[512,4096]{1,0:T(8,128)(2,1)} %get-tuple-element.80), channel_id=1, source_target_pairs={{0,1},{1,0},{2,3},{3,2},{4,5},{5,4},{6,7},{7,6},{8,9},{9,8},{10,11... | collective-permute-start | bytes 12582920 | tf_op jit(solution)/shard_map/ppermute | solution.py:62
  352.8 8.8 %collective-permute-start.4 = (bf16[2,2,64,512]{3,2,0,1:T(8,128)(2,1)S(1)}, bf16[2,2,64,512]{3,2,0,1:T(8,128)(2,1)S(1)}, u32[]{:S(2)}, u32[]{:S(2)}) collective-permute-start(bf16[2,2,64,512]{3,2,0,1:T(8,128)(2,1)S(1)} %dynamic-slice_bitcast_fusion.10), channel_id=1, source_target_pairs={{0,16},{16,0},{1,17},{17,1},{2,18},{18,2},{3,19},{19,3},{4,20},{20... | collective-permute-start | bytes 786440 | tf_op jit(solution)/shard_map/ppermute | solution.py:62
  354.8 14.4 %collective-permute-start.8 = (bf16[2,2,64,512]{3,2,0,1:T(8,128)(2,1)S(1)}, bf16[2,2,64,512]{3,2,0,1:T(8,128)(2,1)S(1)}, u32[]{:S(2)}, u32[]{:S(2)}) collective-permute-start(bf16[2,2,64,512]{3,2,0,1:T(8,128)(2,1)S(1)} %dynamic-slice_bitcast_fusion.9), channel_id=1, source_target_pairs={{0,8},{1,9},{2,10},{3,11},{4,12},{5,13},{6,14},{7,15},{8,0},{9,1},... | collective-permute-start | bytes 786440 | tf_op jit(solution)/shard_map/ppermute | solution.py:62
  361.7 10.2 %collective-permute-start.5 = (bf16[2,64,512]{2,1,0:T(8,128)(2,1)S(1)}, bf16[2,64,512]{2,1,0:T(8,128)(2,1)S(1)}, u32[]{:S(2)}, u32[]{:S(2)}) collective-permute-start(bf16[2,64,512]{2,1,0:T(8,128)(2,1)S(1)} %dynamic-slice_bitcast_fusion.15), channel_id=1, source_target_pairs={{0,4},{1,5},{2,6},{3,7},{4,0},{5,1},{6,2},{7,3},{8,12},{9,13},{10,... | collective-permute-start | bytes 393224 | tf_op jit(solution)/shard_map/ppermute | solution.py:62
  369.3 5.5 %collective-permute-start.9 = (bf16[2,64,512]{2,1,0:T(8,128)(2,1)S(1)}, bf16[2,64,512]{2,1,0:T(8,128)(2,1)S(1)}, u32[]{:S(2)}, u32[]{:S(2)}) collective-permute-start(bf16[2,64,512]{2,1,0:T(8,128)(2,1)S(1)} %dynamic-slice_bitcast_fusion.14), channel_id=1, source_target_pairs={{0,2},{1,3},{2,0},{3,1},{4,6},{5,7},{6,4},{7,5},{8,10},{9,11},{10,... | collective-permute-start | bytes 393224 | tf_op jit(solution)/shard_map/ppermute | solution.py:62
  372.0 7.1 %collective-permute-start.6 = (bf16[64,512]{1,0:T(8,128)(2,1)S(1)}, bf16[64,512]{1,0:T(8,128)(2,1)S(1)}, u32[]{:S(2)}, u32[]{:S(2)}) collective-permute-start(bf16[64,512]{1,0:T(8,128)(2,1)S(1)} %dynamic-slice_bitcast_fusion.20), channel_id=1, source_target_pairs={{0,8},{1,9},{2,10},{3,11},{4,12},{5,13},{6,14},{7,15},{8,0},{9,1},... | collective-permute-start | bytes 196616 | tf_op jit(solution)/shard_map/ppermute | solution.py:62
  374.8 4.3 collective-permute-start.10
  377.2 18.1 %collective-permute-start.17 = (bf16[2,2,2,32,1536]{4,3,1,2,0:T(8,128)(2,1)S(1)}, bf16[2,2,2,32,1536]{4,3,1,2,0:T(8,128)(2,1)S(1)}, u32[]{:S(2)}, u32[]{:S(2)}) collective-permute-start(bf16[2,2,2,32,1536]{4,3,1,2,0:T(8,128)(2,1)S(1)} %bitcast.219), channel_id=1, source_target_pairs={{0,2},{1,3},{2,0},{3,1},{4,6},{5,7},{6,4},{7,5},{8,10},{9,11},{10,... | collective-permute-start | bytes 2359304 | tf_op jit(solution)/shard_map/ppermute | solution.py:62
  379.4 18.8 %collective-permute-start.21 = (bf16[2,2,2,32,1536]{4,3,0,2,1:T(8,128)(2,1)S(1)}, bf16[2,2,2,32,1536]{4,3,0,2,1:T(8,128)(2,1)S(1)}, u32[]{:S(2)}, u32[]{:S(2)}) collective-permute-start(bf16[2,2,2,32,1536]{4,3,0,2,1:T(8,128)(2,1)S(1)} %bitcast.220), channel_id=1, source_target_pairs={{0,4},{1,5},{2,6},{3,7},{4,0},{5,1},{6,2},{7,3},{8,12},{9,13},{10,... | collective-permute-start | bytes 2359304 | tf_op jit(solution)/shard_map/ppermute | solution.py:62
  396.3 12.2 %collective-permute-start.18 = (bf16[2,2,32,1536]{3,2,0,1:T(8,128)(2,1)}, bf16[2,2,32,1536]{3,2,0,1:T(8,128)(2,1)S(1)}, u32[]{:S(2)}, u32[]{:S(2)}) collective-permute-start(bf16[2,2,32,1536]{3,2,0,1:T(8,128)(2,1)} %dynamic-slice_bitcast_fusion.5), channel_id=1, source_target_pairs={{0,16},{16,0},{1,17},{17,1},{2,18},{18,2},{3,19},{19,3},{4,20},{20... | collective-permute-start | bytes 1179656 | tf_op jit(solution)/shard_map/ppermute | solution.py:62
  399.1 19.0 %collective-permute-start.22 = (bf16[2,2,32,1536]{3,2,0,1:T(8,128)(2,1)}, bf16[2,2,32,1536]{3,2,0,1:T(8,128)(2,1)S(1)}, u32[]{:S(2)}, u32[]{:S(2)}) collective-permute-start(bf16[2,2,32,1536]{3,2,0,1:T(8,128)(2,1)} %dynamic-slice_bitcast_fusion.4), channel_id=1, source_target_pairs={{0,8},{1,9},{2,10},{3,11},{4,12},{5,13},{6,14},{7,15},{8,0},{9,1},... | collective-permute-start | bytes 1179656 | tf_op jit(solution)/shard_map/ppermute | solution.py:62
  403.0 53.7 %collective-permute-start.36 = (bf16[2,2,2,128,1024]{4,3,0,1,2:T(8,128)(2,1)S(1)}, bf16[2,2,2,128,1024]{4,3,0,1,2:T(8,128)(2,1)S(1)}, u32[]{:S(2)}, u32[]{:S(2)}) collective-permute-start(bf16[2,2,2,128,1024]{4,3,0,1,2:T(8,128)(2,1)S(1)} %bitcast.217), channel_id=1, source_target_pairs={{0,16},{16,0},{1,17},{17,1},{2,18},{18,2},{3,19},{19,3},{4,20},{20... | collective-permute-start | bytes 6291464 | tf_op jit(solution)/shard_map/ppermute | solution.py:62
  406.9 52.8 %collective-permute-start.31 = (bf16[2,2,2,32,4096]{4,3,1,2,0:T(8,128)(2,1)S(1)}, bf16[2,2,2,32,4096]{4,3,1,2,0:T(8,128)(2,1)S(1)}, u32[]{:S(2)}, u32[]{:S(2)}) collective-permute-start(bf16[2,2,2,32,4096]{4,3,1,2,0:T(8,128)(2,1)S(1)} %bitcast.218), channel_id=1, source_target_pairs={{0,2},{1,3},{2,0},{3,1},{4,6},{5,7},{6,4},{7,5},{8,10},{9,11},{10,... | collective-permute-start | bytes 6291464 | tf_op jit(solution)/shard_map/ppermute | solution.py:62
  408.6 12.6 %collective-permute-start.19 = (bf16[2,32,1536]{2,1,0:T(8,128)(2,1)S(1)}, bf16[2,32,1536]{2,1,0:T(8,128)(2,1)S(1)}, u32[]{:S(2)}, u32[]{:S(2)}) collective-permute-start(bf16[2,32,1536]{2,1,0:T(8,128)(2,1)S(1)} %dynamic-slice_bitcast_fusion.12), channel_id=1, source_target_pairs={{0,4},{1,5},{2,6},{3,7},{4,0},{5,1},{6,2},{7,3},{8,12},{9,13},{10,... | collective-permute-start | bytes 589832 | tf_op jit(solution)/shard_map/ppermute | solution.py:62
  418.3 38.4 %collective-permute-start.23 = (bf16[2,32,1536]{2,1,0:T(8,128)(2,1)S(1)}, bf16[2,32,1536]{2,1,0:T(8,128)(2,1)S(1)}, u32[]{:S(2)}, u32[]{:S(2)}) collective-permute-start(bf16[2,32,1536]{2,1,0:T(8,128)(2,1)S(1)} %dynamic-slice_bitcast_fusion.11), channel_id=1, source_target_pairs={{0,2},{1,3},{2,0},{3,1},{4,6},{5,7},{6,4},{7,5},{8,10},{9,11},{10,... | collective-permute-start | bytes 589832 | tf_op jit(solution)/shard_map/ppermute | solution.py:62
  421.3 41.5 %collective-permute-start.20 = (bf16[32,1536]{1,0:T(8,128)(2,1)S(1)}, bf16[32,1536]{1,0:T(8,128)(2,1)S(1)}, u32[]{:S(2)}, u32[]{:S(2)}) collective-permute-start(bf16[32,1536]{1,0:T(8,128)(2,1)S(1)} %dynamic-slice_bitcast_fusion.17), channel_id=1, source_target_pairs={{0,8},{1,9},{2,10},{3,11},{4,12},{5,13},{6,14},{7,15},{8,0},{9,1},... | collective-permute-start | bytes 294920 | tf_op jit(solution)/shard_map/ppermute | solution.py:62
  458.1 22.2 %collective-permute-start.37 = (bf16[2,2,128,1024]{3,2,0,1:T(8,128)(2,1)S(1)}, bf16[2,2,128,1024]{3,2,0,1:T(8,128)(2,1)S(1)}, u32[]{:S(2)}, u32[]{:S(2)}) collective-permute-start(bf16[2,2,128,1024]{3,2,0,1:T(8,128)(2,1)S(1)} %dynamic-slice_bitcast_fusion), channel_id=1, source_target_pairs={{0,2},{1,3},{2,0},{3,1},{4,6},{5,7},{6,4},{7,5},{8,10},{9,11},{10,... | collective-permute-start | bytes 3145736 | tf_op jit(solution)/shard_map/ppermute | solution.py:62
  460.6 23.0 %collective-permute-start.32 = (bf16[2,2,32,4096]{3,2,0,1:T(8,128)(2,1)S(1)}, bf16[2,2,32,4096]{3,2,0,1:T(8,128)(2,1)S(1)}, u32[]{:S(2)}, u32[]{:S(2)}) collective-permute-start(bf16[2,2,32,4096]{3,2,0,1:T(8,128)(2,1)S(1)} %dynamic-slice_bitcast_fusion.1), channel_id=1, source_target_pairs={{0,16},{16,0},{1,17},{17,1},{2,18},{18,2},{3,19},{19,3},{4,20},{20... | collective-permute-start | bytes 3145736 | tf_op jit(solution)/shard_map/ppermute | solution.py:62
  461.9 22.8 %collective-permute-start.24 = (bf16[32,1536]{1,0:T(8,128)(2,1)S(1)}, bf16[32,1536]{1,0:T(8,128)(2,1)S(1)}, u32[]{:S(2)}, u32[]{:S(2)}) collective-permute-start(bf16[32,1536]{1,0:T(8,128)(2,1)S(1)} %dynamic-slice_bitcast_fusion.16), channel_id=1, source_target_pairs={{0,16},{16,0},{1,17},{17,1},{2,18},{18,2},{3,19},{19,3},{4,20},{20... | collective-permute-start | bytes 294920 | tf_op jit(solution)/shard_map/ppermute | solution.py:62
  480.7 17.7 %collective-permute-start.38 = (bf16[2,128,1024]{2,1,0:T(8,128)(2,1)S(1)}, bf16[2,128,1024]{2,1,0:T(8,128)(2,1)S(1)}, u32[]{:S(2)}, u32[]{:S(2)}) collective-permute-start(bf16[2,128,1024]{2,1,0:T(8,128)(2,1)S(1)} %dynamic-slice_bitcast_fusion.2), channel_id=1, source_target_pairs={{0,4},{1,5},{2,6},{3,7},{4,0},{5,1},{6,2},{7,3},{8,12},{9,13},{10,... | collective-permute-start | bytes 1572872 | tf_op jit(solution)/shard_map/ppermute | solution.py:62
  483.9 22.5 %collective-permute-start.33 = (bf16[2,32,4096]{2,1,0:T(8,128)(2,1)S(1)}, bf16[2,32,4096]{2,1,0:T(8,128)(2,1)S(1)}, u32[]{:S(2)}, u32[]{:S(2)}) collective-permute-start(bf16[2,32,4096]{2,1,0:T(8,128)(2,1)S(1)} %dynamic-slice_bitcast_fusion.3), channel_id=1, source_target_pairs={{0,4},{1,5},{2,6},{3,7},{4,0},{5,1},{6,2},{7,3},{8,12},{9,13},{10,... | collective-permute-start | bytes 1572872 | tf_op jit(solution)/shard_map/ppermute | solution.py:62
  498.7 19.0 %collective-permute-start.39 = (bf16[128,1024]{1,0:T(8,128)(2,1)S(1)}, bf16[128,1024]{1,0:T(8,128)(2,1)S(1)}, u32[]{:S(2)}, u32[]{:S(2)}) collective-permute-start(bf16[128,1024]{1,0:T(8,128)(2,1)S(1)} %dynamic-slice_bitcast_fusion.6), channel_id=1, source_target_pairs={{0,8},{1,9},{2,10},{3,11},{4,12},{5,13},{6,14},{7,15},{8,0},{9,1},... | collective-permute-start | bytes 786440 | tf_op jit(solution)/shard_map/ppermute | solution.py:62
  506.5 14.3 %collective-permute-start.34 = (bf16[32,4096]{1,0:T(8,128)(2,1)S(1)}, bf16[32,4096]{1,0:T(8,128)(2,1)S(1)}, u32[]{:S(2)}, u32[]{:S(2)}) collective-permute-start(bf16[32,4096]{1,0:T(8,128)(2,1)S(1)} %dynamic-slice_bitcast_fusion.7), channel_id=1, source_target_pairs={{0,8},{1,9},{2,10},{3,11},{4,12},{5,13},{6,14},{7,15},{8,0},{9,1},... | collective-permute-start | bytes 786440 | tf_op jit(solution)/shard_map/ppermute | solution.py:62
  (18 other events, 102.9 us)

commit v3 on v2

v3 whole, which is shorter than its diff:
```python
import functools

import jax
import jax.numpy as jnp
from jax import lax
from jax.experimental import pallas as pl
from jax.experimental.pallas import tpu as pltpu
from jax.sharding import PartitionSpec as P

D = 1024
H = 16
HD = 64
ROW_LEN = 1024
BLOCK = 128
BLOCKS = ROW_LEN // BLOCK
TILE = 256
CUTS = (0, 768, 1024)
VMEM_MIB = 48
LANES = 512
VECTOR_ROWS = 16
SKIP_CUTS = (0, 512, 1024)
HEADS = 8
GROUPS = H // HEADS
FAR = 1e30
epsilon = 1e-05
f32 = jnp.float32
bf16 = jnp.bfloat16
MIB = 1024 * 1024


def nn(left, right):
    return jnp.dot(left, right, preferred_element_type=f32)


def nt(left, right):
    return lax.dot_general(left, right, (((1,), (1,)), ((), ())), preferred_element_type=f32)


def tn(left, right):
    return lax.dot_general(left, right, (((0,), (0,)), ((), ())), preferred_element_type=f32)


def settings(**more):
    return pltpu.CompilerParams(vmem_limit_bytes=VMEM_MIB * MIB, **more)


def cost(flops, moved):
    return pl.CostEstimate(flops=int(flops), bytes_accessed=int(moved), transcendentals=0)


def held(shape):
    zeros = (0,) * len(shape)
    return pl.BlockSpec(shape, lambda *_: zeros, pipeline_mode=pl.Buffered(1))


def tiled(columns):
    return pl.BlockSpec((TILE, columns), lambda i: (i, 0))


def summed_over(columns):
    return pl.BlockSpec((8, columns), lambda i: (0, 0))


def launch(kernel, operands, pins=(), in_specs=(), scalars=0, **rest):
    count, extra = len(operands), len(pins)

    def body(*refs):
        kernel(*refs[:count], *refs[count + extra :])

    in_specs = list(in_specs) + [pl.BlockSpec(memory_space=pl.ANY)] * extra
    if scalars:
        rest["grid_spec"] = pltpu.PrefetchScalarGridSpec(
            num_scalar_prefetch=scalars,
            grid=rest.pop("grid"),
            in_specs=in_specs,
            out_specs=rest.pop("out_specs"),
            scratch_shapes=rest.pop("scratch_shapes"),
        )
    else:
        rest["in_specs"] = in_specs
    return pl.pallas_call(body, **rest)(*operands, *pins)


def swapped(value, axis, apart):
    mask = 2**apart
    pairs = [(source, source ^ mask) for source in range(lax.axis_size(axis))]
    return lax.ppermute(value, axis, pairs)


def mesh_bits():
    dp_bits = lax.axis_size("dp").bit_length() - 1
    half_bits = lax.axis_size("half").bit_length() - 1
    return [("half", bit) for bit in reversed(range(half_bits))] + [
        ("dp", bit) for bit in reversed(range(dp_bits))
    ]


def digits():
    count = len(mesh_bits())
    return count - 1, 0, count - 2, list(range(count - 3, 0, -1))


def my_sides():
    return jnp.stack([(lax.axis_index(axis) >> apart) & 1 for axis, apart in mesh_bits()]).astype(jnp.int32)


class Piece:
    def __init__(self, left, rows, kept, got=None, offset=0):
        self.left, self.rows, self.kept, self.got, self.offset = tuple(left), rows, kept, got, offset


def started(sent, kept):
    count = len(mesh_bits()) - 1
    flat = lambda value: value.reshape(-1, LANES)
    kept = flat(kept)
    return Piece(range(count), kept.shape[0] >> count, kept, swapped(flat(sent), "dp", 0))


def mix_kernel(plan, loaded, sides_ref, *refs):
    for take in plan:
        low = take["bits"]
        rows, whole = take["rows"], take["whole"]
        kept_in, got_in = refs[take["kept"]], refs[take["got"]]
        for to, offset, other in ((take["to_sent"], take["sent_at"], True), (take["to_kept"], 0, False)):
            side = sides_ref[take["digit"]]
            side = 1 - side if other else side
            out = refs[loaded + to]

            def one(at, carry, side=side, out=out, offset=offset, take=take, low=low, rows=rows, whole=whole):
                block = ((((at >> low) * 2) + side) << low) + (at & ((1 << low) - 1))
                start = block * whole + take["first"]
                mine = refs[take["kept"]][pl.ds(pl.multiple_of(start, 8), rows), :]
                theirs = refs[take["got"]][pl.ds(pl.multiple_of(take["got_at"] + start, 8), rows), :]
                total = mine.astype(f32) + theirs.astype(f32)
                out[pl.ds(pl.multiple_of(offset + at * rows, 8), rows), :] = total.astype(bf16)
                return carry

            lax.fori_loop(0, take["blocks"], one, 0)


def whole_of(array):
    zeros = (0,) * array.ndim
    return pl.BlockSpec(array.shape, lambda *_: zeros)


def place_in(arrays, array):
    for at, known in enumerate(arrays):
        if known is array:
            return at
    arrays.append(array)
    return len(arrays) - 1


def mix(parts):
    arrays, plan, shapes, pieces = [], [], [], []
    bundles = {}
    for piece, cuts in parts:
        for first, last, digit in cuts:
            rows = last - first
            at = piece.left.index(digit)
            left = piece.left[:at] + piece.left[at + 1 :]
            blocks = 1 << len(left)
            plan.append(
                dict(
                    kept=place_in(arrays, piece.kept),
                    got=place_in(arrays, piece.got),
                    got_at=piece.offset,
                    whole=piece.rows,
                    first=first,
                    rows=rows,
                    blocks=blocks,
                    bits=len(left) - at,
                    digit=digit,
                    to_kept=len(pieces),
                    sent_at=bundles.get(digit, 0),
                )
            )
            pieces.append(Piece(left, rows, None, None, bundles.get(digit, 0)))
            shapes.append((blocks * rows, LANES))
            bundles[digit] = bundles.get(digit, 0) + blocks * rows
    links = list(bundles)
    for take in plan:
        take["to_sent"] = len(pieces) + links.index(take["digit"])
    shapes = shapes + [(bundles[digit], LANES) for digit in links]
    outs = [jax.ShapeDtypeStruct(shape, bf16) for shape in shapes]
    results = pl.pallas_call(
        functools.partial(mix_kernel, plan, len(arrays)),
        in_specs=[pl.BlockSpec(memory_space=pltpu.SMEM)] + [whole_of(array) for array in arrays],
        out_specs=[whole_of(out) for out in outs],
        out_shape=outs,
        compiler_params=settings(),
        cost_estimate=cost(1e6, 4 * sum(shape[0] for shape in shapes) * LANES),
        name="mix",
    )(my_sides(), *arrays)
    arrived = {}
    for digit, sent in zip(links, results[len(pieces) :]):
        axis, apart = mesh_bits()[digit]
        arrived[digit] = swapped(sent, axis, apart)
    for take, piece, kept in zip(plan, pieces, results):
        piece.kept, piece.got = kept, arrived[take["digit"]]
    return pieces


def finish_kernel(plan, loaded, *refs):
    for take in plan:
        first, rows = take["first"], take["rows"]
        start = take["got_at"] + first
        total = refs[take["kept"]][first : first + rows, :].astype(f32) + refs[take["got"]][
            start : start + rows, :
        ].astype(f32)
        column = take["column"]
        refs[loaded + take["out"]][:, column : column + LANES] = total


def finish(shapes, panels):
    arrays, plan = [], []
    for piece, first, out, column in panels:
        plan.append(
            dict(
                kept=place_in(arrays, piece.kept),
                got=place_in(arrays, piece.got),
                got_at=piece.offset,
                first=first,
                rows=shapes[out][0],
                out=out,
                column=column,
            )
        )
    outs = [jax.ShapeDtypeStruct(shape, f32) for shape in shapes]
    return pl.pallas_call(
        functools.partial(finish_kernel, plan, len(arrays)),
        in_specs=[whole_of(array) for array in arrays],
        out_specs=[whole_of(out) for out in outs],
        out_shape=outs,
        compiler_params=settings(),
        cost_estimate=cost(1e6, 8e6),
        name="finish",
    )(*arrays)


def vector_piece(vectors):
    count = len(mesh_bits())
    devices = 1 << count
    values = jnp.concatenate([vector.reshape(devices, -1) for vector in vectors], axis=1).astype(bf16)
    values = jnp.pad(values[:, None, :], ((0, 0), (0, VECTOR_ROWS - 1), (0, LANES - values.shape[1])))
    values = values.reshape(devices // 2, 2, VECTOR_ROWS, LANES)
    mine = lax.axis_index("dp") & 1
    return started(
        lax.dynamic_index_in_dim(values, 1 - mine, 1, keepdims=False),
        lax.dynamic_index_in_dim(values, mine, 1, keepdims=False),
    )


class Sent:
    def __init__(self, value, axis, apart):
        self.got = swapped(value, axis, apart)


def in_order(values, arrived=(), ready=()):
    gots = []
    for piece in arrived:
        place_in(gots, piece.got)
    kepts = tuple(piece.kept for piece in ready)
    tied = lax.optimization_barrier((tuple(values), tuple(gots), kepts))
    places = [place_in(gots, piece.got) for piece in arrived]
    for piece, place in zip(arrived, places):
        piece.got = tied[1][place]
    for piece, kept in zip(ready, tied[2]):
        piece.kept = kept
    return tied[0]


def split_rows(total, core, rows_each):
    rows, columns = total.shape
    cut = total.reshape(rows // (2 * rows_each), 2, rows_each, columns)
    first, second = cut[:, 0], cut[:, 1]
    even = core == 0
    return jnp.where(even, second, first).astype(bf16), jnp.where(even, first, second).astype(bf16)


def panels_of(blocks, panels, rows_each):
    spec = pl.BlockSpec((blocks, None, rows_each, LANES), lambda i: (0, i, 0, 0))
    return spec, jax.ShapeDtypeStruct((blocks, panels, rows_each, LANES), bf16)


def row_stats(values):
    mean = jnp.mean(values, axis=-1, keepdims=True)
    centred = values - mean
    scale = lax.rsqrt(jnp.mean(centred * centred, axis=-1, keepdims=True) + epsilon)
    return centred * scale, scale


def norm_back(values, gain, grad):
    normal, scale = row_stats(values)
    inner = grad * gain
    along = jnp.mean(inner * normal, axis=-1, keepdims=True)
    return scale * (inner - jnp.mean(inner, axis=-1, keepdims=True) - normal * along), grad * normal


def add_rows(out_ref, *each):
    @pl.when(pl.program_id(0) == 0)
    def _():
        out_ref[...] = jnp.zeros_like(out_ref)

    for row, values in enumerate(each):
        out_ref[row : row + 1, :] += jnp.sum(values, axis=0, keepdims=True)


def enter_kernel(part, mirror, merge, gain, shift, qkv, *rest):
    hidden, normed, projected = rest[-3:]
    value = part[...] + nn(mirror[...], merge[...])
    hidden[...] = value
    low = (row_stats(value)[0] * gain[...] + shift[...]).astype(bf16)
    normed[...] = low
    projected[...] = nn(low, qkv[...]).astype(bf16)


def enter(start, part, mirror, merge_low, gain, shift, qkv, before):
    tokens = part.shape[0]
    offset = start // TILE
    at = lambda columns: pl.BlockSpec((TILE, columns), lambda i: (offset + i, 0))
    operands = (part, mirror, merge_low, gain, shift, qkv)
    return pl.pallas_call(
        enter_kernel,
        grid=(mirror.shape[0] // TILE,),
        in_specs=[at(D), tiled(D), held((D, D)), held((1, D)), held((1, D)), held((D, 3 * D))]
        + [pl.BlockSpec(memory_space=pl.ANY)] * len(before),
        out_specs=[at(D), at(D), at(3 * D)],
        out_shape=[
            jax.ShapeDtypeStruct((tokens, D), f32),
            jax.ShapeDtypeStruct((tokens, D), bf16),
            jax.ShapeDtypeStruct((tokens, 3 * D), bf16),
        ],
        input_output_aliases={len(operands) + i: i for i in range(len(before))},
        compiler_params=settings(),
        cost_estimate=cost(8 * mirror.shape[0] * D * D, 26 * MIB),
        name="enter",
    )(*operands, *before)


def leave_kernel(hidden, mixed, out_weight, gain, shift, residual, normed):
    value = hidden[...] + nn(mixed[...], out_weight[...])
    residual[...] = value
    normed[...] = (row_stats(value)[0] * gain[...] + shift[...]).astype(bf16)


def leave(hidden, mixed, out_weight, gain, shift):
    tokens = hidden.shape[0]
    return pl.pallas_call(
        leave_kernel,
        grid=(tokens // TILE,),
        in_specs=[tiled(D), tiled(D), held((D, D)), held((1, D)), held((1, D))],
        out_specs=[tiled(D), tiled(D)],
        out_shape=[jax.ShapeDtypeStruct((tokens, D), f32), jax.ShapeDtypeStruct((tokens, D), bf16)],
        compiler_params=settings(),
        cost_estimate=cost(2 * tokens * D * D, 14 * MIB),
        name="leave",
    )(hidden, mixed, out_weight, gain, shift)


def windows(lengths):
    ends = jnp.cumsum(lengths, axis=1)
    starts = ends - lengths
    low = (jnp.arange(BLOCKS, dtype=jnp.int32) * BLOCK)[None, :, None]
    holds_low = (low >= starts[:, None, :]) & (low < ends[:, None, :])
    high = low + (BLOCK - 1)
    holds_high = (high >= starts[:, None, :]) & (high < ends[:, None, :])
    window_low = jnp.sum(jnp.where(holds_low, starts[:, None, :], 0), axis=2) // BLOCK
    window_high = (jnp.sum(jnp.where(holds_high, ends[:, None, :], 0), axis=2) + BLOCK - 1) // BLOCK
    return window_low.reshape(-1), (window_high - window_low).reshape(-1)


def row_segments(lengths):
    ends = jnp.cumsum(lengths, axis=1)
    position = jnp.arange(ROW_LEN, dtype=jnp.int32)
    return jnp.sum((position[None, :, None] >= ends[:, None, :]).astype(jnp.int32), axis=2)


def head_slopes():
    return jnp.array([2.0 ** (-8.0 * (head + 1.0) / H) for head in range(H)], f32)


def fill_distance(far_ref, column, line):
    for b in range(BLOCKS):
        rows = slice(b * BLOCK, (b + 1) * BLOCK)
        i = lax.broadcasted_iota(jnp.int32, (BLOCK, ROW_LEN), 0) + b * BLOCK
        j = lax.broadcasted_iota(jnp.int32, (BLOCK, ROW_LEN), 1)
        distance = jnp.abs(i - j).astype(f32)
        far_ref[rows, :] = jnp.where(column[rows, :] == line[...], distance, FAR)


def masked_pair(value, lows):
    zero = jnp.zeros_like(value)
    return jnp.concatenate([jnp.where(lows, value, zero), jnp.where(lows, zero, value)], axis=0)


def over_blocks(low_ref, count_ref, row, variant):
    def block(b, carry):
        rows = pl.ds(pl.multiple_of(b * BLOCK, BLOCK), BLOCK)
        start = pl.multiple_of(low_ref[row * BLOCKS + b] * BLOCK, BLOCK)
        count = count_ref[row * BLOCKS + b]
        for n in range(1, BLOCKS + 1):
            pl.when(count == n)(functools.partial(variant, rows, pl.ds(start, n * BLOCK)))
        return carry

    lax.fori_loop(0, BLOCKS, block, 0)


def attend_kernel(
    low_ref, count_ref, slope_ref, column, line, q_ref, k_ref, v_ref, o_ref, lse_ref, far_ref, value_ref
):
    row = pl.program_id(0)
    group = pl.program_id(1)

    @pl.when(group == 0)
    def _():
        fill_distance(far_ref, column, line)
        lse_ref[...] = jnp.zeros_like(lse_ref)

    lane = lax.broadcasted_iota(jnp.int32, (1, 128), 1)
    lows = lane < HD
    for pair in range(HEADS // 2):
        value_ref[pair, :, :128] = v_ref[:, pair * 128 : pair * 128 + 128]
        value_ref[pair, :, 128:] = jnp.ones((ROW_LEN, 128), bf16)

    def variant(rows, cols):
        far = far_ref[rows, cols]
        logs = lse_ref[rows, :]
        for pair in range(HEADS // 2):
            at = slice(pair * 128, pair * 128 + 128)
            head = group * HEADS + pair * 2
            query = masked_pair(q_ref[rows, at] * bf16(HD**-0.5), lows)
            score = nt(query, k_ref[cols, at])
            score = score - jnp.concatenate([slope_ref[head] * far, slope_ref[head + 1] * far], axis=0)
            top = jnp.max(score, axis=1, keepdims=True)
            soft = jnp.exp(score - top).astype(bf16)
            both = nn(soft, value_ref[pair, cols, :])
            total = both[:, 128:]
            log_total = top + jnp.log(total)
            logs = jnp.where(lane == head, log_total[:BLOCK], logs)
            logs = jnp.where(lane == head + 1, log_total[BLOCK:], logs)
            mixed = jnp.where(lows, both[:BLOCK, :128], both[BLOCK:, :128])
            o_ref[rows, at] = (mixed / jnp.where(lows, total[:BLOCK], total[BLOCK:])).astype(bf16)
        lse_ref[rows, :] = logs

    over_blocks(low_ref, count_ref, row, variant)


def head_group(part):
    return pl.BlockSpec((ROW_LEN, HEADS * HD), lambda r, g, *_: (r, part * GROUPS + g))


def attention_operands(lengths):
    rows = lengths.shape[0]
    segments = row_segments(lengths)
    return windows(lengths) + (
        head_slopes(),
        segments.reshape(rows * ROW_LEN, 1),
        segments.reshape(rows, 1, ROW_LEN),
    )


def segment_specs():
    return [
        pl.BlockSpec((ROW_LEN, 1), lambda r, *_: (r, 0)),
        pl.BlockSpec((None, 1, ROW_LEN), lambda r, *_: (r, 0, 0)),
    ]


def attend(projected, operands):
    tokens = projected.shape[0]
    rows = tokens // ROW_LEN
    return launch(
        attend_kernel,
        operands + (projected, projected, projected),
        scalars=3,
        out_shape=[jax.ShapeDtypeStruct((tokens, D), bf16), jax.ShapeDtypeStruct((tokens, 128), f32)],
        grid=(rows, GROUPS),
        in_specs=segment_specs() + [head_group(0), head_group(1), head_group(2)],
        out_specs=[head_group(0), pl.BlockSpec((ROW_LEN, 128), lambda r, g, *_: (r, 0))],
        scratch_shapes=[
            pltpu.VMEM((ROW_LEN, ROW_LEN), f32),
            pltpu.VMEM((HEADS // 2, ROW_LEN, 256), bf16),
        ],
        compiler_params=settings(),
        cost_estimate=cost(rows * 20e9, 30 * MIB),
        name="attend",
    )


def attend_back_kernel(
    group,
    low_ref,
    count_ref,
    slope_ref,
    column,
    line,
    q_ref,
    k_ref,
    v_ref,
    grad_ref,
    lse_ref,
    delta_ref,
    out_ref,
    far_ref,
    turned_ref,
    key_ref,
):
    row = pl.program_id(0)
    fill_distance(far_ref, column, line)
    lows = lax.broadcasted_iota(jnp.int32, (1, 128), 1) < HD
    tops = lax.broadcasted_iota(jnp.int32, (128, 1), 0) < HD
    turned_ref[...] = jnp.zeros_like(turned_ref)
    for pair in range(HEADS // 2):
        key_ref[pair] = k_ref[:, pair * 128 : pair * 128 + 128].T

    def variant(rows, cols):
        far = far_ref[rows, cols]
        for pair in range(HEADS // 2):
            at = slice(pair * 128, pair * 128 + 128)
            head = group * HEADS + pair * 2
            query = q_ref[cols, at] * bf16(HD**-0.5)
            grad = grad_ref[cols, at]
            score = nt(masked_pair(k_ref[rows, at], lows), query)
            soft_grad = nt(masked_pair(v_ref[rows, at], lows), grad)
            softs, score_grads = [], []
            for side in range(2):
                part = slice(side * BLOCK, side * BLOCK + BLOCK)
                own = pl.ds(pair * 2 + side, 1)
                soft = jnp.exp(score[part] - slope_ref[head + side] * far - lse_ref[own, cols])
                score_grads.append((soft * (soft_grad[part] - delta_ref[own, cols])).astype(bf16))
                softs.append(soft.astype(bf16))
            score_grad = jnp.concatenate(score_grads, axis=0)
            value_grad = nn(jnp.concatenate(softs, axis=0), grad)
            key_grad = nn(score_grad, query)
            out_ref[2, rows, at] = jnp.where(lows, value_grad[:BLOCK], value_grad[BLOCK:]).astype(bf16)
            out_ref[1, rows, at] = jnp.where(lows, key_grad[:BLOCK], key_grad[BLOCK:]).astype(bf16)
            key = key_ref[pair, :, rows]
            zero = jnp.zeros_like(key)
            keys = jnp.concatenate([jnp.where(tops, key, zero), jnp.where(tops, zero, key)], axis=1)
            turned_ref[at, cols] += nn(keys, score_grad)

    over_blocks(low_ref, count_ref, row, variant)
    out_ref[0] = (turned_ref[...].T * HD**-0.5).astype(bf16)


def attend_back(group, projected, grad, lse_rows, delta_rows, operands, pins):
    tokens = projected.shape[0]
    rows = tokens // ROW_LEN
    of_group = lambda part: pl.BlockSpec((ROW_LEN, HEADS * HD), lambda r, *_: (r, part * GROUPS + group))
    thin = pl.BlockSpec((None, HEADS, ROW_LEN), lambda r, *_: (r, group, 0))
    return launch(
        functools.partial(attend_back_kernel, group),
        operands + (projected, projected, projected, grad, lse_rows, delta_rows),
        pins,
        scalars=3,
        out_shape=jax.ShapeDtypeStruct((3, tokens, HEADS * HD), bf16),
        grid=(rows,),
        in_specs=segment_specs() + [of_group(0), of_group(1), of_group(2), of_group(0), thin, thin],
        out_specs=pl.BlockSpec((3, ROW_LEN, HEADS * HD), lambda r, *_: (0, r, 0)),
        scratch_shapes=[
            pltpu.VMEM((ROW_LEN, ROW_LEN), f32),
            pltpu.VMEM((HEADS * HD, ROW_LEN), f32),
            pltpu.VMEM((HEADS // 2, 128, ROW_LEN), bf16),
        ],
        compiler_params=settings(),
        cost_estimate=cost(rows * 18e9, 16 * MIB),
        name="attend_back",
    )


PULL = 0.44
ERFC = (
    0.1241083994,
    0.1244657618,
    0.1084788423,
    0.1084610390,
    -0.0110834557,
    0.1493682951,
    -0.1395405297,
    0.0357417408,
)


def gelu_pair(value):
    size = jnp.abs(value)
    t = 1.0 / (1.0 + (PULL * 0.5**0.5) * size)
    poly = jnp.full_like(t, ERFC[-1])
    for term in reversed(ERFC[:-1]):
        poly = poly * t + term
    bell = jnp.exp(value * value * -0.5)
    tail = bell * t * poly
    whole = jnp.where(value < 0, tail, 1.0 - tail)
    return value * whole, whole + value * (bell * (0.5 / jnp.pi) ** 0.5)


def feed_kernel(
    rows_up,
    rows_down,
    core_ref,
    normed,
    cotangent,
    up_weight,
    up_bias,
    back,
    activated,
    normed_grad,
    bias_grad,
    up_sent,
    up_kept,
    down_sent,
    down_kept,
):
    core = core_ref[0]

    @pl.when(pl.program_id(0) == 0)
    def _():
        normed_grad[...] = jnp.zeros_like(normed_grad)

    value = nn(normed[...], up_weight[...]) + up_bias[...]
    active, slope = gelu_pair(value)
    active = active.astype(bf16)
    activated[...] = active
    grad = (back[...].astype(f32) * slope).astype(bf16)
    bias_grad[...] = jnp.sum(grad.astype(f32), axis=0, keepdims=True)
    normed_grad[...] += nt(grad, up_weight[...])
    for value, out in zip(split_rows(tn(active, cotangent[...]), core, rows_down), (down_sent, down_kept)):
        for panel in range(D // LANES):
            out[:, panel] = value[:, :, panel * LANES : panel * LANES + LANES]
    up_sent[...], up_kept[...] = split_rows(tn(normed[...], grad), core, rows_up)


def feed(core, normed, cotangent, up_weight, up_bias, back, width=LANES):
    tokens = normed.shape[0]
    hidden_units = up_weight.shape[1]
    devices = lax.axis_size("half") * lax.axis_size("dp")
    across = lambda rows: pl.BlockSpec((rows, width), lambda i: (0, i))
    shape = jax.ShapeDtypeStruct
    up_spec, up_shape = panels_of(devices // 2, hidden_units // LANES, D // devices)
    rows_down = hidden_units // devices
    down_spec = pl.BlockSpec((width // (2 * rows_down), D // LANES, rows_down, LANES), lambda i: (i, 0, 0, 0))
    down_shape = shape((devices // 2, D // LANES, rows_down, LANES), bf16)
    return launch(
        functools.partial(feed_kernel, D // devices, hidden_units // devices),
        (core, normed, cotangent, up_weight, up_bias, back),
        grid=(hidden_units // width,),
        in_specs=[
            pl.BlockSpec(memory_space=pltpu.SMEM),
            held((tokens, D)),
            held((tokens, D)),
            across(D),
            across(1),
            across(tokens),
        ],
        out_specs=[
            across(tokens),
            pl.BlockSpec((tokens, D), lambda i: (0, 0)),
            across(1),
            up_spec,
            up_spec,
            down_spec,
            down_spec,
        ],
        out_shape=[
            shape((tokens, hidden_units), bf16),
            shape((tokens, D), f32),
            shape((1, hidden_units), f32),
            up_shape,
            up_shape,
            down_shape,
            down_shape,
        ],
        compiler_params=settings(),
        cost_estimate=cost(8 * tokens * D * hidden_units, 60 * MIB),
        name="feed",
    )


def output_kernel(activated, down_weight, residual, bias, output):
    output[...] = (residual[...] + bias[...] + nn(activated[...], down_weight[...])).astype(bf16)


def layer_output(activated, down_weight, residual, bias, pins):
    tokens, hidden_units = activated.shape
    across = lambda rows: pl.BlockSpec((rows, TILE), lambda i: (0, i))
    return launch(
        output_kernel,
        (activated, down_weight, residual, bias),
        pins,
        grid=(D // TILE,),
        in_specs=[held((tokens, hidden_units)), across(hidden_units), across(tokens), across(1)],
        out_specs=across(tokens),
        out_shape=jax.ShapeDtypeStruct((tokens, D), bf16),
        compiler_params=settings(),
        cost_estimate=cost(2 * tokens * D * hidden_units, 24 * MIB),
        name="layer_output",
    )


def second_back_kernel(
    normed_grad,
    residual,
    cotangent,
    gain,
    out_weight,
    mixed,
    lse,
    residual_grad,
    attention_grad,
    mixed_grad,
    delta_rows,
    lse_rows,
    sums,
):
    incoming = normed_grad[...]
    outer = cotangent[...].astype(f32)
    through, gain_terms = norm_back(residual[...], gain[...], incoming)
    value = outer + through
    residual_grad[...] = value
    low = value.astype(bf16)
    attention_grad[...] = low
    mixed_low = nt(low, out_weight[...]).astype(bf16)
    mixed_grad[...] = mixed_low
    product = mixed_low.astype(f32) * mixed[...].astype(f32)
    high = product.astype(bf16)
    rest = (product - high.astype(f32)).astype(bf16)
    of_head = lax.broadcasted_iota(jnp.int32, (H, D), 1) // HD
    member = (of_head == lax.broadcasted_iota(jnp.int32, (H, D), 0)).astype(bf16)
    delta_rows[...] = nt(member, high) + nt(member, rest)
    lse_rows[...] = lse[...].T[:H]
    add_rows(sums, gain_terms, incoming, outer)


def second_back(normed_grad, residual, cotangent, gain, out_weight, mixed, lse):
    tokens = residual.shape[0]
    per_row = ROW_LEN // TILE
    shape = jax.ShapeDtypeStruct
    thin = pl.BlockSpec((None, H, TILE), lambda i: (i // per_row, 0, i % per_row))
    return pl.pallas_call(
        second_back_kernel,
        grid=(tokens // TILE,),
        in_specs=[tiled(D), tiled(D), tiled(D), held((1, D)), held((D, D)), tiled(D), tiled(128)],
        out_specs=[tiled(D), tiled(D), tiled(D), thin, thin, summed_over(D)],
        out_shape=[
            shape((tokens, D), f32),
            shape((tokens, D), bf16),
            shape((tokens, D), bf16),
            shape((tokens // ROW_LEN, H, ROW_LEN), f32),
            shape((tokens // ROW_LEN, H, ROW_LEN), f32),
            shape((8, D), f32),
        ],
        compiler_params=settings(),
        cost_estimate=cost(3 * tokens * D * D, 22 * MIB),
        name="second_back",
    )(normed_grad, residual, cotangent, gain, out_weight, mixed, lse)


def first_back_kernel(
    first, second, hidden, residual_grad, gain, qkv, hidden_grad, sums
):
    incoming = jnp.zeros(hidden.shape, f32)
    wide = HEADS * HD
    for part in range(3):
        for at, grad in enumerate((first, second)):
            start = part * D + at * wide
            incoming += nt(grad[part], qkv[:, start : start + wide])
    through, gain_terms = norm_back(hidden[...], gain[...], incoming)
    low = (residual_grad[...] + through).astype(bf16)
    hidden_grad[...] = low
    add_rows(sums, gain_terms, incoming, low.astype(f32))


def first_back(projected_grads, hidden, residual_grad, gain, qkv, pins):
    tokens = hidden.shape[0]
    shape = jax.ShapeDtypeStruct
    group = pl.BlockSpec((3, TILE, HEADS * HD), lambda i: (0, i, 0))
    return launch(
        first_back_kernel,
        projected_grads + (hidden, residual_grad, gain, qkv),
        pins,
        grid=(tokens // TILE,),
        in_specs=[group, group, tiled(D), tiled(D), held((1, D)), held((D, 3 * D))],
        out_specs=[tiled(D), summed_over(D)],
        out_shape=[shape((tokens, D), bf16), shape((8, D), f32)],
        compiler_params=settings(),
        cost_estimate=cost(6 * tokens * D * D, 22 * MIB),
        name="first_back",
    )


def joined_kernel(grad, merge, out):
    out[...] = nt(grad[...], merge[...]).astype(bf16)


def joined_grad(hidden_grad, merge_half, pins, name):
    tokens = hidden_grad.shape[0]
    return launch(
        joined_kernel,
        (hidden_grad, merge_half),
        pins,
        grid=(tokens // TILE,),
        in_specs=[tiled(D), held((D, D))],
        out_specs=tiled(D),
        out_shape=jax.ShapeDtypeStruct((tokens, D), bf16),
        compiler_params=settings(),
        cost_estimate=cost(2 * tokens * D * D, 6 * MIB),
        name=name,
    )


def weight_kernel(rows_each, core_ref, left, right, sent, kept):
    sent[...], kept[...] = split_rows(tn(left[...], right[...]), core_ref[0], rows_each)


def out_query_kernel(rows_each, core_ref, mixed, attention_grad, normed, projected_grad, sent, kept):
    step = pl.program_id(0)
    first = D // (HEADS * HD)

    @pl.when(step < first)
    def _():
        weight_kernel(rows_each, core_ref, mixed, attention_grad, sent, kept)

    @pl.when(step >= first)
    def _():
        weight_kernel(rows_each, core_ref, normed, projected_grad, sent, kept)


def out_query_grad(core, mixed, attention_grad, normed, projected_grad, pins):
    tokens = mixed.shape[0]
    devices = lax.axis_size("half") * lax.axis_size("dp")
    width = HEADS * HD
    first = D // width
    out, out_shape = panels_of(devices // 2, first + 3, D // devices)
    return launch(
        functools.partial(out_query_kernel, D // devices),
        (core, mixed, attention_grad, normed, projected_grad),
        pins,
        grid=(first + 3,),
        in_specs=[
            pl.BlockSpec(memory_space=pltpu.SMEM),
            held((tokens, D)),
            pl.BlockSpec((tokens, width), lambda i: (0, jnp.minimum(i, first - 1))),
            held((tokens, D)),
            pl.BlockSpec((None, tokens, width), lambda i: (jnp.maximum(i - first, 0), 0, 0)),
        ],
        out_specs=[out, out],
        out_shape=[out_shape, out_shape],
        compiler_params=settings(),
        cost_estimate=cost(2 * tokens * D * (first + 3) * width, 20 * MIB),
        name="out_query_grad",
    )


def merge_kernel(rows_each, core_ref, frames, *refs):
    mirrors, (right, sent, kept) = refs[:-3], refs[-3:]
    half = sent.shape[0] // 2
    sent[:half], kept[:half] = split_rows(tn(frames[...], right[...]), core_ref[0], rows_each)
    total = jnp.zeros((D, right.shape[1]), f32)
    start = 0
    for mirror in mirrors:
        end = start + mirror.shape[0]
        total += tn(mirror[...], right[start:end, :])
        start = end
    sent[half:], kept[half:] = split_rows(total, core_ref[0], rows_each)


def merge_grad(core, frames, mirrors, right, width=LANES):
    tokens = frames.shape[0]
    devices = lax.axis_size("half") * lax.axis_size("dp")
    out, out_shape = panels_of(devices // 2, D // width, 2 * D // devices)
    return launch(
        functools.partial(merge_kernel, 2 * D // devices),
        (core, frames, *mirrors, right),
        grid=(D // width,),
        in_specs=[pl.BlockSpec(memory_space=pltpu.SMEM), held((tokens, D))]
        + [held(mirror.shape) for mirror in mirrors]
        + [pl.BlockSpec((tokens, width), lambda i: (0, i))],
        out_specs=[out, out],
        out_shape=[out_shape, out_shape],
        compiler_params=settings(),
        cost_estimate=cost(4 * tokens * D * D, 16 * MIB),
        name="merge_grad",
    )


def query_grad(core, normed, projected_grad):
    tokens = normed.shape[0]
    devices = lax.axis_size("half") * lax.axis_size("dp")
    width = HEADS * HD
    out, out_shape = panels_of(devices // 2, 3, D // devices)
    return launch(
        functools.partial(weight_kernel, D // devices),
        (core, normed, projected_grad),
        grid=(3,),
        in_specs=[
            pl.BlockSpec(memory_space=pltpu.SMEM),
            held((tokens, D)),
            pl.BlockSpec((None, tokens, width), lambda i: (i, 0, 0)),
        ],
        out_specs=[out, out],
        out_shape=[out_shape, out_shape],
        compiler_params=settings(),
        cost_estimate=cost(6 * tokens * D * width, 16 * MIB),
        name="query_grad",
    )


def on_device(
    frames,
    skip_rows,
    lengths,
    merge_weight,
    merge_bias,
    norm1_gain,
    norm1_bias,
    qkv_weight,
    out_weight,
    norm2_gain,
    norm2_bias,
    up_weight,
    up_bias,
    down_weight,
    down_bias,
    cotangent,
):
    tokens = frames.shape[0]
    line = lambda vector: vector.reshape(1, -1)
    core = (lax.axis_index("dp") & 1).astype(jnp.int32).reshape(1)
    mirrors = [swapped(skip_rows[start:end], "half", 0) for start, end in zip(CUTS[:-1], CUTS[1:])]
    operands = attention_operands(lengths)
    back = nt(cotangent, down_weight).astype(bf16)
    part = nn(frames, merge_weight[:D]) + merge_bias
    entered = ()
    for start, mirror in zip(CUTS, mirrors):
        entered = enter(
            start, part, mirror, merge_weight[D:], line(norm1_gain), line(norm1_bias), qkv_weight, entered
        )
    hidden, normed, projected = entered
    mixed, lse = attend(projected, operands)
    residual, normed_two = leave(hidden, mixed, out_weight, line(norm2_gain), line(norm2_bias))
    activated, normed_two_grad, up_bias_grad, up_sent, up_kept, down_sent, down_kept = feed(
        core, normed_two, cotangent, up_weight, line(up_bias), back
    )
    _, x, y, (l, *deep) = digits()
    down = started(down_sent, down_kept)
    up = started(up_sent, up_kept)
    residual_grad, attention_grad, mixed_grad, delta_rows, lse_rows, sums_two = second_back(
        normed_two_grad, residual, cotangent, line(norm2_gain), out_weight, mixed, lse
    )
    (mixed_grad,) = in_order((mixed_grad,), (down,))
    cut = down.rows // 2
    one, two = mix([(down, ((0, cut, x), (cut, down.rows, y)))])
    (mixed_grad,) = in_order((mixed_grad,), (up,), (one, two))
    cut = up.rows // 2
    three, = mix([(up, ((0, cut, l),))])
    four = (cut, up.rows)
    (mixed_grad,) = in_order((mixed_grad,), (), (three,))
    first = attend_back(0, projected, mixed_grad, lse_rows, delta_rows, operands, ())
    (first,) = in_order((first,), (one, two, three))
    one, two, three, four = mix([(one, cuts(one, y)), (two, cuts(two, l)), (three, cuts(three, x)), (up, ((*four, x),))])
    (first,) = in_order((first,), (), (one, two, three, four))
    out_query = started(*out_query_grad(core, mixed, attention_grad, normed, first, ()))
    (mixed_grad,) = in_order((mixed_grad,), (), (out_query,))
    second = attend_back(1, projected, mixed_grad, lse_rows, delta_rows, operands, ())
    (second,) = in_order((second,), (one, two, three, four, out_query))
    panel = D // (lax.axis_size("half") * lax.axis_size("dp"))
    cut = 3 * panel
    one, two, three, four, out_one, out_two = mix(
        [
            (one, cuts(one, l)),
            (two, cuts(two, x)),
            (three, cuts(three, y)),
            (four, cuts(four, y)),
            (out_query, ((0, cut, x), (cut, out_query.rows, l))),
        ]
    )
    (second,) = in_order((second,), (), (one, two, three, four, out_one, out_two))
    query = started(*query_grad(core, normed, second))
    (second,) = in_order((second,), (), (query,))
    hidden_grad, sums_one = first_back(
        (first, second), hidden, residual_grad, line(norm1_gain), qkv_weight, ()
    )
    skip_parts = [
        joined_grad(hidden_grad[start:end], merge_weight[D:], (), "skip_grad")
        for start, end in zip(SKIP_CUTS[:-1], SKIP_CUTS[1:])
    ]
    (hidden_grad, sums_one, *skip_parts) = in_order(
        (hidden_grad, sums_one, *skip_parts), (one, two, three, four, out_one, out_two, query)
    )
    skip_one = Sent(skip_parts[0], "half", 0)
    one, two, three, four, out_one, out_two, query = mix(
        [
            (one, cuts(one, deep[0])),
            (two, cuts(two, deep[0])),
            (three, cuts(three, deep[0])),
            (four, cuts(four, l)),
            (out_one, cuts(out_one, y)),
            (out_two, cuts(out_two, y)),
            (query, cuts(query, l)),
        ]
    )
    (hidden_grad,) = in_order((hidden_grad,), (), (one, two, three, four, out_one, out_two, query))
    vectors = vector_piece((sums_one[2], sums_one[0], sums_one[1], sums_two[0], sums_two[1], up_bias_grad, sums_two[2]))
    merge = started(*merge_grad(core, frames, mirrors, hidden_grad))
    (hidden_grad,) = in_order((hidden_grad,), (), (merge,))
    frames_grad = joined_grad(hidden_grad, merge_weight[:D], (), "frames_grad")
    (frames_grad, residual, skip_parts[1]) = in_order(
        (frames_grad, residual, skip_parts[1]),
        (merge, vectors, skip_one, one, two, three, four, out_one, out_two, query),
    )
    skip_two = Sent(skip_parts[1], "half", 0)
    cut = merge.rows // 2
    done = [one, two, three]
    four, out_one, out_two, query, merge_one, merge_two, vectors = mix(
        [
            (four, cuts(four, deep[0])),
            (out_one, cuts(out_one, l)),
            (out_two, cuts(out_two, deep[0])),
            (query, cuts(query, y)),
            (merge, ((0, cut, y), (cut, merge.rows, l))),
            (vectors, cuts(vectors, y)),
        ]
    )
    (residual,) = in_order((residual,), (), (four, out_one, out_two, query, merge_one, merge_two, vectors))
    output = layer_output(activated, down_weight, residual, line(down_bias), ())
    (output,) = in_order((output,), (four, out_one, out_two, query, merge_one, merge_two, vectors))
    out_one, out_two, query, merge_one, merge_two, vectors = mix(
        [
            (out_one, cuts(out_one, deep[0])),
            (out_two, cuts(out_two, x)),
            (query, cuts(query, deep[0])),
            (merge_one, cuts(merge_one, l)),
            (merge_two, cuts(merge_two, y)),
            (vectors, cuts(vectors, l)),
        ]
    )
    query, merge_one, merge_two, vectors = mix(
        [
            (query, cuts(query, x)),
            (merge_one, cuts(merge_one, deep[0])),
            (merge_two, cuts(merge_two, deep[0])),
            (vectors, cuts(vectors, deep[0])),
        ]
    )
    merge_one, merge_two, vectors = mix([(each, cuts(each, x)) for each in (merge_one, merge_two, vectors)])
    pieces = [one, two, three, four, out_one, out_two, query, merge_one, merge_two, vectors]
    while any(piece.left for piece in pieces):
        open_pieces = [piece for piece in pieces if piece.left]
        closed = mix([(piece, cuts(piece, piece.left[0])) for piece in open_pieces])
        pieces = [closed.pop(0) if piece.left else piece for piece in pieces]
    one, two, three, four, out_one, out_two, query, merge_one, merge_two, vectors = pieces
    devices = lax.axis_size("half") * lax.axis_size("dp")
    hidden_units = up_weight.shape[1]
    wide = HEADS * HD
    per = three.rows // panel
    plan = [(one, 0, 0, 0), (two, 0, 0, LANES)]
    plan += [(three, at * panel, 1, at * LANES) for at in range(per)]
    plan += [(four, at * panel, 1, (per + at) * LANES) for at in range(per)]
    plan += [(out_one, 0, 2, 0), (out_one, panel, 2, LANES), (out_one, 2 * panel, 3, 0)]
    plan += [(out_two, at * panel, 3, (at + 1) * D) for at in range(2)]
    plan += [(query, at * panel, 3, at * D + wide) for at in range(3)]
    plan += [(merge_one, 0, 4, 0), (merge_two, 0, 4, LANES), (vectors, 0, 5, 0)]
    down_weight_grad, up_weight_grad, out_weight_grad, qkv_weight_grad, merge_weight_grad, sums = finish(
        [
            (hidden_units // devices, D),
            (D // devices, hidden_units),
            (D // devices, D),
            (D // devices, 3 * D),
            (2 * D // devices, D),
            (VECTOR_ROWS, LANES),
        ],
        plan,
    )
    small = []
    start = 0
    for size in (D, D, D, D, D, hidden_units, D):
        small.append(sums[0, start : start + size // devices])
        start += size // devices
    skip_grad = jnp.concatenate((skip_one.got, skip_two.got), axis=0)
    return (
        output,
        frames_grad,
        skip_grad,
        merge_weight_grad,
        small[0],
        small[1],
        small[2],
        qkv_weight_grad,
        out_weight_grad,
        small[3],
        small[4],
        up_weight_grad,
        small[5],
        down_weight_grad,
        small[6],
    )


def cuts(piece, digit):
    return ((0, piece.rows, digit),)


def solution(mesh):
    rows = P(("half", "dp"), None)
    parts = P(("half", "dp"))
    in_specs = (rows, rows, rows) + (P(),) * 12 + (rows,)
    out_specs = (rows, rows, rows, rows, parts, parts, parts, rows, rows, parts, parts, rows, parts, rows, parts)
    return jax.shard_map(
        on_device, mesh=mesh, in_specs=in_specs, out_specs=out_specs, check_vma=False
    )
```

time: 529 us -> 441 us (0.83)
  waiting for transfers between devices: 195 us -> 72.1 us
  Pallas kernels: 206 us -> 264 us
  starting transfers between devices: 52.8 us -> 30.1 us
  other arithmetic: 22.1 us -> 6.17 us
  local copies, waits for them, and re-layouts: 24.3 us -> 37.5 us
    ppermute x40 -> x32, waiting for transfers between devices: 195 us -> 72.1 us  [swapped(): return lax.ppermute(value, axis, pairs)]
    pallas_call x8 -> x24, Pallas kernels: 191 us -> 244 us  [the longest x12 187 us: launch(): return pl.pallas_call(body, **rest)(*operands, *pins)]
    ppermute x40 -> x32, starting transfers between devices: 52.8 us -> 30.1 us  [swapped(): return lax.ppermute(value, axis, pairs)]
    convert_element_type x26 -> x0, other arithmetic: 12.5 us -> none  [the longest x5 7.89 us: reduced(): block = (kept.astype(f32) + got.astype(f32)).astype(bf16)]
    unnamed x60 -> x102, local copies, waits for them, and re-layouts: 14.2 us -> 22.5 us
  transfers between devices with their start and end apart: 40 -> 32, of which waited for: 23 -> 15; matrix products, arithmetic and copies ran while one was open for 9% -> 9% of each run, Pallas kernels for 4% -> 25%
where the time goes in v3:
time: 441 us; the launch traced here: 433 us
  Pallas kernels  264 us (60%)
  waiting for transfers between devices  72.1 us (16%)
  local copies, waits for them, and re-layouts  37.5 us (9%)
  starting transfers between devices  30.1 us (7%)
  matrix products  21.3 us (5%)
  other arithmetic  6.17 us (1%)
    pallas_call x12, Pallas kernels, launch(): return pl.pallas_call(body, **rest)(*operands, *pins)  187 us
    ppermute x32, waiting for transfers between devices, swapped(): return lax.ppermute(value, axis, pairs)  72.1 us
    pallas_call x9, Pallas kernels, mix(): pl.pallas_call(functools.partial(mix_kernel, plan, len(arrays)), in_specs...  35.8 us
    ppermute x32, starting transfers between devices, swapped(): return lax.ppermute(value, axis, pairs)  30.1 us
    unnamed x102, local copies, waits for them, and re-layouts  22.5 us
    pallas_call x2, Pallas kernels, enter(): pl.pallas_call(enter_kernel, grid=(mirror.shape[0] // TILE,), in_specs=[a...  19.8 us
    dot_general x1, matrix products, nt(): lax.dot_general(left, right, (((1,), (1,)), ((), ())), preferred_element_...  14.8 us
    pallas_call x1, Pallas kernels, second_back(): pl.pallas_call(second_back_kernel, grid=(tokens // TILE,), in_specs=[tile...  12.5 us
  transfers between devices with their start and end apart: 32, of which 15 were waited for; matrix products, arithmetic and copies ran while one was open for 9% of the time, Pallas kernels for 25%

profile of v3, /device:TPU:0, one launch (start us, length us, event | category | flops | bytes accessed | tf_op | source)
XLA Modules:
  0.0 432.9 jit_solution(6950923899139088216)
XLA Ops:
  0.7 2.8 slice.70
  3.5 2.9 collective-permute-start.1
  6.4 1.9 slice.68
  8.3 1.8 fusion.2
  10.6 6.6 %broadcast_add_fusion.part = f32[1024,1024]{1,0:T(8,128)} fusion(f32[1024]{0:T(1024)S(1)} %copy-done.49, bf16[1024,1024]{1,0:T(8,128)(2,1)} %refs_1_.2, bf16[2048,1024]{1,0:T(8,128)(2,1)} %param.20), kind=kOutput, calls=%fused_computation.2 | convolution fusion | flops 2148532224 | bytes 8392704 | tf_op jit(solution)/shard_map/dot_general | solution.py:32
  17.3 14.8 %convolution_convert_fusion.refs_5_ = bf16[1024,4096]{1,0:T(8,128)(2,1)} fusion(bf16[1024,1024]{1,0:T(8,128)(2,1)} %cotangent.1, bf16[4096,1024]{1,0:T(8,128)(2,1)} %refs_1_.3), kind=kOutput, calls=%fused_computation | convolution fusion | flops 8594128896 | bytes 18874368 | tf_op jit(solution)/shard_map/dot_general | solution.py:36
  32.1 9.9 %collective-permute-done.1.mirror.refs_2_ = bf16[768,1024]{1,0:T(8,128)(2,1)} collective-permute-done((bf16[768,1024]{1,0:T(8,128)(2,1)}, bf16[768,1024]{1,0:T(8,128)(2,1)}, u32[]{:S(2)}, u32[]{:S(2)}) %collective-permute-start.1) | collective-permute-done | bytes 1572896 | tf_op jit(solution)/shard_map/ppermute | solution.py:87
  42.0 12.6 %enter.2 = (f32[1024,1024]{1,0:T(8,128)}, bf16[1024,1024]{1,0:T(8,128)(2,1)S(1)}, bf16[1024,3072]{1,0:T(8,128)(2,1)}) custom-call(f32[1024,1024]{1,0:T(8,128)} %broadcast_add_fusion.part, bf16[768,1024]{1,0:T(8,128)(2,1)} %collective-permute-done.1.mirror.refs_2_, bf16[1024,1024]{1,0:T(8,128)(2,1)S(1)} %get-tuple-element.368.merge.refs_1_, ...), custom_call_target="tpu_custom_call" | custom-call | flops 6442450944 | bytes 27262976 | tf_op jit(solution)/shard_map/enter/pallas_call | solution.py:323
  54.6 7.2 %enter.3 = (f32[1024,1024]{1,0:T(8,128)}, bf16[1024,1024]{1,0:T(8,128)(2,1)S(1)}, bf16[1024,3072]{1,0:T(8,128)(2,1)}) custom-call(f32[1024,1024]{1,0:T(8,128)} %broadcast_add_fusion.part, bf16[256,1024]{1,0:T(8,128)(2,1)S(1)} %collective-permute-done.mirror.refs_3_, ...), custom_call_target="tpu_custom_call", output_to_operand_aliasing={{0}: (6, {}), {1}: (7, {}), {2}: (8, {})} | custom-call | flops 2147483648 | bytes 27262976 | tf_op jit(solution)/shard_map/enter/pallas_call | solution.py:323
  63.1 27.2 %attend.1 = (bf16[1024,1024]{1,0:T(8,128)(2,1)S(1)}, f32[1024,128]{1,0:T(8,128)S(1)}) custom-call(s32[8]{0:T(128)S(1)} %get-tuple-element.366.refs_0_, s32[8]{0:T(128)S(1)} %get-tuple-element.365.refs_1_, f32[16]{0:T(128)S(1)} %copy-done.42, s32[1024,1]{1,0:T(8,128)S(1)} %copy.45.refs_3_, s32[1,1,1024]{2,1,0:T(1,128)S(1)} %bitcast.54, ...), custom_call_target="tpu_custom_call" | custom-call | flops 20000000000 | bytes 31457280 | tf_op jit(solution)/shard_map/attend/pallas_call | solution.py:81
  90.4 8.1 %leave.1 = (f32[1024,1024]{1,0:T(8,128)}, bf16[1024,1024]{1,0:T(8,128)(2,1)S(1)}) custom-call(f32[1024,1024]{1,0:T(8,128)} %get-tuple-element.189.hidden.refs_2_, bf16[1024,1024]{1,0:T(8,128)(2,1)S(1)} %get-tuple-element.191.mixed.refs_1_, bf16[1024,1024]{1,0:T(8,128)(2,1)} %out_weight.3, f32[1,1024]{1,0:T(1,128)S(1)} %bitcast.51, f32[1,1024]{1,0:T(1,128)S(1)} %bitcast.57), custom_call_target="tpu_custom_call" | custom-call | flops 2147483648 | bytes 14680064 | tf_op jit(solution)/shard_map/leave/pallas_call | solution.py:349
  98.5 58.5 %feed.1 = (bf16[1024,4096]{1,0:T(8,128)(2,1)}, f32[1024,1024]{1,0:T(8,128)}, f32[1,4096]{1,0:T(1,128)S(1)}, bf16[16,8,32,512]{3,2,1,0:T(8,128)(2,1)}, bf16[16,8,...) custom-call(s32[1]{0:T(128)} %bitcast.refs_0_, ...), custom_call_target="tpu_custom_call" | custom-call | flops 34359738368 | bytes 62914560 | tf_op jit(solution)/shard_map/feed/pallas_call | solution.py:81
  158.1 12.5 %second_back.1 = (f32[1024,1024]{1,0:T(8,128)}, bf16[1024,1024]{1,0:T(8,128)(2,1)S(1)}, bf16[1024,1024]{1,0:T(8,128)(2,1)S(1)}, f32[1,16,1024]{2,1,0:T(8,128)S(1...) custom-call(f32[1024,1024]{1,0:T(8,128)} %get-tuple-element.194.normed_grad, ...), custom_call_target="tpu_custom_call" | custom-call | flops 3221225472 | bytes 23068672 | tf_op jit(solution)/shard_map/second_back/pallas_call | solution.py:739
  171.9 4.7 %mix.9 = (bf16[1024,512]{1,0:T(8,128)(2,1)S(1)}, bf16[1024,512]{1,0:T(8,128)(2,1)S(1)}, bf16[1024,512]{1,0:T(8,128)(2,1)S(1)}, bf16[1024,512]{1,0:T(8,128)(2,1)S(1)}) custom-call(s32[5]{0:T(128)S(1)} %stack.17.sides_ref, bf16[4096,512]{1,0:T(8,128)(2,1)} %bitcast.68, bf16[4096,512]{1,0:T(8,128)(2,1)} %collective-permute-done.2.refs_1_), custom_call_target="tpu_custom_call" | custom-call | flops 1000000 | bytes 8388608 | tf_op jit(solution)/shard_map/mix/pallas_call | solution.py:186
  177.7 5.1 %mix.10 = (bf16[1024,512]{1,0:T(8,128)(2,1)S(1)}, bf16[1024,512]{1,0:T(8,128)(2,1)}) custom-call(s32[5]{0:T(128)S(1)} %stack.17.sides_ref, bf16[4096,512]{1,0:T(8,128)(2,1)} %bitcast.66, bf16[4096,512]{1,0:T(8,128)(2,1)} %collective-permute-done.3.refs_1_.refs_7_), custom_call_target="tpu_custom_call" | custom-call | flops 1000000 | bytes 4194304 | tf_op jit(solution)/shard_map/mix/pallas_call | solution.py:186
  183.7 3.1 collective-permute-start.6
  188.4 20.7 %attend_back.2.refs_4_.refs_0_ = bf16[3,1024,512]{2,1,0:T(8,128)(2,1)S(1)} custom-call(s32[8]{0:T(128)S(1)} %get-tuple-element.366.refs_0_, s32[8]{0:T(128)S(1)} %get-tuple-element.365.refs_1_, f32[16]{0:T(128)S(1)} %copy-done.42, s32[1024,1]{1,0:T(8,128)S(1)} %copy.45.refs_3_, s32[1,1,1024]{2,1,0:T(1,128)S(1)} %bitcast.55, ...), custom_call_target="tpu_custom_call" | custom-call | flops 17999998976 | bytes 16777216 | tf_op jit(solution)/shard_map/attend_back/pallas_call | solution.py:81
  209.1 1.6 copy-done.43
  213.0 7.4 %mix.11 = (bf16[512,512]{1,0:T(8,128)(2,1)S(1)}, bf16[512,512]{1,0:T(8,128)(2,1)S(1)}, bf16[512,512]{1,0:T(8,128)(2,1)S(1)}, bf16[1024,512]{1,0:T(8,128)(2,1)S(1...) custom-call(s32[5]{0:T(128)S(1)} %stack.17.sides_ref, ...), custom_call_target="tpu_custom_call" | custom-call | flops 1000000 | bytes 10485760 | tf_op jit(solution)/shard_map/mix/pallas_call | solution.py:186
  221.3 1.6 copy-done.37
  222.9 10.0 %out_query_grad.1 = (bf16[16,5,32,512]{3,2,1,0:T(8,128)(2,1)}, bf16[16,5,32,512]{3,2,1,0:T(8,128)(2,1)}) custom-call(s32[1]{0:T(128)} %bitcast.refs_0_, bf16[1024,1024]{1,0:T(8,128)(2,1)S(1)} %copy-done.1, bf16[1024,1024]{1,0:T(8,128)(2,1)S(1)} %copy-done.37, bf16[1024,1024]{1,0:T(8,128)(2,1)} %copy-done.3, bf16[3,1024,512]{2,1,0:T(8,128)(2,1)} %copy-done.43), custom_call_target="tpu_custom_call" | custom-call | flops 5368709120 | bytes 20971520 | tf_op jit(solution)/shard_map/out_query_grad/pallas_call | solution.py:81
  235.1 21.1 %attend_back.3.refs_2_.refs_1_ = bf16[3,1024,512]{2,1,0:T(8,128)(2,1)S(1)} custom-call(s32[8]{0:T(128)S(1)} %get-tuple-element.366.refs_0_, s32[8]{0:T(128)S(1)} %get-tuple-element.365.refs_1_, f32[16]{0:T(128)S(1)} %copy-done.42, s32[1024,1]{1,0:T(8,128)S(1)} %copy.45.refs_3_, s32[1,1,1024]{2,1,0:T(1,128)S(1)} %bitcast.56, ...), custom_call_target="tpu_custom_call" | custom-call | flops 17999998976 | bytes 16777216 | tf_op jit(solution)/shard_map/attend_back/pallas_call | solution.py:81
  256.2 1.7 copy-done.45
  258.0 11.9 %collective-permute-done.9.refs_5_ = bf16[1536,512]{1,0:T(8,128)(2,1)S(1)} collective-permute-done((bf16[1536,512]{1,0:T(8,128)(2,1)}, bf16[1536,512]{1,0:T(8,128)(2,1)S(1)}, u32[]{:S(2)}, u32[]{:S(2)}) %collective-permute-start.9) | collective-permute-done | bytes 1572896 | tf_op jit(solution)/shard_map/ppermute | solution.py:87
  271.1 6.2 %mix.12 = (bf16[256,512]{1,0:T(8,128)(2,1)S(1)}, bf16[256,512]{1,0:T(8,128)(2,1)S(1)}, bf16[256,512]{1,0:T(8,128)(2,1)S(1)}, bf16[512,512]{1,0:T(8,128)(2,1)S(1)...) custom-call(s32[5]{0:T(128)S(1)} %stack.17.sides_ref, ...), custom_call_target="tpu_custom_call" | custom-call | flops 1000000 | bytes 10485760 | tf_op jit(solution)/shard_map/mix/pallas_call | solution.py:186
  278.1 5.3 %query_grad.1 = (bf16[16,3,32,512]{3,2,1,0:T(8,128)(2,1)S(1)}, bf16[16,3,32,512]{3,2,1,0:T(8,128)(2,1)S(1)}) custom-call(s32[1]{0:T(128)} %bitcast.refs_0_, bf16[1024,1024]{1,0:T(8,128)(2,1)S(1)} %copy-done.4, bf16[3,1024,512]{2,1,0:T(8,128)(2,1)} %copy-done.45), custom_call_target="tpu_custom_call" | custom-call | flops 3221225472 | bytes 16777216 | tf_op jit(solution)/shard_map/query_grad/pallas_call | solution.py:81
  286.9 1.9 copy-done.44
  288.8 13.6 %first_back.1 = (bf16[1024,1024]{1,0:T(8,128)(2,1)S(1)}, f32[8,1024]{1,0:T(8,128)S(1)}) custom-call(bf16[3,1024,512]{2,1,0:T(8,128)(2,1)S(1)} %copy-done.44, bf16[3,1024,512]{2,1,0:T(8,128)(2,1)} %copy-done.45, f32[1024,1024]{1,0:T(8,128)} %get-tuple-element.189.hidden.refs_2_, f32[1024,1024]{1,0:T(8,128)} %get-tuple-element.254.refs_3_, ...), custom_call_target="tpu_custom_call" | custom-call | flops 6442450944 | bytes 23068672 | tf_op jit(solution)/shard_map/first_back/pallas_call | solution.py:81
  308.4 2.1 collective-permute-done.12.refs_3_
  310.5 4.9 %mix.13 = (bf16[128,512]{1,0:T(8,128)(2,1)S(1)}, bf16[128,512]{1,0:T(8,128)(2,1)S(1)}, bf16[128,512]{1,0:T(8,128)(2,1)S(1)}, bf16[256,512]{1,0:T(8,128)(2,1)S(1)...) custom-call(s32[5]{0:T(128)S(1)} %stack.17.sides_ref, ...), custom_call_target="tpu_custom_call" | custom-call | flops 1000000 | bytes 8388608 | tf_op jit(solution)/shard_map/mix/pallas_call | solution.py:186
  317.3 9.0 %merge_grad.1 = (bf16[16,2,64,512]{3,2,1,0:T(8,128)(2,1)}, bf16[16,2,64,512]{3,2,1,0:T(8,128)(2,1)}) custom-call(s32[1]{0:T(128)} %bitcast.refs_0_, bf16[1024,1024]{1,0:T(8,128)(2,1)} %refs_1_.2, bf16[768,1024]{1,0:T(8,128)(2,1)} %collective-permute-done.1.mirror.refs_2_, bf16[256,1024]{1,0:T(8,128)(2,1)S(1)} %copy-done.18, bf16[1024,1024]{1,0:T(8,128)(2,1)} %copy-done.5), custom_call_target="tpu_custom_call" | custom-call | flops 4294967296 | bytes 16777216 | tf_op jit(solution)/shard_map/merge_grad/pallas_call | solution.py:81
  334.6 1.8 concatenate.35
  337.3 1.6 collective-permute-start.20
  339.0 2.5 collective-permute-start.18
  343.1 3.8 frames_grad.1
  346.9 14.7 %collective-permute-done.18.refs_1_ = bf16[384,512]{1,0:T(8,128)(2,1)S(1)} collective-permute-done((bf16[384,512]{1,0:T(8,128)(2,1)}, bf16[384,512]{1,0:T(8,128)(2,1)S(1)}, u32[]{:S(2)}, u32[]{:S(2)}) %collective-permute-start.18) | collective-permute-done | bytes 393248 | tf_op jit(solution)/shard_map/ppermute | solution.py:87
  361.6 1.9 collective-permute-done.19.refs_1_
  363.6 5.0 %mix.14 = (bf16[128,512]{1,0:T(8,128)(2,1)S(1)}, bf16[192,512]{1,0:T(8,128)(2,1)S(1)}, bf16[128,512]{1,0:T(8,128)(2,1)S(1)}, bf16[384,512]{1,0:T(8,128)(2,1)S(1)...) custom-call(s32[5]{0:T(128)S(1)} %stack.17.sides_ref, ...), custom_call_target="tpu_custom_call" | custom-call | flops 1000000 | bytes 8126464 | tf_op jit(solution)/shard_map/mix/pallas_call | solution.py:186
  368.9 2.7 collective-permute-start.22
  372.5 14.6 %layer_output.1 = bf16[1024,1024]{1,0:T(8,128)(2,1)} custom-call(bf16[1024,4096]{1,0:T(8,128)(2,1)} %get-tuple-element.193.refs_0_, bf16[4096,1024]{1,0:T(8,128)(2,1)} %refs_1_.3, f32[1024,1024]{1,0:T(8,128)S(1)} %copy-done.2, f32[1,1024]{1,0:T(1,128)S(1)} %bitcast.65), custom_call_target="tpu_custom_call" | custom-call | flops 8589934592 | bytes 25165824 | tf_op jit(solution)/shard_map/layer_output/pallas_call | solution.py:81
  387.2 4.9 %collective-permute-done.21.refs_3_.refs_5_ = bf16[256,512]{1,0:T(8,128)(2,1)S(1)} collective-permute-done((bf16[256,512]{1,0:T(8,128)(2,1)S(1)}, bf16[256,512]{1,0:T(8,128)(2,1)S(1)}, u32[]{:S(2)}, u32[]{:S(2)}) %collective-permute-start.21) | collective-permute-done | bytes 262176 | tf_op jit(solution)/shard_map/ppermute | solution.py:87
  398.1 5.1 %collective-permute-done.28.refs_5_ = bf16[256,512]{1,0:T(8,128)(2,1)S(1)} collective-permute-done((bf16[256,512]{1,0:T(8,128)(2,1)S(1)}, bf16[256,512]{1,0:T(8,128)(2,1)S(1)}, u32[]{:S(2)}, u32[]{:S(2)}) %collective-permute-start.28) | collective-permute-done | bytes 262176 | tf_op jit(solution)/shard_map/ppermute | solution.py:87
  403.2 4.9 %collective-permute-done.25.refs_1_.refs_7_ = bf16[288,512]{1,0:T(8,128)(2,1)S(1)} collective-permute-done((bf16[288,512]{1,0:T(8,128)(2,1)S(1)}, bf16[288,512]{1,0:T(8,128)(2,1)S(1)}, u32[]{:S(2)}, u32[]{:S(2)}) %collective-permute-start.25) | collective-permute-done | bytes 294944 | tf_op jit(solution)/shard_map/ppermute | solution.py:87
  410.1 2.3 collective-permute-start.30
  412.8 1.6 collective-permute-start.29
  414.4 9.9 %collective-permute-done.30.refs_1_ = bf16[288,512]{1,0:T(8,128)(2,1)S(1)} collective-permute-done((bf16[288,512]{1,0:T(8,128)(2,1)S(1)}, bf16[288,512]{1,0:T(8,128)(2,1)S(1)}, u32[]{:S(2)}, u32[]{:S(2)}) %collective-permute-start.30) | collective-permute-done | bytes 294944 | tf_op jit(solution)/shard_map/ppermute | solution.py:87
  425.4 2.8 pad_maximum_fusion
  428.2 2.0 collective-permute-done.31.refs_13_
  (175 shorter events, 50.7 us)
Async XLA Ops:
  3.5 38.5 %collective-permute-start.1 = (bf16[768,1024]{1,0:T(8,128)(2,1)}, bf16[768,1024]{1,0:T(8,128)(2,1)}, u32[]{:S(2)}, u32[]{:S(2)}) collective-permute-start(bf16[768,1024]{1,0:T(8,128)(2,1)} %slice.70), channel_id=1, source_target_pairs={{0,16},{16,0},{1,17},{17,1},{2,18},{18,2},{3,19},{19,3},{4,20},{20... | collective-permute-start | bytes 4718600 | tf_op jit(solution)/shard_map/ppermute | solution.py:87
  8.3 46.3 %collective-permute-start = (bf16[256,1024]{1,0:T(8,128)(2,1)}, bf16[256,1024]{1,0:T(8,128)(2,1)S(1)}, u32[]{:S(2)}, u32[]{:S(2)}) collective-permute-start(bf16[256,1024]{1,0:T(8,128)(2,1)} %slice.68), channel_id=1, source_target_pairs={{0,16},{16,0},{1,17},{17,1},{2,18},{18,2},{3,19},{19,3},{4,20},{20... | collective-permute-start | bytes 1572872 | tf_op jit(solution)/shard_map/ppermute | solution.py:87
  17.3 24.7 %copy-start.34 = (f32[1024]{0:T(1024)S(1)}, f32[1024]{0:T(1024)}, u32[]{:S(2)}) copy-start(f32[1024]{0:T(1024)} %param.23) | copy-start | bytes 12292
  17.3 24.7 %copy-start.35 = (f32[1024]{0:T(1024)S(1)}, f32[1024]{0:T(1024)}, u32[]{:S(2)}) copy-start(f32[1024]{0:T(1024)} %param.22) | copy-start | bytes 12292
  63.1 27.2 %copy-start.31 = (f32[1024]{0:T(1024)S(1)}, f32[1024]{0:T(1024)}, u32[]{:S(2)}) copy-start(f32[1024]{0:T(1024)} %param.26) | copy-start | bytes 12292
  63.1 27.2 %copy-start.33 = (f32[1024]{0:T(1024)S(1)}, f32[1024]{0:T(1024)}, u32[]{:S(2)}) copy-start(f32[1024]{0:T(1024)} %param.27) | copy-start | bytes 12292
  157.6 14.4 %collective-permute-start.2 = (bf16[4096,512]{1,0:T(8,128)(2,1)}, bf16[4096,512]{1,0:T(8,128)(2,1)}, u32[]{:S(2)}, u32[]{:S(2)}) collective-permute-start(bf16[4096,512]{1,0:T(8,128)(2,1)} %bitcast.76), channel_id=1, source_target_pairs={{0,1},{1,0},{2,3},{3,2},{4,5},{5,4},{6,7},{7,6},{8,9},{9,8},{10,11... | collective-permute-start | bytes 12582920 | tf_op jit(solution)/shard_map/ppermute | solution.py:87
  157.6 20.1 %collective-permute-start.3 = (bf16[4096,512]{1,0:T(8,128)(2,1)}, bf16[4096,512]{1,0:T(8,128)(2,1)}, u32[]{:S(2)}, u32[]{:S(2)}) collective-permute-start(bf16[4096,512]{1,0:T(8,128)(2,1)} %bitcast.75), channel_id=1, source_target_pairs={{0,1},{1,0},{2,3},{3,2},{4,5},{5,4},{6,7},{7,6},{8,9},{9,8},{10,11... | collective-permute-start | bytes 12582920 | tf_op jit(solution)/shard_map/ppermute | solution.py:87
  171.9 10.8 %copy-start.29 = (f32[8,1024]{1,0:T(8,128)}, f32[8,1024]{1,0:T(8,128)S(1)}, u32[]{:S(2)}) copy-start(f32[8,1024]{1,0:T(8,128)S(1)} %get-tuple-element.286) | copy-start | bytes 98308
  183.7 27.0 %collective-permute-start.6 = (bf16[1024,512]{1,0:T(8,128)(2,1)}, bf16[1024,512]{1,0:T(8,128)(2,1)}, u32[]{:S(2)}, u32[]{:S(2)}) collective-permute-start(bf16[1024,512]{1,0:T(8,128)(2,1)} %get-tuple-element.214), channel_id=1, source_target_pairs={{0,4},{1,5},{2,6},{3,7},{4,0},{5,1},{6,2},{7,3},{8,12},{9,13},{10,... | collective-permute-start | bytes 3145736 | tf_op jit(solution)/shard_map/ppermute | solution.py:87
  186.9 24.8 %collective-permute-start.4 = (bf16[1024,512]{1,0:T(8,128)(2,1)S(1)}, bf16[1024,512]{1,0:T(8,128)(2,1)S(1)}, u32[]{:S(2)}, u32[]{:S(2)}) collective-permute-start(bf16[1024,512]{1,0:T(8,128)(2,1)S(1)} %get-tuple-element.212), channel_id=1, source_target_pairs={{0,16},{16,0},{1,17},{17,1},{2,18},{18,2},{3,19},{19,3},{4,20},{20... | collective-permute-start | bytes 3145736 | tf_op jit(solution)/shard_map/ppermute | solution.py:87
  188.4 24.6 %collective-permute-start.5 = (bf16[1024,512]{1,0:T(8,128)(2,1)S(1)}, bf16[1024,512]{1,0:T(8,128)(2,1)}, u32[]{:S(2)}, u32[]{:S(2)}) collective-permute-start(bf16[1024,512]{1,0:T(8,128)(2,1)S(1)} %get-tuple-element.213), channel_id=1, source_target_pairs={{0,2},{1,3},{2,0},{3,1},{4,6},{5,7},{6,4},{7,5},{8,10},{9,11},{10,... | collective-permute-start | bytes 3145736 | tf_op jit(solution)/shard_map/ppermute | solution.py:87
  210.7 10.6 %copy-start.1 = (bf16[1024,1024]{1,0:T(8,128)(2,1)S(1)}, bf16[1024,1024]{1,0:T(8,128)(2,1)}, u32[]{:S(2)}) copy-start(bf16[1024,1024]{1,0:T(8,128)(2,1)} %copy-done) | copy-start | bytes 6291460
  232.9 37.0 %collective-permute-start.10 = (bf16[2560,512]{1,0:T(8,128)(2,1)}, bf16[2560,512]{1,0:T(8,128)(2,1)}, u32[]{:S(2)}, u32[]{:S(2)}) collective-permute-start(bf16[2560,512]{1,0:T(8,128)(2,1)} %bitcast.77), channel_id=1, source_target_pairs={{0,1},{1,0},{2,3},{3,2},{4,5},{5,4},{6,7},{7,6},{8,9},{9,8},{10,11... | collective-permute-start | bytes 7864328 | tf_op jit(solution)/shard_map/ppermute | solution.py:87
  232.9 37.0 %collective-permute-start.9 = (bf16[1536,512]{1,0:T(8,128)(2,1)}, bf16[1536,512]{1,0:T(8,128)(2,1)S(1)}, u32[]{:S(2)}, u32[]{:S(2)}) collective-permute-start(bf16[1536,512]{1,0:T(8,128)(2,1)} %get-tuple-element.233), channel_id=1, source_target_pairs={{0,16},{16,0},{1,17},{17,1},{2,18},{18,2},{3,19},{19,3},{4,20},{20... | collective-permute-start | bytes 4718600 | tf_op jit(solution)/shard_map/ppermute | solution.py:87
  233.4 24.5 %collective-permute-start.7 = (bf16[512,512]{1,0:T(8,128)(2,1)S(1)}, bf16[512,512]{1,0:T(8,128)(2,1)S(1)}, u32[]{:S(2)}, u32[]{:S(2)}) collective-permute-start(bf16[512,512]{1,0:T(8,128)(2,1)S(1)} %get-tuple-element.231), channel_id=1, source_target_pairs={{0,2},{1,3},{2,0},{3,1},{4,6},{5,7},{6,4},{7,5},{8,10},{9,11},{10,... | collective-permute-start | bytes 1572872 | tf_op jit(solution)/shard_map/ppermute | solution.py:87
  234.0 24.0 %collective-permute-start.8 = (bf16[512,512]{1,0:T(8,128)(2,1)S(1)}, bf16[512,512]{1,0:T(8,128)(2,1)S(1)}, u32[]{:S(2)}, u32[]{:S(2)}) collective-permute-start(bf16[512,512]{1,0:T(8,128)(2,1)S(1)} %get-tuple-element.232), channel_id=1, source_target_pairs={{0,4},{1,5},{2,6},{3,7},{4,0},{5,1},{6,2},{7,3},{8,12},{9,13},{10,... | collective-permute-start | bytes 1572872 | tf_op jit(solution)/shard_map/ppermute | solution.py:87
  258.0 20.2 %copy-start.4 = (bf16[1024,1024]{1,0:T(8,128)(2,1)S(1)}, bf16[1024,1024]{1,0:T(8,128)(2,1)}, u32[]{:S(2)}) copy-start(bf16[1024,1024]{1,0:T(8,128)(2,1)} %copy-done.3) | copy-start | bytes 6291460
  284.6 25.9 %collective-permute-start.14 = (bf16[1536,512]{1,0:T(8,128)(2,1)S(1)}, bf16[1536,512]{1,0:T(8,128)(2,1)}, u32[]{:S(2)}, u32[]{:S(2)}) collective-permute-start(bf16[1536,512]{1,0:T(8,128)(2,1)S(1)} %bitcast.63), channel_id=1, source_target_pairs={{0,1},{1,0},{2,3},{3,2},{4,5},{5,4},{6,7},{7,6},{8,9},{9,8},{10,11... | collective-permute-start | bytes 4718600 | tf_op jit(solution)/shard_map/ppermute | solution.py:87
  284.6 25.9 %collective-permute-start.12 = (bf16[1024,512]{1,0:T(8,128)(2,1)}, bf16[1024,512]{1,0:T(8,128)(2,1)}, u32[]{:S(2)}, u32[]{:S(2)}) collective-permute-start(bf16[1024,512]{1,0:T(8,128)(2,1)} %get-tuple-element.258), channel_id=1, source_target_pairs={{0,16},{16,0},{1,17},{17,1},{2,18},{18,2},{3,19},{19,3},{4,20},{20... | collective-permute-start | bytes 3145736 | tf_op jit(solution)/shard_map/ppermute | solution.py:87
  285.2 23.2 %collective-permute-start.11 = (bf16[768,512]{1,0:T(8,128)(2,1)S(1)}, bf16[768,512]{1,0:T(8,128)(2,1)S(1)}, u32[]{:S(2)}, u32[]{:S(2)}) collective-permute-start(bf16[768,512]{1,0:T(8,128)(2,1)S(1)} %get-tuple-element.257), channel_id=1, source_target_pairs={{0,4},{1,5},{2,6},{3,7},{4,0},{5,1},{6,2},{7,3},{8,12},{9,13},{10,... | collective-permute-start | bytes 2359304 | tf_op jit(solution)/shard_map/ppermute | solution.py:87
  285.6 22.7 %collective-permute-start.13 = (bf16[768,512]{1,0:T(8,128)(2,1)}, bf16[768,512]{1,0:T(8,128)(2,1)S(1)}, u32[]{:S(2)}, u32[]{:S(2)}) collective-permute-start(bf16[768,512]{1,0:T(8,128)(2,1)} %get-tuple-element.259), channel_id=1, source_target_pairs={{0,2},{1,3},{2,0},{3,1},{4,6},{5,7},{6,4},{7,5},{8,10},{9,11},{10,... | collective-permute-start | bytes 2359304 | tf_op jit(solution)/shard_map/ppermute | solution.py:87
  317.2 9.0 %copy-start.21 = (bf16[256,512]{1,0:T(8,128)(2,1)}, bf16[256,512]{1,0:T(8,128)(2,1)S(1)}, u32[]{:S(2)}) copy-start(bf16[256,512]{1,0:T(8,128)(2,1)S(1)} %get-tuple-element.297.refs_4_) | copy-start | bytes 786436
  317.2 9.0 %copy-start.23 = (bf16[128,512]{1,0:T(8,128)(2,1)}, bf16[128,512]{1,0:T(8,128)(2,1)S(1)}, u32[]{:S(2)}) copy-start(bf16[128,512]{1,0:T(8,128)(2,1)S(1)} %get-tuple-element.317.refs_0_) | copy-start | bytes 393220
  317.2 9.0 %copy-start.25 = (bf16[128,512]{1,0:T(8,128)(2,1)}, bf16[128,512]{1,0:T(8,128)(2,1)S(1)}, u32[]{:S(2)}) copy-start(bf16[128,512]{1,0:T(8,128)(2,1)S(1)} %get-tuple-element.319.refs_2_) | copy-start | bytes 393220
  317.2 9.0 %copy-start.27 = (bf16[128,512]{1,0:T(8,128)(2,1)}, bf16[128,512]{1,0:T(8,128)(2,1)S(1)}, u32[]{:S(2)}) copy-start(bf16[128,512]{1,0:T(8,128)(2,1)S(1)} %get-tuple-element.320.refs_3_) | copy-start | bytes 393220
  317.3 9.0 %copy-start.39 = (bf16[384,512]{1,0:T(8,128)(2,1)}, bf16[384,512]{1,0:T(8,128)(2,1)S(1)}, u32[]{:S(2)}) copy-start(bf16[384,512]{1,0:T(8,128)(2,1)S(1)} %get-tuple-element.289) | copy-start | bytes 1179652
  326.3 15.2 %copy-start.6 = (bf16[1024,1024]{1,0:T(8,128)(2,1)S(1)}, bf16[1024,1024]{1,0:T(8,128)(2,1)}, u32[]{:S(2)}) copy-start(bf16[1024,1024]{1,0:T(8,128)(2,1)} %copy-done.5) | copy-start | bytes 6291460
  326.3 37.2 %collective-permute-start.15 = (bf16[2048,512]{1,0:T(8,128)(2,1)}, bf16[2048,512]{1,0:T(8,128)(2,1)}, u32[]{:S(2)}, u32[]{:S(2)}) collective-permute-start(bf16[2048,512]{1,0:T(8,128)(2,1)} %bitcast.24), channel_id=1, source_target_pairs={{0,1},{1,0},{2,3},{3,2},{4,5},{5,4},{6,7},{7,6},{8,9},{9,8},{10,11... | collective-permute-start | bytes 6291464 | tf_op jit(solution)/shard_map/ppermute | solution.py:87
  329.4 34.2 %collective-permute-start.19 = (bf16[1024,512]{1,0:T(8,128)(2,1)}, bf16[1024,512]{1,0:T(8,128)(2,1)}, u32[]{:S(2)}, u32[]{:S(2)}) collective-permute-start(bf16[1024,512]{1,0:T(8,128)(2,1)} %get-tuple-element.290), channel_id=1, source_target_pairs={{0,4},{1,5},{2,6},{3,7},{4,0},{5,1},{6,2},{7,3},{8,12},{9,13},{10,... | collective-permute-start | bytes 3145736 | tf_op jit(solution)/shard_map/ppermute | solution.py:87
  330.0 33.6 %collective-permute-start.17 = (bf16[512,1024]{1,0:T(8,128)(2,1)}, bf16[512,1024]{1,0:T(8,128)(2,1)}, u32[]{:S(2)}, u32[]{:S(2)}) collective-permute-start(bf16[512,1024]{1,0:T(8,128)(2,1)} %copy-done.12), channel_id=1, source_target_pairs={{0,16},{16,0},{1,17},{17,1},{2,18},{18,2},{3,19},{19,3},{4,20},{20... | collective-permute-start | bytes 3145736 | tf_op jit(solution)/shard_map/ppermute | solution.py:87
  337.3 1.7 collective-permute-start.16
  337.3 24.3 %collective-permute-start.20 = (bf16[640,512]{1,0:T(8,128)(2,1)}, bf16[640,512]{1,0:T(8,128)(2,1)S(1)}, u32[]{:S(2)}, u32[]{:S(2)}) collective-permute-start(bf16[640,512]{1,0:T(8,128)(2,1)} %copy-done.38), channel_id=1, source_target_pairs={{0,2},{1,3},{2,0},{3,1},{4,6},{5,7},{6,4},{7,5},{8,10},{9,11},{10,... | collective-permute-start | bytes 1966088 | tf_op jit(solution)/shard_map/ppermute | solution.py:87
  339.0 22.7 %collective-permute-start.18 = (bf16[384,512]{1,0:T(8,128)(2,1)}, bf16[384,512]{1,0:T(8,128)(2,1)S(1)}, u32[]{:S(2)}, u32[]{:S(2)}) collective-permute-start(bf16[384,512]{1,0:T(8,128)(2,1)} %copy-done.39), channel_id=1, source_target_pairs={{0,8},{1,9},{2,10},{3,11},{4,12},{5,13},{6,14},{7,15},{8,0},{9,1},... | collective-permute-start | bytes 1179656 | tf_op jit(solution)/shard_map/ppermute | solution.py:87
  343.1 20.5 %copy-start.15 = (bf16[768,512]{1,0:T(8,128)(2,1)S(1)}, bf16[768,512]{1,0:T(8,128)(2,1)}, u32[]{:S(2)}) copy-start(bf16[768,512]{1,0:T(8,128)(2,1)} %copy-done.14) | copy-start | bytes 2359300
  343.1 20.5 %copy-start.20 = (bf16[256,512]{1,0:T(8,128)(2,1)S(1)}, bf16[256,512]{1,0:T(8,128)(2,1)}, u32[]{:S(2)}) copy-start(bf16[256,512]{1,0:T(8,128)(2,1)} %copy-done.19) | copy-start | bytes 786436
  343.1 20.5 %copy-start.22 = (bf16[256,512]{1,0:T(8,128)(2,1)S(1)}, bf16[256,512]{1,0:T(8,128)(2,1)}, u32[]{:S(2)}) copy-start(bf16[256,512]{1,0:T(8,128)(2,1)} %copy-done.21) | copy-start | bytes 786436
  368.6 24.8 %collective-permute-start.23 = (bf16[1024,512]{1,0:T(8,128)(2,1)}, bf16[1024,512]{1,0:T(8,128)(2,1)S(1)}, u32[]{:S(2)}, u32[]{:S(2)}) collective-permute-start(bf16[1024,512]{1,0:T(8,128)(2,1)} %get-tuple-element.312), channel_id=1, source_target_pairs={{0,2},{1,3},{2,0},{3,1},{4,6},{5,7},{6,4},{7,5},{8,10},{9,11},{10,... | collective-permute-start | bytes 3145736 | tf_op jit(solution)/shard_map/ppermute | solution.py:87
  368.9 23.9 %collective-permute-start.22 = (bf16[704,512]{1,0:T(8,128)(2,1)S(1)}, bf16[704,512]{1,0:T(8,128)(2,1)S(1)}, u32[]{:S(2)}, u32[]{:S(2)}) collective-permute-start(bf16[704,512]{1,0:T(8,128)(2,1)S(1)} %get-tuple-element.311), channel_id=1, source_target_pairs={{0,4},{1,5},{2,6},{3,7},{4,0},{5,1},{6,2},{7,3},{8,12},{9,13},{10,... | collective-permute-start | bytes 2162696 | tf_op jit(solution)/shard_map/ppermute | solution.py:87
  371.6 20.4 %collective-permute-start.21 = (bf16[256,512]{1,0:T(8,128)(2,1)S(1)}, bf16[256,512]{1,0:T(8,128)(2,1)S(1)}, u32[]{:S(2)}, u32[]{:S(2)}) collective-permute-start(bf16[256,512]{1,0:T(8,128)(2,1)S(1)} %get-tuple-element.310), channel_id=1, source_target_pairs={{0,8},{1,9},{2,10},{3,11},{4,12},{5,13},{6,14},{7,15},{8,0},{9,1},... | collective-permute-start | bytes 786440 | tf_op jit(solution)/shard_map/ppermute | solution.py:87
  372.0 53.4 %collective-permute-start.24 = (bf16[512,1024]{1,0:T(8,128)(2,1)S(1)}, bf16[512,1024]{1,0:T(8,128)(2,1)S(1)}, u32[]{:S(2)}, u32[]{:S(2)}) collective-permute-start(bf16[512,1024]{1,0:T(8,128)(2,1)S(1)} %skip_grad.3), channel_id=1, source_target_pairs={{0,16},{16,0},{1,17},{17,1},{2,18},{18,2},{3,19},{19,3},{4,20},{20... | collective-permute-start | bytes 3145736 | tf_op jit(solution)/shard_map/ppermute | solution.py:87
  394.6 14.6 %collective-permute-start.27 = (bf16[320,512]{1,0:T(8,128)(2,1)S(1)}, bf16[320,512]{1,0:T(8,128)(2,1)S(1)}, u32[]{:S(2)}, u32[]{:S(2)}) collective-permute-start(bf16[320,512]{1,0:T(8,128)(2,1)S(1)} %get-tuple-element.337), channel_id=1, source_target_pairs={{0,4},{1,5},{2,6},{3,7},{4,0},{5,1},{6,2},{7,3},{8,12},{9,13},{10,... | collective-permute-start | bytes 983048 | tf_op jit(solution)/shard_map/ppermute | solution.py:87
  396.0 12.1 %collective-permute-start.25 = (bf16[288,512]{1,0:T(8,128)(2,1)S(1)}, bf16[288,512]{1,0:T(8,128)(2,1)S(1)}, u32[]{:S(2)}, u32[]{:S(2)}) collective-permute-start(bf16[288,512]{1,0:T(8,128)(2,1)S(1)} %get-tuple-element.332), channel_id=1, source_target_pairs={{0,8},{1,9},{2,10},{3,11},{4,12},{5,13},{6,14},{7,15},{8,0},{9,1},... | collective-permute-start | bytes 884744 | tf_op jit(solution)/shard_map/ppermute | solution.py:87
  396.8 6.4 %collective-permute-start.28 = (bf16[256,512]{1,0:T(8,128)(2,1)S(1)}, bf16[256,512]{1,0:T(8,128)(2,1)S(1)}, u32[]{:S(2)}, u32[]{:S(2)}) collective-permute-start(bf16[256,512]{1,0:T(8,128)(2,1)S(1)} %get-tuple-element.339), channel_id=1, source_target_pairs={{0,2},{1,3},{2,0},{3,1},{4,6},{5,7},{6,4},{7,5},{8,10},{9,11},{10,... | collective-permute-start | bytes 786440 | tf_op jit(solution)/shard_map/ppermute | solution.py:87
  410.1 14.2 %collective-permute-start.30 = (bf16[288,512]{1,0:T(8,128)(2,1)S(1)}, bf16[288,512]{1,0:T(8,128)(2,1)S(1)}, u32[]{:S(2)}, u32[]{:S(2)}) collective-permute-start(bf16[288,512]{1,0:T(8,128)(2,1)S(1)} %get-tuple-element.344), channel_id=1, source_target_pairs={{0,8},{1,9},{2,10},{3,11},{4,12},{5,13},{6,14},{7,15},{8,0},{9,1},... | collective-permute-start | bytes 884744 | tf_op jit(solution)/shard_map/ppermute | solution.py:87
  412.4 15.8 %collective-permute-start.26 = (bf16[64,512]{1,0:T(8,128)(2,1)S(1)}, bf16[64,512]{1,0:T(8,128)(2,1)S(1)}, u32[]{:S(2)}, u32[]{:S(2)}) collective-permute-start(bf16[64,512]{1,0:T(8,128)(2,1)S(1)} %get-tuple-element.334), channel_id=1, source_target_pairs={{0,16},{16,0},{1,17},{17,1},{2,18},{18,2},{3,19},{19,3},{4,20},{20... | collective-permute-start | bytes 196616 | tf_op jit(solution)/shard_map/ppermute | solution.py:87
  412.8 15.4 %collective-permute-start.29 = (bf16[96,512]{1,0:T(8,128)(2,1)S(1)}, bf16[96,512]{1,0:T(8,128)(2,1)S(1)}, u32[]{:S(2)}, u32[]{:S(2)}) collective-permute-start(bf16[96,512]{1,0:T(8,128)(2,1)S(1)} %get-tuple-element.342), channel_id=1, source_target_pairs={{0,16},{16,0},{1,17},{17,1},{2,18},{18,2},{3,19},{19,3},{4,20},{20... | collective-permute-start | bytes 294920 | tf_op jit(solution)/shard_map/ppermute | solution.py:87
  425.0 5.2 %collective-permute-start.31 = (bf16[144,512]{1,0:T(8,128)(2,1)S(1)}, bf16[144,512]{1,0:T(8,128)(2,1)S(1)}, u32[]{:S(2)}, u32[]{:S(2)}) collective-permute-start(bf16[144,512]{1,0:T(8,128)(2,1)S(1)} %get-tuple-element.348), channel_id=1, source_target_pairs={{0,16},{16,0},{1,17},{17,1},{2,18},{18,2},{3,19},{19,3},{4,20},{20... | collective-permute-start | bytes 442376 | tf_op jit(solution)/shard_map/ppermute | solution.py:87
  (35 other events, 125.9 us)
